TPU v7x, 32 devices: a whole 2x2x4 slice. The times are simulated.
32 devices in a mesh: comp: 2 (over core), gx: 4 (over z), gy: 4 (over y, x).
Axes of the slice: x: 2, y: 2, z: 4, core: 2. Of those that a mesh axis runs over, the one named last changes fastest.
Arguments:
- atmos_state: float32 [10, 20, 128, 512], P(None, None, ('comp', 'gx'), 'gy'), may hold values from -6 to 6
- atmos_diffusion: float32 [10], replicated, may hold values from 0.03 to 0.12
- remap_atmos: float32 [512, 128, 128], P(('comp', 'gx', 'gy')), may hold values from -0.1237436867076458 to 1.5237436867076457
- exchange_owner: int32 [512, 1], P(('comp', 'gx', 'gy')), may hold values from 0 to 15; in each aligned block of 16 rows (0 to 15, 16 to 31, ...) at most 2 rows name the same one
- exchange_slot: int32 [512], P(('comp', 'gx', 'gy')), may hold values from 0 to 15
- remap_ocean: float32 [512, 128, 128], P(('comp', 'gx', 'gy')), may hold values from -0.1237436867076458 to 1.5237436867076457
- ocean_owner: int32 [512, 1], P(('comp', 'gx', 'gy')), may hold values from 0 to 15; in each aligned block of 16 rows (0 to 15, 16 to 31, ...) at most 2 rows name the same one
- ocean_slot: int32 [512], P(('comp', 'gx', 'gy')), may hold values from 0 to 63
- ocean_state: float32 [4, 8, 256, 512], P(None, None, 'gx', 'gy'), may hold values from -6 to 6
- ocean_mixing: float32 [4], replicated, may hold values from 0.03 to 0.12
- wet_mask: int32 [256, 512], P('gx', 'gy'), may hold values 0 or 1
Outputs:
- atmos_next: float32 [10, 20, 128, 512], P(None, None, ('comp', 'gx'), 'gy')
- ocean_next: float32 [4, 8, 256, 512], P(None, None, 'gx', 'gy')
- ocean_surface: float32 [4, 128, 512], P(None, ('comp', 'gx'), 'gy')
Inputs may be any that keep to these rules, and one draw needn't show every extreme that they name: `exchange_owner`: among the rows of one device, no owner appears more than 2 times, and one appears exactly 2 times. `ocean_owner`: among the rows of one device, no owner appears more than 2 times, and one appears exactly 2 times.
All inputs are finite; a program needn't handle non-finite values. No bound on the sum of `wet_mask` on one device may be relied on, other than what follows from the above.
Results may differ from a plain program's by a relative error of at most 0.000088.
Values sent between devices are 32-bit elements; how exact they have to be, the bound alone decides.
No kernel may reach another device: no remote copies, remote signals or barrier semaphores. Data moves between devices by JAX's collectives and lax.ppermute only.
A program may use at most 128 MiB of HBM per device.

v0:
```python
import functools

import jax
import jax.numpy as jnp
from jax import lax
from jax.experimental import pallas as pl
from jax.experimental.pallas import tpu as pltpu
from jax.sharding import PartitionSpec as P

F32 = jnp.float32
BF16 = jnp.bfloat16
FORCING_SCALE = (0.1, -0.1, 0.1, 0.1)
SECTION = ("gx", "gy")
EVERY = ("comp", "gx", "gy")
CAPACITY = 2
PIECE_ROWS = 12
FLUX_ROWS = 16
VMEM_LIMIT = 40 * 1024 * 1024


def shifted(block, axis, distance):
    devices = range(lax.axis_size(axis))
    route = [((i - distance) % len(devices), i) for i in devices]
    return lax.ppermute(block, axis, route)


def dot(left, right, transposed=False):
    dims = (((1,), (1 if transposed else 0,)), ((), ()))
    return lax.dot_general(left, right, dims, preferred_element_type=F32)


def halves(values):
    high = values.astype(BF16)
    return high, (values - high.astype(F32)).astype(BF16)


def remapped(rows, block, transposed=False):
    rows_high, rows_low = halves(rows)
    block_high, block_low = halves(block)
    return (
        dot(rows_high, block_high, transposed)
        + dot(rows_low, block_high, transposed)
        + dot(rows_high, block_low, transposed)
    )


def picked(selection, values):
    chosen = selection.astype(BF16)
    high = values.astype(BF16)
    rest = values - high.astype(F32)
    middle = rest.astype(BF16)
    low = (rest - middle.astype(F32)).astype(BF16)
    return dot(chosen, high) + dot(chosen, middle) + dot(chosen, low)


def one_hot(labels):
    lanes = lax.broadcasted_iota(jnp.int32, labels.shape, 1).astype(F32)
    return (labels == lanes).astype(F32)


def grid_index(shape):
    return lax.broadcasted_iota(jnp.int32, shape, 0), lax.broadcasted_iota(jnp.int32, shape, 1)


def around(cells, north, south, west, east):
    rows, lanes = grid_index(cells.shape)
    row_count, width = cells.shape
    return (
        jnp.where(rows == 0, north, pltpu.roll(cells, 1, 0)),
        jnp.where(rows == row_count - 1, south, pltpu.roll(cells, row_count - 1, 0)),
        jnp.where(lanes == 0, west, pltpu.roll(cells, 1, 1)),
        jnp.where(lanes == width - 1, east, pltpu.roll(cells, width - 1, 1)),
    )


def diffused(cells, upper, lower, sides, diffusion):
    beside = sides[0] + sides[1] + sides[2] + sides[3] - 4.0 * cells
    return cells + diffusion * beside + 0.1 * (upper + lower - 2.0 * cells)


def edges_kernel(sizes, state, ocean, wet, first_rows, last_rows, first_cols, last_cols):
    fields, levels, rows, ocean_blocks, sea_rows = sizes
    blocks = fields * levels
    wet_row = blocks + ocean_blocks
    half = fields // 2
    tail = first_rows.shape[0] - wet_row
    width = state.shape[1]
    for out, at, sea_at in ((first_rows, 0, 0), (last_rows, rows - 1, sea_rows - 1)):
        out[pl.ds(wet_row, tail), :] = jnp.zeros((tail, width), F32)
        out[pl.ds(0, blocks), :] = state[pl.ds(at, blocks, stride=rows), :]
        out[pl.ds(blocks, ocean_blocks), :] = ocean[pl.ds(sea_at, ocean_blocks, stride=sea_rows), :]
        out[pl.ds(wet_row, 1), :] = wet[pl.ds(sea_at, 1), :].astype(F32)
    lanes = lax.broadcasted_iota(jnp.int32, (rows, width), 1)
    for part in range(2):
        first = jnp.zeros((rows, width), F32)
        last = jnp.zeros((rows, width), F32)
        for lane in range(half * levels):
            at = (part * half * levels + lane) * rows
            cells = state[pl.ds(at, rows), :]
            first = jnp.where(lanes == lane, cells[:, 0:1], first)
            last = jnp.where(lanes == lane, cells[:, width - 1 : width], last)
        first_cols[pl.ds(part * rows, rows), :] = first
        last_cols[pl.ds(part * rows, rows), :] = last
    lanes = lax.broadcasted_iota(jnp.int32, (sea_rows, width), 1)
    cells = wet[...].astype(F32)
    first = jnp.where(lanes == ocean_blocks, cells[:, 0:1], 0.0)
    last = jnp.where(lanes == ocean_blocks, cells[:, width - 1 : width], 0.0)
    for lane in range(ocean_blocks):
        cells = ocean[pl.ds(lane * sea_rows, sea_rows), :]
        first = jnp.where(lanes == lane, cells[:, 0:1], first)
        last = jnp.where(lanes == lane, cells[:, width - 1 : width], last)
    first_cols[pl.ds(2 * rows, sea_rows), :] = first
    last_cols[pl.ds(2 * rows, sea_rows), :] = last


def atmos_kernel(sizes, with_edges, state, north, south, west, east, diffusion, out, *edges):
    fields, levels, rows = sizes
    half = fields // 2
    width = state.shape[1]
    lanes = lax.broadcasted_iota(jnp.int32, (rows, width), 1)
    if with_edges:
        for cols in edges[2:]:
            cols[...] = jnp.zeros(cols.shape, F32)

    def field_step(field, carry):
        part = field // half
        within = (field - part * half) * levels
        held = pl.ds(pl.multiple_of(part * rows, rows), rows)
        back = lax.rem(width - within, width)
        west_cols = pltpu.roll(west[held, :], back, 1)
        east_cols = pltpu.roll(east[held, :], back, 1)
        number = diffusion[field]
        first = jnp.zeros((rows, width), F32)
        last = jnp.zeros((rows, width), F32)
        for level in range(levels):
            block = field * levels + level
            start = pl.multiple_of(block * rows, rows)
            cells = state[pl.ds(start, rows), :]
            upper = cells if level == 0 else state[pl.ds(start - rows, rows), :]
            lower = cells if level == levels - 1 else state[pl.ds(start + rows, rows), :]
            sides = around(
                cells,
                north[pl.ds(block, 1), :],
                south[pl.ds(block, 1), :],
                west_cols[:, level : level + 1],
                east_cols[:, level : level + 1],
            )
            after = diffused(cells, upper, lower, sides, number)
            out[pl.ds(start, rows), :] = after
            if with_edges:
                first = jnp.where(lanes == level, after[:, 0:1], first)
                last = jnp.where(lanes == level, after[:, width - 1 : width], last)
        if with_edges:
            edges[2][held, :] += pltpu.roll(first, within, 1)
            edges[3][held, :] += pltpu.roll(last, within, 1)
        return carry

    lax.fori_loop(0, fields, field_step, 0)
    if with_edges:
        blocks = fields * levels
        edges[0][...] = out[pl.ds(0, blocks, stride=rows), :]
        edges[1][...] = out[pl.ds(rows - 1, blocks, stride=rows), :]


def ocean_kernel(sizes, ocean, wet, north, south, west, east, mixing, out):
    fields, levels, rows, skipped, skipped_cols = sizes
    width = ocean.shape[1]
    cols = pl.ds(skipped_cols, rows)
    wet_cells = wet[...].astype(F32)
    wet_block = fields * levels
    wet_sides = around(
        wet_cells,
        north[pl.ds(skipped + wet_block, 1), :],
        south[pl.ds(skipped + wet_block, 1), :],
        west[cols, :][:, wet_block : wet_block + 1],
        east[cols, :][:, wet_block : wet_block + 1],
    )

    def field_step(field, carry):
        back = lax.rem(width - field * levels, width)
        west_cols = pltpu.roll(west[cols, :], back, 1)
        east_cols = pltpu.roll(east[cols, :], back, 1)
        number = mixing[field] * wet_cells
        for level in range(levels):
            block = field * levels + level
            start = pl.multiple_of(block * rows, rows)
            cells = ocean[pl.ds(start, rows), :]
            upper = cells if level == 0 else ocean[pl.ds(start - rows, rows), :]
            lower = cells if level == levels - 1 else ocean[pl.ds(start + rows, rows), :]
            sides = around(
                cells,
                north[pl.ds(skipped + block, 1), :],
                south[pl.ds(skipped + block, 1), :],
                west_cols[:, level : level + 1],
                east_cols[:, level : level + 1],
            )
            total = wet_sides[0] * (sides[0] - cells)
            for side in range(1, 4):
                total = total + wet_sides[side] * (sides[side] - cells)
            tendency = number * total + 0.1 * (upper + lower - 2.0 * cells)
            out[pl.ds(start, rows), :] = cells + wet_cells * tendency
        return carry

    lax.fori_loop(0, fields, field_step, 0)


def ranks_of(index, row, count, tally):
    def clear(at, carry):
        tally[at] = 0
        return carry

    lax.fori_loop(0, tally.shape[0], clear, 0)
    places = []
    for entry in range(count):
        owner = index[row, entry]
        rank = tally[owner]
        tally[owner] = rank + 1
        places.append((owner, rank))
    return places


def pieces_kernel(
    sizes, state, north, south, west, east, remap, index, diffusion, out, surface, tally
):
    fields, levels, rows, targets = sizes
    half = fields // 2
    width = out.shape[1]
    for field in range(fields):
        block = field * levels + levels - 1
        lane = (field % half) * levels + levels - 1
        held = pl.ds((field // half) * rows, rows)
        cells = state[field, 1]
        sides = around(
            cells,
            north[pl.ds(block, 1), :],
            south[pl.ds(block, 1), :],
            west[held, :][:, lane : lane + 1],
            east[held, :][:, lane : lane + 1],
        )
        surface[pl.ds(field * rows, rows), :] = diffused(
            cells, state[field, 0], cells, sides, diffusion[field]
        )
    out[...] = jnp.zeros(out.shape, F32)
    slots = targets * CAPACITY
    out[pl.ds(fields, slots, stride=PIECE_ROWS), :] = jnp.full((slots, width), -1.0, F32)
    places = ranks_of(index, 0, rows, tally)
    for tile in range(rows):
        owner, rank = places[tile]
        start = (owner * CAPACITY + rank) * PIECE_ROWS
        piece = remapped(surface[pl.ds(tile, fields, stride=rows), :], remap[tile])
        label = jnp.full((1, width), index[1, tile].astype(F32))
        out[pl.ds(start, fields), :] = piece
        out[pl.ds(start + fields, 1), :] = label


def flux_kernel(sizes, arrived, remap, index, out, gather, fluxes, tally):
    fields, flux_count, rows, targets, sections = sizes
    width = out.shape[1]
    slots = targets * CAPACITY
    select = one_hot(arrived[pl.ds(fields, slots, stride=PIECE_ROWS), :])
    gather[...] = select
    values = jnp.concatenate(
        [arrived[pl.ds(field, slots, stride=PIECE_ROWS), :] for field in range(fields)], axis=1
    )
    exchange = picked(jnp.transpose(select)[:rows, :], values)
    a = [exchange[:, field * width : (field + 1) * width] for field in range(fields)]
    speed = jnp.sqrt(a[2] * a[2] + a[3] * a[3] + 0.5)
    fluxes[pl.ds(0, rows), :] = speed * (a[0] - a[4]) + a[6] + a[7]
    fluxes[pl.ds(rows, rows), :] = speed * a[1] + a[5] + a[8]
    fluxes[pl.ds(2 * rows, rows), :] = speed * a[2] * (1.0 + 0.2 * jnp.tanh(a[9]))
    fluxes[pl.ds(3 * rows, rows), :] = speed * a[3]
    out[...] = jnp.zeros(out.shape, F32)
    devices = targets * sections
    label_row = CAPACITY * flux_count
    for entry in range(CAPACITY):
        out[pl.ds(label_row + entry, devices, stride=FLUX_ROWS), :] = jnp.full(
            (devices, width), -1.0, F32
        )
    places = ranks_of(index, 2, rows, tally)
    for tile in range(rows):
        owner, rank = places[tile]
        mapped = remapped(fluxes[pl.ds(tile, flux_count, stride=rows), :], remap[tile])
        label = jnp.full((1, width), index[3, tile].astype(F32))
        for section in range(sections):
            start = (section * targets + owner) * FLUX_ROWS
            out[pl.ds(start + rank * flux_count, flux_count), :] = mapped
            out[pl.ds(start + label_row + rank, 1), :] = label


def sea_kernel(sizes, landed, base, wet, own, out, answers):
    flux_count, sea_rows, targets, sections = sizes
    width = landed.shape[1]
    devices = targets * sections
    label_row = CAPACITY * flux_count
    select = jnp.concatenate(
        [
            one_hot(landed[pl.ds(label_row + entry, devices, stride=FLUX_ROWS), :])
            for entry in range(CAPACITY)
        ],
        axis=0,
    )
    values = jnp.concatenate(
        [
            jnp.concatenate(
                [
                    landed[pl.ds(entry * flux_count + flux, devices, stride=FLUX_ROWS), :]
                    for flux in range(flux_count)
                ],
                axis=1,
            )
            for entry in range(CAPACITY)
        ],
        axis=0,
    )
    forcing = picked(jnp.transpose(select)[:sea_rows, :], values)
    wet_cells = wet[...].astype(F32)
    tops = []
    for flux in range(flux_count):
        top = base[flux, 0] + wet_cells * (
            FORCING_SCALE[flux] * forcing[:, flux * width : (flux + 1) * width]
        )
        out[flux, 0] = top
        tops.append(top)
    all_tops = jnp.concatenate(tops, axis=1)
    first = own[0] * (targets * FLUX_ROWS)
    for entry in range(CAPACITY):
        mine = one_hot(landed[pl.ds(first + label_row + entry, targets, stride=FLUX_ROWS), :])
        reply = picked(mine[:, :sea_rows], all_tops)
        for flux in range(flux_count):
            answers[
                pl.ds(entry * flux_count + flux, targets, stride=CAPACITY * flux_count), :
            ] = reply[:, flux * width : (flux + 1) * width]


def reply_kernel(sizes, answered, remap, index, gather, out, on_exchange, tally):
    flux_count, rows, targets = sizes
    width = out.shape[1]
    slots = targets * CAPACITY
    places = ranks_of(index, 2, rows, tally)
    for tile in range(rows):
        owner, rank = places[tile]
        start = (owner * CAPACITY + rank) * flux_count
        on_exchange[pl.ds(tile * flux_count, flux_count), :] = remapped(
            answered[pl.ds(start, flux_count), :], remap[tile], True
        )
    values = jnp.concatenate(
        [on_exchange[pl.ds(flux, rows, stride=flux_count), :] for flux in range(flux_count)], axis=1
    )
    replies = picked(gather[...][:, :rows], values)
    for flux in range(flux_count):
        out[pl.ds(flux, slots, stride=flux_count), :] = replies[
            :, flux * width : (flux + 1) * width
        ]


def surface_kernel(sizes, returned, remap, index, out, tally):
    flux_count, rows, targets = sizes
    places = ranks_of(index, 0, rows, tally)
    for tile in range(rows):
        owner, rank = places[tile]
        start = (owner * CAPACITY + rank) * flux_count
        out[pl.ds(tile, flux_count, stride=rows), :] = remapped(
            returned[pl.ds(start, flux_count), :], remap[tile], True
        )


VMEM = pl.BlockSpec(memory_space=pltpu.VMEM)
SMEM = pl.BlockSpec(memory_space=pltpu.SMEM)


def array(*shape):
    return jax.ShapeDtypeStruct(shape, F32)


def call(kernel, name, outs, in_specs, scratch=(), flops=0, moved=0, **more):
    return pl.pallas_call(
        kernel,
        name=name,
        out_shape=outs,
        in_specs=in_specs,
        scratch_shapes=list(scratch),
        compiler_params=pltpu.CompilerParams(vmem_limit_bytes=VMEM_LIMIT),
        cost_estimate=pl.CostEstimate(flops=flops, bytes_accessed=moved, transcendentals=0),
        **more,
    )


def on_device(
    atmos_state,
    atmos_diffusion,
    remap_atmos,
    exchange_owner,
    exchange_slot,
    remap_ocean,
    ocean_owner,
    ocean_slot,
    ocean_state,
    ocean_mixing,
    wet_mask,
):
    targets = lax.axis_size(SECTION)
    sections = lax.axis_size("comp")
    devices = targets * sections
    fields, levels, rows, width = atmos_state.shape
    sea_fields, sea_levels, sea_rows, _ = ocean_state.shape
    blocks = fields * levels
    sea_blocks = sea_fields * sea_levels
    edge_rows = -(-(blocks + sea_blocks + 1) // 8) * 8
    edge_cols = 2 * rows + sea_rows
    slots = targets * CAPACITY
    ring = ("comp", "gx")

    index = jnp.stack([exchange_owner[:, 0], exchange_slot, ocean_owner[:, 0], ocean_slot])
    section = lax.axis_index("comp").astype(jnp.int32).reshape(1)
    state = atmos_state.reshape(blocks * rows, width)
    ocean = ocean_state.reshape(sea_blocks * sea_rows, width)

    first_rows, last_rows, first_cols, last_cols = call(
        functools.partial(edges_kernel, (fields, levels, rows, sea_blocks, sea_rows)),
        "edges",
        (
            array(edge_rows, width),
            array(edge_rows, width),
            array(edge_cols, width),
            array(edge_cols, width),
        ),
        [VMEM] * 3,
        moved=state.size * 4 + ocean.size * 4,
    )(state, ocean, wet_mask)
    west = shifted(last_cols, "gy", 1)
    east = shifted(first_cols, "gy", -1)
    north = shifted(last_rows, ring, 1)
    south = shifted(first_rows, ring, -1)

    pieces = pl.pallas_call(
        functools.partial(pieces_kernel, (fields, levels, rows, targets)),
        name="pieces",
        grid=(1,),
        out_shape=array(slots * PIECE_ROWS, width),
        in_specs=[
            pl.BlockSpec((fields, 2, rows, width), lambda i: (0, levels // 2 - 1, 0, 0)),
            VMEM,
            VMEM,
            VMEM,
            VMEM,
            VMEM,
            SMEM,
            SMEM,
        ],
        out_specs=VMEM,
        scratch_shapes=[pltpu.VMEM((fields * rows, width), F32), pltpu.SMEM((targets,), jnp.int32)],
        compiler_params=pltpu.CompilerParams(vmem_limit_bytes=VMEM_LIMIT),
        cost_estimate=pl.CostEstimate(
            flops=6 * fields * rows * width * width,
            bytes_accessed=remap_atmos.size * 4,
            transcendentals=0,
        ),
    )(atmos_state, north, south, west, east, remap_atmos, index, atmos_diffusion)
    arrived = lax.all_to_all(
        pieces.reshape(targets, CAPACITY * PIECE_ROWS, width), SECTION, 0, 0, tiled=True
    )

    after_first, up_rows, down_rows, left_cols, right_cols = call(
        functools.partial(atmos_kernel, (fields, levels, rows), True),
        "first_step",
        (
            array(blocks * rows, width),
            array(blocks, width),
            array(blocks, width),
            array(2 * rows, width),
            array(2 * rows, width),
        ),
        [VMEM] * 5 + [SMEM],
        flops=20 * state.size,
        moved=state.size * 8,
    )(state, north, south, west, east, atmos_diffusion)
    west_next = shifted(right_cols, "gy", 1)
    east_next = shifted(left_cols, "gy", -1)
    north_next = shifted(down_rows, ring, 1)
    south_next = shifted(up_rows, ring, -1)
    sea_base = call(
        functools.partial(ocean_kernel, (sea_fields, sea_levels, sea_rows, blocks, 2 * rows)),
        "sea_base",
        array(sea_blocks * sea_rows, width),
        [VMEM] * 6 + [SMEM],
        flops=30 * ocean.size,
        moved=ocean.size * 8,
    )(ocean, wet_mask, north, south, west, east, ocean_mixing)

    outgoing, gather = call(
        functools.partial(flux_kernel, (fields, sea_fields, rows, targets, sections)),
        "fluxes",
        (array(devices * FLUX_ROWS, width), array(slots, width)),
        [VMEM, VMEM, SMEM],
        [
            pltpu.VMEM((sea_fields * rows, width), F32),
            pltpu.SMEM((targets,), jnp.int32),
        ],
        flops=6 * sea_fields * rows * width * width,
        moved=remap_ocean.size * 4,
    )(arrived.reshape(slots * PIECE_ROWS, width), remap_ocean, index)
    landed = lax.all_to_all(
        outgoing.reshape(devices, FLUX_ROWS, width), EVERY, 0, 0, tiled=True
    )

    top_block = pl.BlockSpec((sea_fields, 1, sea_rows, width), lambda i: (0, 0, 0, 0))
    ocean_next, answers = pl.pallas_call(
        functools.partial(sea_kernel, (sea_fields, sea_rows, targets, sections)),
        name="sea_top",
        grid=(1,),
        out_shape=(
            array(sea_fields, sea_levels, sea_rows, width),
            array(slots * sea_fields, width),
        ),
        in_specs=[VMEM, top_block, VMEM, SMEM],
        out_specs=(top_block, VMEM),
        input_output_aliases={1: 0},
        compiler_params=pltpu.CompilerParams(vmem_limit_bytes=VMEM_LIMIT),
        cost_estimate=pl.CostEstimate(flops=0, bytes_accessed=landed.size * 4, transcendentals=0),
    )(
        landed.reshape(devices * FLUX_ROWS, width),
        sea_base.reshape(sea_fields, sea_levels, sea_rows, width),
        wet_mask,
        section,
    )
    answered = lax.all_to_all(
        answers.reshape(targets, CAPACITY * sea_fields, width), SECTION, 0, 0, tiled=True
    )

    atmos_next = call(
        functools.partial(atmos_kernel, (fields, levels, rows), False),
        "second_step",
        array(blocks * rows, width),
        [VMEM] * 5 + [SMEM],
        flops=20 * state.size,
        moved=state.size * 8,
    )(after_first, north_next, south_next, west_next, east_next, atmos_diffusion)

    replies = call(
        functools.partial(reply_kernel, (sea_fields, rows, targets)),
        "replies",
        array(slots * sea_fields, width),
        [VMEM, VMEM, SMEM, VMEM],
        [
            pltpu.VMEM((sea_fields * rows, width), F32),
            pltpu.SMEM((targets,), jnp.int32),
        ],
        flops=6 * sea_fields * rows * width * width,
        moved=remap_ocean.size * 4,
    )(answered.reshape(slots * sea_fields, width), remap_ocean, index, gather)
    returned = lax.all_to_all(
        replies.reshape(targets, CAPACITY * sea_fields, width), SECTION, 0, 0, tiled=True
    )
    ocean_surface = call(
        functools.partial(surface_kernel, (sea_fields, rows, targets)),
        "surface",
        array(sea_fields * rows, width),
        [VMEM, VMEM, SMEM],
        [pltpu.SMEM((targets,), jnp.int32)],
        flops=6 * sea_fields * rows * width * width,
        moved=remap_atmos.size * 4,
    )(returned.reshape(slots * sea_fields, width), remap_atmos, index)
    return (
        atmos_next.reshape(atmos_state.shape),
        ocean_next,
        ocean_surface.reshape(sea_fields, rows, width),
    )


def solution(mesh):
    in_specs = (
        P(None, None, ("comp", "gx"), "gy"),
        P(),
        P(("comp", "gx", "gy"), None, None),
        P(("comp", "gx", "gy"), None),
        P(("comp", "gx", "gy")),
        P(("comp", "gx", "gy"), None, None),
        P(("comp", "gx", "gy"), None),
        P(("comp", "gx", "gy")),
        P(None, None, "gx", "gy"),
        P(),
        P("gx", "gy"),
    )
    out_specs = (
        P(None, None, ("comp", "gx"), "gy"),
        P(None, None, "gx", "gy"),
        P(None, ("comp", "gx"), "gy"),
    )
    return jax.shard_map(
        on_device, mesh=mesh, in_specs=in_specs, out_specs=out_specs, check_vma=False
    )
```

profile of v0, /device:TPU:0, one launch (start us, length us, event | category | flops | bytes accessed | tf_op | source)
XLA Modules:
  0.0 93.2 jit_solution(12597558164134089711)
XLA Ops:
  0.7 1.4 %copy-done = f32[10,20,16,128]{3,2,1,0:T(8,128)S(1)} copy-done((f32[10,20,16,128]{3,2,1,0:T(8,128)S(1)}, f32[10,20,16,128]{3,2,1,0:T(8,128)}, u32[]{:S(2)}) %copy-start) | copy-done | bytes 1638424
  4.1 2.1 %edges.1 = (f32[240,128]{1,0:T(8,128)S(1)}, f32[240,128]{1,0:T(8,128)S(1)}, f32[96,128]{1,0:T(8,128)S(1)}, f32[96,128]{1,0:T(8,128)S(1)}) custom-call(f32[3200,128]{1,0:T(8,128)S(1)} %bitcast.18, f32[2048,128]{1,0:T(8,128)S(1)} %bitcast.20, s32[64,128]{1,0:T(8,128)S(1)} %copy-done.7), custom_call_target="tpu_custom_call" | custom-call | bytes 2686976 | tf_op jit(solution)/shard_map/edges/pallas_call | solution.py:418
  6.2 3.1 %collective-permute-start = (f32[240,128]{1,0:T(8,128)S(1)}, f32[240,128]{1,0:T(8,128)S(1)}, u32[]{:S(2)}, u32[]{:S(2)}) collective-permute-start(f32[240,128]{1,0:T(8,128)S(1)} %get-tuple-element.16), channel_id=1, source_target_pairs={{28,0},{0,4},{4,8},{8,12},{12,16},{16,20},{20,24},{24,28},{29,1},{... | collective-permute-start | bytes 368648 | tf_op jit(solution)/shard_map/ppermute | solution.py:24
  9.3 1.5 %collective-permute-start.1 = (f32[240,128]{1,0:T(8,128)S(1)}, f32[240,128]{1,0:T(8,128)S(1)}, u32[]{:S(2)}, u32[]{:S(2)}) collective-permute-start(f32[240,128]{1,0:T(8,128)S(1)} %get-tuple-element.17), channel_id=1, source_target_pairs={{4,0},{8,4},{12,8},{16,12},{20,16},{24,20},{28,24},{0,28},{5,1},{9... | collective-permute-start | bytes 368648 | tf_op jit(solution)/shard_map/ppermute | solution.py:24
  10.8 1.9 %collective-permute-start.2 = (f32[96,128]{1,0:T(8,128)S(1)}, f32[96,128]{1,0:T(8,128)S(1)}, u32[]{:S(2)}, u32[]{:S(2)}) collective-permute-start(f32[96,128]{1,0:T(8,128)S(1)} %get-tuple-element.18), channel_id=1, source_target_pairs={{3,0},{0,1},{1,2},{2,3},{7,4},{4,5},{5,6},{6,7},{11,8},{8,9},{9,10... | collective-permute-start | bytes 147464 | tf_op jit(solution)/shard_map/ppermute | solution.py:24
  13.8 2.3 %collective-permute-done.2.west = f32[96,128]{1,0:T(8,128)S(1)} collective-permute-done((f32[96,128]{1,0:T(8,128)S(1)}, f32[96,128]{1,0:T(8,128)S(1)}, u32[]{:S(2)}, u32[]{:S(2)}) %collective-permute-start.2) | collective-permute-done | bytes 49184 | tf_op jit(solution)/shard_map/ppermute | solution.py:24
  17.2 1.4 %pieces.1 = f32[384,128]{1,0:T(8,128)S(1)} custom-call(f32[10,20,16,128]{3,2,1,0:T(8,128)S(1)} %copy-done, f32[240,128]{1,0:T(8,128)S(1)} %collective-permute-done.north, f32[240,128]{1,0:T(8,128)S(1)} %collective-permute-done.1.south, f32[96,128]{1,0:T(8,128)S(1)} %collective-permute-done.2.west, f32[96,128]{1,0:T(8,128)S(1)} %collective-permute-done.3.east, ...), custom_call_target="tpu_custom_call" | custom-call | flops 15728640 | bytes 1048576 | tf_op jit(solution)/shard_map/pieces/pallas_call | solution.py:435
  18.6 13.6 %all_to_all.20 = f32[16,24,128]{2,1,0:T(8,128)S(1)} all-to-all(f32[16,24,128]{2,1,0:T(8,128)S(1)} %bitcast.24), channel_id=1, replica_groups=mesh['comp'=2,'gx'=4,'gy'=4] {'gx','gy'}, dimensions={0} | all-to-all | bytes 393216 | tf_op jit(solution)/shard_map/all_to_all | solution.py:459
  32.2 2.1 %fluxes.1 = (f32[512,128]{1,0:T(8,128)}, f32[32,128]{1,0:T(8,128)S(1)}) custom-call(f32[384,128]{1,0:T(8,128)S(1)} %bitcast.23, f32[16,128,128]{2,1,0:T(8,128)S(1)} %copy-done.3, s32[4,16]{1,0:T(4,128)S(1)} %pad_add_fusion.index), custom_call_target="tpu_custom_call" | custom-call | flops 6291456 | bytes 1048576 | tf_op jit(solution)/shard_map/fluxes/pallas_call | solution.py:490
  34.4 2.6 %all-to-all-start.1 = ((f32[32,16,128]{2,1,0:T(8,128)}), f32[32,16,128]{2,1,0:T(8,128)S(1)}, u32[]{:S(2)}, u32[]{:S(2)}) async-start(f32[32,16,128]{2,1,0:T(8,128)} %bitcast.9), calls=%async_computation.1 | async-start | bytes 524288 | tf_op jit(solution)/shard_map/all_to_all | solution.py:502
  37.0 3.3 %sea_base.1 = f32[2048,128]{1,0:T(8,128)} custom-call(f32[2048,128]{1,0:T(8,128)S(1)} %bitcast.21, s32[64,128]{1,0:T(8,128)S(1)} %copy-done.8, f32[240,128]{1,0:T(8,128)S(1)} %collective-permute-done.north, f32[240,128]{1,0:T(8,128)S(1)} %collective-permute-done.1.south, f32[96,128]{1,0:T(8,128)S(1)} %collective-permute-done.2.west, ...), custom_call_target="tpu_custom_call" | custom-call | flops 7864320 | bytes 2097152 | tf_op jit(solution)/shard_map/sea_base/pallas_call | solution.py:481
  40.3 7.9 %all-to-all-done.1 = f32[32,16,128]{2,1,0:T(8,128)S(1)} async-done(((f32[32,16,128]{2,1,0:T(8,128)}), f32[32,16,128]{2,1,0:T(8,128)S(1)}, u32[]{:S(2)}, u32[]{:S(2)}) %all-to-all-start.1) | async-done | bytes 262176 | tf_op jit(solution)/shard_map/all_to_all | solution.py:502
  48.2 2.0 %sea_top.1 = (f32[4,8,64,128]{3,2,1,0:T(8,128)}, f32[128,128]{1,0:T(8,128)S(1)}) custom-call(f32[512,128]{1,0:T(8,128)S(1)} %bitcast.22, f32[4,8,64,128]{3,2,1,0:T(8,128)} %bitcast.28, s32[64,128]{1,0:T(8,128)S(1)} %copy-done.8, s32[1]{0:T(128)} %bitcast.12.own), custom_call_target="tpu_custom_call", output_to_operand_aliasing={{0}: (1, {})} | custom-call | bytes 262144 | tf_op jit(solution)/shard_map/sea_top/pallas_call | solution.py:507
  50.2 10.1 %all_to_all.21 = f32[16,8,128]{2,1,0:T(8,128)S(1)} all-to-all(f32[16,8,128]{2,1,0:T(8,128)S(1)} %bitcast.27), channel_id=1, replica_groups=mesh['comp'=2,'gx'=4,'gy'=4] {'gx','gy'}, dimensions={0} | all-to-all | bytes 131072 | tf_op jit(solution)/shard_map/all_to_all | solution.py:526
  60.3 1.2 %copy-done.4 = f32[16,128,128]{2,1,0:T(8,128)S(1)} copy-done((f32[16,128,128]{2,1,0:T(8,128)S(1)}, f32[16,128,128]{2,1,0:T(8,128)}, u32[]{:S(2)}) %copy-start.4) | copy-done | bytes 1048600
  61.5 2.4 %replies.1 = f32[128,128]{1,0:T(8,128)} custom-call(f32[128,128]{1,0:T(8,128)S(1)} %bitcast.26, f32[16,128,128]{2,1,0:T(8,128)S(1)} %copy-done.4, s32[4,16]{1,0:T(4,128)S(1)} %pad_add_fusion.index, f32[32,128]{1,0:T(8,128)S(1)} %get-tuple-element.28.gather), custom_call_target="tpu_custom_call" | custom-call | flops 6291456 | bytes 1048576 | tf_op jit(solution)/shard_map/replies/pallas_call | solution.py:539
  63.9 3.5 %all-to-all-start.3 = ((f32[16,8,128]{2,1,0:T(8,128)}), f32[16,8,128]{2,1,0:T(8,128)S(1)}, u32[]{:S(2)}, u32[]{:S(2)}) async-start(f32[16,8,128]{2,1,0:T(8,128)} %bitcast.15), calls=%async_computation.3 | async-start | bytes 131072 | tf_op jit(solution)/shard_map/all_to_all | solution.py:551
  67.4 9.3 %first_step.1 = (f32[3200,128]{1,0:T(8,128)S(1)}, f32[200,128]{1,0:T(8,128)S(1)}, f32[200,128]{1,0:T(8,128)S(1)}, f32[32,128]{1,0:T(8,128)S(1)}, f32[32,128]{1,0:T(8,128)S(1)}) custom-call(f32[3200,128]{1,0:T(8,128)S(1)} %bitcast.19, f32[240,128]{1,0:T(8,128)S(1)} %collective-permute-done.north, f32[240,128]{1,0:T(8,128)S(1)} %collective-permute-done.1.south, ...), custom_call_target="tpu_custom_call" | custom-call | flops 8192000 | bytes 3276800 | tf_op jit(solution)/shard_map/first_step/pallas_call | solution.py:463
  76.7 1.9 %collective-permute-start.4 = (f32[200,128]{1,0:T(8,128)S(1)}, f32[200,128]{1,0:T(8,128)S(1)}, u32[]{:S(2)}, u32[]{:S(2)}) collective-permute-start(f32[200,128]{1,0:T(8,128)S(1)} %get-tuple-element.21), channel_id=1, source_target_pairs={{28,0},{0,4},{4,8},{8,12},{12,16},{16,20},{20,24},{24,28},{29,1},{... | collective-permute-start | bytes 307208 | tf_op jit(solution)/shard_map/ppermute | solution.py:24
  78.6 1.7 %collective-permute-start.5 = (f32[200,128]{1,0:T(8,128)S(1)}, f32[200,128]{1,0:T(8,128)S(1)}, u32[]{:S(2)}, u32[]{:S(2)}) collective-permute-start(f32[200,128]{1,0:T(8,128)S(1)} %get-tuple-element.22), channel_id=1, source_target_pairs={{4,0},{8,4},{12,8},{16,12},{20,16},{24,20},{28,24},{0,28},{5,1},{9... | collective-permute-start | bytes 307208 | tf_op jit(solution)/shard_map/ppermute | solution.py:24
  80.3 1.8 %collective-permute-start.6 = (f32[32,128]{1,0:T(8,128)S(1)}, f32[32,128]{1,0:T(8,128)S(1)}, u32[]{:S(2)}, u32[]{:S(2)}) collective-permute-start(f32[32,128]{1,0:T(8,128)S(1)} %get-tuple-element.23), channel_id=1, source_target_pairs={{3,0},{0,1},{1,2},{2,3},{7,4},{4,5},{5,6},{6,7},{11,8},{8,9},{9,10... | collective-permute-start | bytes 49160 | tf_op jit(solution)/shard_map/ppermute | solution.py:24
  83.3 1.7 %collective-permute-done.6.west = f32[32,128]{1,0:T(8,128)S(1)} collective-permute-done((f32[32,128]{1,0:T(8,128)S(1)}, f32[32,128]{1,0:T(8,128)S(1)}, u32[]{:S(2)}, u32[]{:S(2)}) %collective-permute-start.6) | collective-permute-done | bytes 16416 | tf_op jit(solution)/shard_map/ppermute | solution.py:24
  85.9 5.1 %second_step.1 = f32[3200,128]{1,0:T(8,128)} custom-call(f32[3200,128]{1,0:T(8,128)S(1)} %get-tuple-element.20.state, f32[200,128]{1,0:T(8,128)S(1)} %collective-permute-done.4.north, f32[200,128]{1,0:T(8,128)S(1)} %collective-permute-done.5.south, f32[32,128]{1,0:T(8,128)S(1)} %collective-permute-done.6.west, f32[32,128]{1,0:T(8,128)S(1)} %collective-permute-done.7.east, ...), custom_call_target="tpu_custom_call" | custom-call | flops 8192000 | bytes 3276800 | tf_op jit(solution)/shard_map/second_step/pallas_call | solution.py:530
  91.0 2.2 %surface.1 = f32[64,128]{1,0:T(8,128)} custom-call(f32[128,128]{1,0:T(8,128)S(1)} %bitcast.25, f32[16,128,128]{2,1,0:T(8,128)S(1)} %copy-done.2, s32[4,16]{1,0:T(4,128)S(1)} %pad_add_fusion.index), custom_call_target="tpu_custom_call" | custom-call | flops 6291456 | bytes 1048576 | tf_op jit(solution)/shard_map/surface/pallas_call | solution.py:554
  (38 shorter events, 6.2 us)
Async XLA Ops:
  0.6 13.1 %copy-start.11 = (s32[16]{0:T(128)S(1)}, s32[16]{0:T(128)}, u32[]{:S(2)}) copy-start(s32[16]{0:T(128)} %param.18) | copy-start | bytes 196
  0.6 13.1 %copy-start.12 = (s32[16,1]{0,1:T(1,128)S(1)}, s32[16,1]{0,1:T(1,128)}, u32[]{:S(2)}) copy-start(s32[16,1]{0,1:T(1,128)} %param.17) | copy-start | bytes 196
  0.7 13.1 %copy-start.13 = (s32[16]{0:T(128)S(1)}, s32[16]{0:T(128)}, u32[]{:S(2)}) copy-start(s32[16]{0:T(128)} %param.15) | copy-start | bytes 196
  0.7 13.1 %copy-start.14 = (s32[16,1]{0,1:T(1,128)S(1)}, s32[16,1]{0,1:T(1,128)}, u32[]{:S(2)}) copy-start(s32[16,1]{0,1:T(1,128)} %param.14) | copy-start | bytes 196
  0.7 16.5 %copy-start.9 = (f32[10]{0:T(128)S(1)}, f32[10]{0:T(128)}, u32[]{:S(2)}) copy-start(f32[10]{0:T(128)} %diffusion.5) | copy-start | bytes 124
  0.7 1.5 %copy-start = (f32[10,20,16,128]{3,2,1,0:T(8,128)S(1)}, f32[10,20,16,128]{3,2,1,0:T(8,128)}, u32[]{:S(2)}) copy-start(f32[10,20,16,128]{3,2,1,0:T(8,128)} %state.1) | copy-start | bytes 4915204
  2.1 1.2 %copy-start.5 = (f32[4,8,64,128]{3,2,1,0:T(8,128)S(1)}, f32[4,8,64,128]{3,2,1,0:T(8,128)}, u32[]{:S(2)}) copy-start(f32[4,8,64,128]{3,2,1,0:T(8,128)} %param.19) | copy-start | bytes 3145732
  4.1 13.1 %copy-start.2 = (f32[16,128,128]{2,1,0:T(8,128)S(1)}, f32[16,128,128]{2,1,0:T(8,128)}, u32[]{:S(2)}) copy-start(f32[16,128,128]{2,1,0:T(8,128)} %remap.7) | copy-start | bytes 3145732
  6.2 11.0 %collective-permute-start = (f32[240,128]{1,0:T(8,128)S(1)}, f32[240,128]{1,0:T(8,128)S(1)}, u32[]{:S(2)}, u32[]{:S(2)}) collective-permute-start(f32[240,128]{1,0:T(8,128)S(1)} %get-tuple-element.16), channel_id=1, source_target_pairs={{28,0},{0,4},{4,8},{8,12},{12,16},{16,20},{20,24},{24,28},{29,1},{... | collective-permute-start | bytes 368648 | tf_op jit(solution)/shard_map/ppermute | solution.py:24
  9.3 7.9 %collective-permute-start.1 = (f32[240,128]{1,0:T(8,128)S(1)}, f32[240,128]{1,0:T(8,128)S(1)}, u32[]{:S(2)}, u32[]{:S(2)}) collective-permute-start(f32[240,128]{1,0:T(8,128)S(1)} %get-tuple-element.17), channel_id=1, source_target_pairs={{4,0},{8,4},{12,8},{16,12},{20,16},{24,20},{28,24},{0,28},{5,1},{9... | collective-permute-start | bytes 368648 | tf_op jit(solution)/shard_map/ppermute | solution.py:24
  10.8 5.2 %collective-permute-start.2 = (f32[96,128]{1,0:T(8,128)S(1)}, f32[96,128]{1,0:T(8,128)S(1)}, u32[]{:S(2)}, u32[]{:S(2)}) collective-permute-start(f32[96,128]{1,0:T(8,128)S(1)} %get-tuple-element.18), channel_id=1, source_target_pairs={{3,0},{0,1},{1,2},{2,3},{7,4},{4,5},{5,6},{6,7},{11,8},{8,9},{9,10... | collective-permute-start | bytes 147464 | tf_op jit(solution)/shard_map/ppermute | solution.py:24
  12.8 4.4 %collective-permute-start.3 = (f32[96,128]{1,0:T(8,128)S(1)}, f32[96,128]{1,0:T(8,128)S(1)}, u32[]{:S(2)}, u32[]{:S(2)}) collective-permute-start(f32[96,128]{1,0:T(8,128)S(1)} %get-tuple-element.19), channel_id=1, source_target_pairs={{1,0},{2,1},{3,2},{0,3},{5,4},{6,5},{7,6},{4,7},{9,8},{10,9},{11,1... | collective-permute-start | bytes 147464 | tf_op jit(solution)/shard_map/ppermute | solution.py:24
  13.8 18.4 %copy-start.3 = (f32[16,128,128]{2,1,0:T(8,128)S(1)}, f32[16,128,128]{2,1,0:T(8,128)}, u32[]{:S(2)}) copy-start(f32[16,128,128]{2,1,0:T(8,128)} %remap.6) | copy-start | bytes 3145732
  18.6 18.4 %copy-start.6 = (f32[4,8,64,128]{3,2,1,0:T(8,128)S(1)}, f32[4,8,64,128]{3,2,1,0:T(8,128)}, u32[]{:S(2)}) copy-start(f32[4,8,64,128]{3,2,1,0:T(8,128)} %param.19) | copy-start | bytes 3145732
  18.6 18.4 %copy-start.8 = (s32[64,128]{1,0:T(8,128)S(1)}, s32[64,128]{1,0:T(8,128)}, u32[]{:S(2)}) copy-start(s32[64,128]{1,0:T(8,128)} %wet.5) | copy-start | bytes 98308
  18.6 18.4 %copy-start.10 = (f32[4]{0:T(128)S(1)}, f32[4]{0:T(128)}, u32[]{:S(2)}) copy-start(f32[4]{0:T(128)} %mixing.1) | copy-start | bytes 52
  34.4 13.8 %all-to-all-start.1 = ((f32[32,16,128]{2,1,0:T(8,128)}), f32[32,16,128]{2,1,0:T(8,128)S(1)}, u32[]{:S(2)}, u32[]{:S(2)}) async-start(f32[32,16,128]{2,1,0:T(8,128)} %bitcast.9), calls=%async_computation.1 | async-start | bytes 524288 | tf_op jit(solution)/shard_map/all_to_all | solution.py:502
  40.3 27.1 %copy-start.1 = (f32[10,20,16,128]{3,2,1,0:T(8,128)S(1)}, f32[10,20,16,128]{3,2,1,0:T(8,128)}, u32[]{:S(2)}) copy-start(f32[10,20,16,128]{3,2,1,0:T(8,128)} %state.1) | copy-start | bytes 4915204
  60.3 1.2 %copy-start.4 = (f32[16,128,128]{2,1,0:T(8,128)S(1)}, f32[16,128,128]{2,1,0:T(8,128)}, u32[]{:S(2)}) copy-start(f32[16,128,128]{2,1,0:T(8,128)} %remap.6) | copy-start | bytes 3145732
  63.9 27.1 %all-to-all-start.3 = ((f32[16,8,128]{2,1,0:T(8,128)}), f32[16,8,128]{2,1,0:T(8,128)S(1)}, u32[]{:S(2)}, u32[]{:S(2)}) async-start(f32[16,8,128]{2,1,0:T(8,128)} %bitcast.15), calls=%async_computation.3 | async-start | bytes 131072 | tf_op jit(solution)/shard_map/all_to_all | solution.py:551
  76.7 9.1 %collective-permute-start.4 = (f32[200,128]{1,0:T(8,128)S(1)}, f32[200,128]{1,0:T(8,128)S(1)}, u32[]{:S(2)}, u32[]{:S(2)}) collective-permute-start(f32[200,128]{1,0:T(8,128)S(1)} %get-tuple-element.21), channel_id=1, source_target_pairs={{28,0},{0,4},{4,8},{8,12},{12,16},{16,20},{20,24},{24,28},{29,1},{... | collective-permute-start | bytes 307208 | tf_op jit(solution)/shard_map/ppermute | solution.py:24
  78.6 7.3 %collective-permute-start.5 = (f32[200,128]{1,0:T(8,128)S(1)}, f32[200,128]{1,0:T(8,128)S(1)}, u32[]{:S(2)}, u32[]{:S(2)}) collective-permute-start(f32[200,128]{1,0:T(8,128)S(1)} %get-tuple-element.22), channel_id=1, source_target_pairs={{4,0},{8,4},{12,8},{16,12},{20,16},{24,20},{28,24},{0,28},{5,1},{9... | collective-permute-start | bytes 307208 | tf_op jit(solution)/shard_map/ppermute | solution.py:24
  80.3 4.6 %collective-permute-start.6 = (f32[32,128]{1,0:T(8,128)S(1)}, f32[32,128]{1,0:T(8,128)S(1)}, u32[]{:S(2)}, u32[]{:S(2)}) collective-permute-start(f32[32,128]{1,0:T(8,128)S(1)} %get-tuple-element.23), channel_id=1, source_target_pairs={{3,0},{0,1},{1,2},{2,3},{7,4},{4,5},{5,6},{6,7},{11,8},{8,9},{9,10... | collective-permute-start | bytes 49160 | tf_op jit(solution)/shard_map/ppermute | solution.py:24
  82.1 3.7 %collective-permute-start.7 = (f32[32,128]{1,0:T(8,128)S(1)}, f32[32,128]{1,0:T(8,128)S(1)}, u32[]{:S(2)}, u32[]{:S(2)}) collective-permute-start(f32[32,128]{1,0:T(8,128)S(1)} %get-tuple-element.24), channel_id=1, source_target_pairs={{1,0},{2,1},{3,2},{0,3},{5,4},{6,5},{7,6},{4,7},{9,8},{10,9},{11,1... | collective-permute-start | bytes 49160 | tf_op jit(solution)/shard_map/ppermute | solution.py:24
  (1 other events, 0.8 us)
where the time goes:
time: 93.7 us; the launch traced here: 93.2 us
  Pallas kernels  29.9 us (32%)
  blocking collectives  23.8 us (25%)
  starting transfers between devices  20.1 us (21%)
  waiting for transfers between devices  13.9 us (15%)
  local copies, waits for them, and re-layouts  4.71 us (5%)
    ppermute x8, starting transfers between devices, shifted(): return lax.ppermute(block, axis, route)  14.1 us
    all_to_all x1, blocking collectives, on_device(): lax.all_to_all(pieces.reshape(targets, CAPACITY * PIECE_ROWS, width), SEC...  13.6 us
    all_to_all x1, blocking collectives, on_device(): lax.all_to_all(answers.reshape(targets, CAPACITY * sea_fields, width), SE...  10.1 us
    pallas_call x1, Pallas kernels, on_device(): call(functools.partial(atmos_kernel, (fields, levels, rows), True), 'firs...  9.35 us
    all_to_all x1, waiting for transfers between devices, on_device(): lax.all_to_all(outgoing.reshape(devices, FLUX_ROWS, width), EVERY, 0, 0,...  7.89 us
    ppermute x8, waiting for transfers between devices, shifted(): return lax.ppermute(block, axis, route)  5.99 us
    pallas_call x1, Pallas kernels, on_device(): call(functools.partial(atmos_kernel, (fields, levels, rows), False), 'sec...  5.11 us
    unnamed x30, local copies, waits for them, and re-layouts  4.71 us
  transfers between devices with their start and end apart: 10, of which 5 were waited for; matrix products, arithmetic and copies ran while one was open for 0% of the time, Pallas kernels for 19%

commit v1 on v0

v1 whole, which is shorter than its diff:
```python
import functools

import jax
import jax.numpy as jnp
from jax import lax
from jax.experimental import pallas as pl
from jax.experimental.pallas import tpu as pltpu
from jax.sharding import PartitionSpec as P

F32 = jnp.float32
BF16 = jnp.bfloat16
FORCING_SCALE = (0.1, -0.1, 0.1, 0.1)
SECTION = ("gx", "gy")
EVERY = ("comp", "gx", "gy")
CAPACITY = 2
PIECE_ROWS = 12
VMEM_LIMIT = 8 * 1024 * 1024
STREAM_LIMIT = 60 * 1024 * 1024


def shifted(block, axis, distance):
    devices = range(lax.axis_size(axis))
    route = [((i - distance) % len(devices), i) for i in devices]
    return lax.ppermute(block, axis, route)


def dot(left, right, transposed=False):
    dims = (((1,), (1 if transposed else 0,)), ((), ()))
    return lax.dot_general(left, right, dims, preferred_element_type=F32)


def halves(values):
    high = values.astype(BF16)
    return high, (values - high.astype(F32)).astype(BF16)


def remapped(rows, weights):
    count, width = rows.shape
    high, low = halves(rows)
    if count < 16:
        filler = jnp.zeros((16 - count, width), F32)
        high, low = halves(jnp.concatenate([rows, filler], axis=0))
    left = jnp.concatenate(
        [
            jnp.concatenate([high, high], axis=1),
            jnp.concatenate([low, jnp.zeros(low.shape, BF16)], axis=1),
        ],
        axis=0,
    )
    product = dot(left, weights)
    return product[:count, :] + product[16 : 16 + count, :]


def both_halves(block):
    return jnp.concatenate(halves(block), axis=0)


def weights_kernel(transposed, remap, weights):
    for tile in range(remap.shape[0]):
        block = remap[tile]
        weights[tile] = both_halves(jnp.transpose(block) if transposed else block)


def picked(selection, values):
    chosen = selection.astype(BF16)
    high = values.astype(BF16)
    rest = values - high.astype(F32)
    middle = rest.astype(BF16)
    low = (rest - middle.astype(F32)).astype(BF16)
    return dot(chosen, high) + dot(chosen, middle) + dot(chosen, low)


def one_hot(labels):
    lanes = lax.broadcasted_iota(jnp.int32, labels.shape, 1).astype(F32)
    return (labels == lanes).astype(F32)


def grid_index(shape):
    return lax.broadcasted_iota(jnp.int32, shape, 0), lax.broadcasted_iota(jnp.int32, shape, 1)


def around(cells, north, south, west, east):
    rows, lanes = grid_index(cells.shape)
    row_count, width = cells.shape
    return (
        jnp.where(rows == 0, north, pltpu.roll(cells, 1, 0)),
        jnp.where(rows == row_count - 1, south, pltpu.roll(cells, row_count - 1, 0)),
        jnp.where(lanes == 0, west, pltpu.roll(cells, 1, 1)),
        jnp.where(lanes == width - 1, east, pltpu.roll(cells, width - 1, 1)),
    )


def diffused(cells, upper, lower, sides, diffusion):
    beside = sides[0] + sides[1] + sides[2] + sides[3] - 4.0 * cells
    return cells + diffusion * beside + 0.1 * (upper + lower - 2.0 * cells)


class Edges:
    def __init__(self, fields, levels, rows, sea_blocks, sea_rows, width):
        self.fields, self.levels, self.rows, self.width = fields, levels, rows, width
        self.sea_blocks, self.sea_rows = sea_blocks, sea_rows
        self.half = fields // 2
        self.part = self.half * levels
        self.part_rows = -(-self.part // 8) * 8
        self.atmos_rows = 2 * self.part_rows
        self.wet_row = self.atmos_rows + sea_blocks
        self.near_rows = -(-(self.wet_row + 1) // 8) * 8
        self.corner_row = self.atmos_rows
        self.far_rows = self.atmos_rows + 8
        self.sea_tiles = sea_blocks * sea_rows // width
        self.sea_cols = 4 * rows
        self.sea_col_rows = -(-(self.sea_tiles + 1) // 8) * 8
        self.col_rows = self.sea_cols + self.sea_col_rows


def squared(values):
    rows, width = values.shape
    if rows == width:
        return values
    return jnp.concatenate([values, jnp.zeros((width - rows, width), F32)], axis=0)


def chunk(source, target, at, rows, arrival):
    part = pl.ds(pl.multiple_of(at * rows, 8), rows)
    return pltpu.make_async_copy(source.at[part], target.at[part], arrival)


def edges_kernel(
    at,
    state_far,
    ocean_far,
    wet_far,
    near_first,
    near_last,
    far_first,
    far_last,
    first,
    last,
    state,
    ocean,
    wet,
    arrivals,
):
    rows, part, width = at.rows, at.part, at.width
    field_rows = at.levels * rows
    sea_parts = 4
    copies = [
        chunk(state_far, state, field, field_rows, arrivals.at[field])
        for field in range(at.fields)
    ]
    copies += [
        chunk(ocean_far, ocean, field, ocean.shape[0] // sea_parts, arrivals.at[at.fields + field])
        for field in range(sea_parts)
    ]
    copies.append(pltpu.make_async_copy(wet_far, wet, arrivals.at[at.fields + sea_parts]))
    for copy in copies:
        copy.start()
    for out in (near_first, near_last, far_first, far_last):
        out[...] = jnp.zeros(out.shape, F32)
    for cols in (first, last):
        cols[pl.ds(at.sea_cols, at.sea_col_rows), :] = jnp.zeros((at.sea_col_rows, width), F32)
    for half in range(2):
        for field in range(half * at.half, (half + 1) * at.half):
            copies[field].wait()
        for row in range(rows):
            lines = state[pl.ds(half * part * rows + row, part, stride=rows), :]
            held = pl.ds(half * at.part_rows, part)
            if row < 2:
                (near_first, far_first)[row][held, :] = lines
            if row >= rows - 2:
                (near_last, far_last)[rows - 1 - row][held, :] = lines
            turned = jnp.transpose(squared(lines))
            near, far = half * rows + row, (2 + half) * rows + row
            first[pl.ds(near, 1), :] = turned[0:1, :]
            first[pl.ds(far, 1), :] = turned[1:2, :]
            last[pl.ds(near, 1), :] = turned[width - 1 : width, :]
            last[pl.ds(far, 1), :] = turned[width - 2 : width - 1, :]
    for copy in copies[at.fields :]:
        copy.wait()
    for out, sea_row in ((near_first, 0), (near_last, at.sea_rows - 1)):
        out[pl.ds(at.atmos_rows, at.sea_blocks), :] = ocean[
            pl.ds(sea_row, at.sea_blocks, stride=at.sea_rows), :
        ]
        out[pl.ds(at.wet_row, 1), :] = wet[pl.ds(sea_row, 1), :].astype(F32)
    for tile in range(at.sea_tiles + 1):
        if tile < at.sea_tiles:
            lines = ocean[pl.ds(tile * width, width), :]
        else:
            lines = squared(wet[...].astype(F32))
        turned = jnp.transpose(lines)
        first[pl.ds(at.sea_cols + tile, 1), :] = turned[0:1, :]
        last[pl.ds(at.sea_cols + tile, 1), :] = turned[width - 1 : width, :]


def corners_kernel(at, far_first, far_last, west, east, to_north, to_south):
    for out, lines, row in ((to_north, far_first, 0), (to_south, far_last, at.rows - 1)):
        out[...] = lines[...]
        for place, (cols, half) in enumerate(((west, 0), (west, 1), (east, 0), (east, 1))):
            out[pl.ds(at.corner_row + place, 1), :] = cols[pl.ds(half * at.rows + row, 1), :]


def spread(at, diffusion, part, places):
    numbers = jnp.zeros(places.shape, F32)
    is_first = places < 0
    is_last = places < 0
    for field in range(at.half):
        start = field * at.levels
        numbers = jnp.where(places >= start, diffusion[part * at.half + field], numbers)
        is_first = is_first | (places == start)
        is_last = is_last | (places == start + at.levels - 1)
    return numbers, is_first, is_last


def ring_step(at, part, halos, edges, diffusion, outs):
    north, south, west, east, far_north, far_south = halos
    near_first, near_last, first, last = edges
    rows, width = at.rows, at.width
    shape = (at.part_rows, width)
    held = pl.ds(part * at.part_rows, shape[0])
    lines, lanes = grid_index(shape)
    numbers, is_first, is_last = spread(at, diffusion, part, lines)
    for out, outside, further, own, is_north in (
        (outs[0], north, far_north, near_first, True),
        (outs[1], south, far_south, near_last, False),
    ):
        turned = jnp.transpose(squared(further[pl.ds(at.corner_row, 8), :]))[: shape[0], :]
        cells, beyond, inside = outside[held, :], further[held, :], own[held, :]
        west_col = jnp.where(lanes == 0, turned[:, part : part + 1], pltpu.roll(cells, 1, 1))
        east_col = jnp.where(
            lanes == width - 1, turned[:, 2 + part : 3 + part], pltpu.roll(cells, width - 1, 1)
        )
        sides = (
            beyond if is_north else inside,
            inside if is_north else beyond,
            west_col,
            east_col,
        )
        upper = jnp.where(is_first, cells, pltpu.roll(cells, 1, 0))
        lower = jnp.where(is_last, cells, pltpu.roll(cells, shape[0] - 1, 0))
        out[...] = diffused(cells, upper, lower, sides, numbers)

    shape = (rows, width)
    near, far = pl.ds(part * rows, rows), pl.ds((2 + part) * rows, rows)
    lines, lanes = grid_index(shape)
    numbers, is_first, is_last = spread(at, diffusion, part, lanes)
    for out, outside, own, corner, is_west in (
        (outs[2], west, first, 0, True),
        (outs[3], east, last, 2, False),
    ):
        cells, beyond, inside = outside[near, :], outside[far, :], own[near, :]
        place = pl.ds(at.corner_row + corner + part, 1)
        sides = (
            jnp.where(lines == 0, far_north[place, :], pltpu.roll(cells, 1, 0)),
            jnp.where(lines == rows - 1, far_south[place, :], pltpu.roll(cells, rows - 1, 0)),
            beyond if is_west else inside,
            inside if is_west else beyond,
        )
        upper = jnp.where(is_first, cells, pltpu.roll(cells, 1, 1))
        lower = jnp.where(is_last, cells, pltpu.roll(cells, width - 1, 1))
        out[...] = diffused(cells, upper, lower, sides, numbers)


def field_step(at, field, state, out, north, south, first_line, west_cols, east_cols, number):
    levels, rows, width = at.levels, at.rows, at.width
    lines, lanes = grid_index((rows, width))
    for level in range(levels):
        line = first_line + field * levels + level
        start = pl.multiple_of((field * levels + level) * rows, rows)
        cells = state[pl.ds(start, rows), :]
        first_level, last_level = level == 0, level == levels - 1
        upper = cells if first_level else state[pl.ds(start - rows, rows), :]
        lower = cells if last_level else state[pl.ds(start + rows, rows), :]
        sides = (
            jnp.where(lines == 0, north[pl.ds(line, 1), :], pltpu.roll(cells, 1, 0)),
            jnp.where(
                lines == rows - 1, south[pl.ds(line, 1), :], pltpu.roll(cells, rows - 1, 0)
            ),
            jnp.where(lanes == 0, pltpu.roll(west_cols, (width - level) % width, 1), pltpu.roll(cells, 1, 1)),
            jnp.where(
                lanes == width - 1,
                pltpu.roll(east_cols, width - 1 - level, 1),
                pltpu.roll(cells, width - 1, 1),
            ),
        )
        out[pl.ds(start, rows), :] = diffused(cells, upper, lower, sides, number)


def steps_kernel(
    at,
    part,
    state_far,
    north,
    south,
    west,
    east,
    far_north,
    far_south,
    near_first,
    near_last,
    first,
    last,
    diffusion,
    *rest,
):
    if part:
        rest = rest[1:]
    out_far, state, middle, out, *ring, arrivals, departures = rest
    rows, width, levels = at.rows, at.width, at.levels
    field_rows = levels * rows
    whole = part * at.half

    def coming(field):
        return pltpu.make_async_copy(
            state_far.at[pl.ds(pl.multiple_of((whole + field) * field_rows, 8), field_rows)],
            state.at[pl.ds(pl.multiple_of(field * field_rows, 8), field_rows)],
            arrivals.at[field],
        )

    def going(field):
        return pltpu.make_async_copy(
            out.at[pl.ds(pl.multiple_of(field * field_rows, 8), field_rows)],
            out_far.at[pl.ds(pl.multiple_of((whole + field) * field_rows, 8), field_rows)],
            departures.at[field],
        )

    for field in range(at.half):
        coming(field).start()
    halos = (north, south, west, east, far_north, far_south)
    ring_step(at, part, halos, (near_first, near_last, first, last), diffusion, ring)
    held = pl.ds(part * rows, rows)

    def both_steps(field, carry):
        back = lax.rem(width - field * levels, width)
        number = diffusion[whole + field]
        west_cols = pltpu.roll(west[held, :], back, 1)
        east_cols = pltpu.roll(east[held, :], back, 1)
        coming(field).wait()
        line = part * at.part_rows
        field_step(at, field, state, middle, north, south, line, west_cols, east_cols, number)
        west_cols = pltpu.roll(ring[2][...], back, 1)
        east_cols = pltpu.roll(ring[3][...], back, 1)
        field_step(at, field, middle, out, ring[0], ring[1], 0, west_cols, east_cols, number)
        going(field).start()
        return carry

    lax.fori_loop(0, at.half, both_steps, 0)
    for field in range(at.half):
        going(field).wait()


def ocean_kernel(
    at,
    levels,
    ocean_far,
    wet,
    north,
    south,
    west,
    east,
    mixing,
    out_far,
    ocean,
    out,
    wests,
    easts,
    arrivals,
    departures,
):
    fields, field_rows = at.sea_blocks // levels, levels * at.sea_rows
    for field in range(fields):
        chunk(ocean_far, ocean, field, field_rows, arrivals.at[field]).start()
    rows, width = at.sea_rows, at.width
    lines, lanes = grid_index((rows, width))
    per_tile = width // rows
    held = pl.ds(at.sea_cols, at.sea_col_rows)
    wests[...] = jnp.transpose(squared(west[held, :]))
    easts[...] = jnp.transpose(squared(east[held, :]))
    wet_cells = wet[...].astype(F32)
    wet_lane = at.sea_tiles
    wet_sides = around(
        wet_cells,
        north[pl.ds(at.wet_row, 1), :],
        south[pl.ds(at.wet_row, 1), :],
        wests[pl.ds(0, rows), :][:, wet_lane : wet_lane + 1],
        easts[pl.ds(0, rows), :][:, wet_lane : wet_lane + 1],
    )

    def field_step(field, carry):
        chunk(ocean_far, ocean, field, field_rows, arrivals.at[field]).wait()
        back = lax.rem(width - field * (levels // per_tile), width)
        west_cols = pltpu.roll(wests[...], back, 1)
        east_cols = pltpu.roll(easts[...], back, 1)
        number = mixing[field] * wet_cells
        for level in range(levels):
            block = field * levels + level
            start = pl.multiple_of(block * rows, rows)
            first_level, last_level = level == 0, level == levels - 1
            cells = ocean[pl.ds(start, rows), :]
            upper = cells if first_level else ocean[pl.ds(start - rows, rows), :]
            lower = cells if last_level else ocean[pl.ds(start + rows, rows), :]
            above = pltpu.roll(cells, 1, 0)
            below = pltpu.roll(cells, rows - 1, 0)
            line = at.atmos_rows + block
            tile, within = level // per_tile, (level % per_tile) * rows
            west_col = pltpu.roll(west_cols[within : within + rows, :], (width - tile) % width, 1)
            east_col = pltpu.roll(east_cols[within : within + rows, :], width - 1 - tile, 1)
            sides = (
                jnp.where(lines == 0, north[pl.ds(line, 1), :], above),
                jnp.where(lines == rows - 1, south[pl.ds(line, 1), :], below),
                jnp.where(lanes == 0, west_col, pltpu.roll(cells, 1, 1)),
                jnp.where(lanes == width - 1, east_col, pltpu.roll(cells, width - 1, 1)),
            )
            total = wet_sides[0] * (sides[0] - cells)
            for side in range(1, 4):
                total = total + wet_sides[side] * (sides[side] - cells)
            tendency = number * total + 0.1 * (upper + lower - 2.0 * cells)
            out[pl.ds(start, rows), :] = cells + wet_cells * tendency
        chunk(out, out_far, field, field_rows, departures.at[field]).start()
        return carry

    lax.fori_loop(0, fields, field_step, 0)
    for field in range(fields):
        chunk(out, out_far, field, field_rows, departures.at[field]).wait()


def ranks_of(index, row, count, tally):
    def clear(at, carry):
        tally[at] = 0
        return carry

    lax.fori_loop(0, tally.shape[0], clear, 0)
    places = []
    for entry in range(count):
        owner = index[row, entry]
        rank = tally[owner]
        tally[owner] = rank + 1
        places.append((owner, rank))
    return places


def inner_kernel(at, state_far, diffusion, out, top, arrival):
    fields, rows, width = at.fields, at.rows, at.width
    copy = pltpu.make_async_copy(state_far.at[:, pl.ds(at.levels - 2, 2)], top, arrival)
    copy.start()
    lines, lanes = grid_index((rows, width))
    copy.wait()
    for field in range(fields):
        cells = top[field, 1]
        sides = (
            jnp.where(lines == 0, 0.0, pltpu.roll(cells, 1, 0)),
            jnp.where(lines == rows - 1, 0.0, pltpu.roll(cells, rows - 1, 0)),
            jnp.where(lanes == 0, 0.0, pltpu.roll(cells, 1, 1)),
            jnp.where(lanes == width - 1, 0.0, pltpu.roll(cells, width - 1, 1)),
        )
        out[pl.ds(field * rows, rows), :] = diffused(
            cells, top[field, 0], cells, sides, diffusion[field]
        )


def pieces_kernel(
    at, targets, inner, north, south, west, east, weights, index, diffusion, out, surface, tally
):
    fields, levels, rows, width = at.fields, at.levels, at.rows, at.width
    lines, lanes = grid_index((rows, width))
    for field in range(fields):
        part = field // at.half
        held = pl.ds(part * rows, rows)
        lane = (field % at.half) * levels + levels - 1
        line = pl.ds(part * at.part_rows + lane, 1)
        outside = (
            jnp.where(lines == 0, north[line, :], 0.0)
            + jnp.where(lines == rows - 1, south[line, :], 0.0)
            + jnp.where(lanes == 0, pltpu.roll(west[held, :], (width - lane) % width, 1), 0.0)
            + jnp.where(lanes == width - 1, pltpu.roll(east[held, :], width - 1 - lane, 1), 0.0)
        )
        here = pl.ds(field * rows, rows)
        surface[here, :] = inner[here, :] + diffusion[field] * outside
    surface[pl.ds(fields * rows, (16 - fields) * rows), :] = jnp.zeros(
        ((16 - fields) * rows, width), F32
    )
    out[...] = jnp.zeros(out.shape, F32)
    slots = targets * CAPACITY
    for row in (fields, fields + 1):
        out[pl.ds(row, slots, stride=PIECE_ROWS), :] = jnp.full((slots, width), -1.0, F32)
    places = ranks_of(index, 2, rows, tally)
    for tile in range(rows):
        owner, rank = places[tile]
        start = (owner * CAPACITY + rank) * PIECE_ROWS
        label = jnp.full((1, width), index[3, tile].astype(F32))
        out[pl.ds(start + fields + 1, 1), :] = label
    places = ranks_of(index, 0, rows, tally)
    for tile in range(rows):
        owner, rank = places[tile]
        start = (owner * CAPACITY + rank) * PIECE_ROWS
        piece = remapped(surface[pl.ds(tile, 16, stride=rows), :], weights[tile])[:fields, :]
        label = jnp.full((1, width), index[1, tile].astype(F32))
        out[pl.ds(start, fields), :] = piece
        out[pl.ds(start + fields, 1), :] = label


def flux_kernel(sizes, arrived, remap, index, out, gather, sea_labels, fluxes, tally):
    fields, flux_count, rows, targets, sections = sizes
    width = out.shape[1]
    slots = targets * CAPACITY
    select = one_hot(arrived[pl.ds(fields, slots, stride=PIECE_ROWS), :])
    gather[...] = select
    sea_labels[...] = arrived[pl.ds(fields + 1, slots, stride=PIECE_ROWS), :]
    values = jnp.concatenate(
        [arrived[pl.ds(field, slots, stride=PIECE_ROWS), :] for field in range(fields)], axis=1
    )
    exchange = picked(jnp.transpose(select)[:rows, :], values)
    a = [exchange[:, field * width : (field + 1) * width] for field in range(fields)]
    speed = jnp.sqrt(a[2] * a[2] + a[3] * a[3] + 0.5)
    fluxes[pl.ds(0, rows), :] = speed * (a[0] - a[4]) + a[6] + a[7]
    fluxes[pl.ds(rows, rows), :] = speed * a[1] + a[5] + a[8]
    fluxes[pl.ds(2 * rows, rows), :] = speed * a[2] * (1.0 + 0.2 * jnp.tanh(a[9]))
    fluxes[pl.ds(3 * rows, rows), :] = speed * a[3]
    out[...] = jnp.zeros(out.shape, F32)
    places = ranks_of(index, 2, rows, tally)
    for tile in range(rows):
        owner, rank = places[tile]
        mapped = remapped(fluxes[pl.ds(tile, flux_count, stride=rows), :], both_halves(remap[tile]))
        for section in range(sections):
            start = ((section * targets + owner) * CAPACITY + rank) * flux_count
            out[pl.ds(start, flux_count), :] = mapped


def sea_kernel(
    sizes,
    landed,
    wet,
    own_labels,
    other_labels,
    own,
    base,
    out,
    answers,
    tops,
    before,
    wet_here,
    arrivals,
    departures,
):
    flux_count, sea_rows, targets = sizes
    fetched = [
        pltpu.make_async_copy(
            out.at[flux, 0], before.at[pl.ds(flux * sea_rows, sea_rows)], arrivals.at[flux]
        )
        for flux in range(flux_count)
    ]
    fetched.append(pltpu.make_async_copy(wet, wet_here, arrivals.at[flux_count]))
    for copy in fetched:
        copy.start()
    width = landed.shape[1]
    slots = targets * CAPACITY
    mine = one_hot(own_labels[...])
    others = one_hot(other_labels[...])
    is_first = own[0] == 0
    select = jnp.concatenate(
        [jnp.where(is_first, mine, others), jnp.where(is_first, others, mine)], axis=0
    )
    values = jnp.concatenate(
        [landed[pl.ds(flux, 2 * slots, stride=flux_count), :] for flux in range(flux_count)], axis=1
    )
    forcing = picked(jnp.transpose(select)[:sea_rows, :], values)
    for copy in fetched:
        copy.wait()
    wet_cells = wet_here[...].astype(F32)
    copies = []
    for flux in range(flux_count):
        held = pl.ds(flux * sea_rows, sea_rows)
        tops[held, :] = before[held, :] + wet_cells * (
            FORCING_SCALE[flux] * forcing[:, flux * width : (flux + 1) * width]
        )
        copies.append(
            pltpu.make_async_copy(tops.at[held], out.at[flux, 0], departures.at[flux])
        )
        copies[flux].start()
    all_tops = jnp.concatenate(
        [tops[pl.ds(flux * sea_rows, sea_rows), :] for flux in range(flux_count)], axis=1
    )
    reply = picked(mine[:, :sea_rows], all_tops)
    for flux in range(flux_count):
        answers[pl.ds(flux, slots, stride=flux_count), :] = reply[
            :, flux * width : (flux + 1) * width
        ]
    for copy in copies:
        copy.wait()


def reply_kernel(sizes, answered, remap, index, gather, out, on_exchange, tally):
    flux_count, rows, targets = sizes
    width = out.shape[1]
    slots = targets * CAPACITY
    places = ranks_of(index, 2, rows, tally)
    for tile in range(rows):
        owner, rank = places[tile]
        start = (owner * CAPACITY + rank) * flux_count
        on_exchange[pl.ds(tile * flux_count, flux_count), :] = remapped(
            answered[pl.ds(start, flux_count), :], both_halves(jnp.transpose(remap[tile]))
        )
    values = jnp.concatenate(
        [on_exchange[pl.ds(flux, rows, stride=flux_count), :] for flux in range(flux_count)], axis=1
    )
    replies = picked(gather[...][:, :rows], values)
    for flux in range(flux_count):
        out[pl.ds(flux, slots, stride=flux_count), :] = replies[
            :, flux * width : (flux + 1) * width
        ]


def surface_kernel(sizes, returned, weights, index, out, tally):
    flux_count, rows, targets = sizes
    places = ranks_of(index, 0, rows, tally)
    for tile in range(rows):
        owner, rank = places[tile]
        start = (owner * CAPACITY + rank) * flux_count
        out[pl.ds(tile, flux_count, stride=rows), :] = remapped(
            returned[pl.ds(start, flux_count), :], weights[tile]
        )


VMEM = pl.BlockSpec(memory_space=pltpu.VMEM)
SMEM = pl.BlockSpec(memory_space=pltpu.SMEM)
ANY = pl.BlockSpec(memory_space=pl.ANY)


def array(*shape):
    return jax.ShapeDtypeStruct(shape, F32)


def call(kernel, name, outs, in_specs, scratch=(), after=(), limit=VMEM_LIMIT, work=1_000_000, **more):
    def body(*refs):
        kernel(*refs[: len(in_specs)], *refs[len(in_specs) + len(after) :])

    run = pl.pallas_call(
        body,
        name=name,
        out_shape=outs,
        in_specs=list(in_specs) + [ANY] * len(after),
        scratch_shapes=list(scratch),
        compiler_params=pltpu.CompilerParams(vmem_limit_bytes=limit),
        cost_estimate=pl.CostEstimate(flops=0, bytes_accessed=work, transcendentals=0),
        **more,
    )
    return lambda *arguments: run(*arguments, *after)


def on_device(
    atmos_state,
    atmos_diffusion,
    remap_atmos,
    exchange_owner,
    exchange_slot,
    remap_ocean,
    ocean_owner,
    ocean_slot,
    ocean_state,
    ocean_mixing,
    wet_mask,
):
    targets = lax.axis_size(SECTION)
    sections = lax.axis_size("comp")
    devices = targets * sections
    fields, levels, rows, width = atmos_state.shape
    sea_fields, sea_levels, sea_rows, _ = ocean_state.shape
    blocks = fields * levels
    sea_blocks = sea_fields * sea_levels
    at = Edges(fields, levels, rows, sea_blocks, sea_rows, width)
    slots = targets * CAPACITY
    ring = ("comp", "gx")
    tally = pltpu.SMEM((targets,), jnp.int32)

    index = jnp.stack([exchange_owner[:, 0], exchange_slot, ocean_owner[:, 0], ocean_slot])
    section = lax.axis_index("comp").astype(jnp.int32).reshape(1)
    state = atmos_state.reshape(blocks * rows, width)
    ocean = ocean_state.reshape(sea_blocks * sea_rows, width)

    state_copy = pltpu.VMEM((blocks * rows, width), F32)
    ocean_copy = pltpu.VMEM((sea_blocks * sea_rows, width), F32)
    wet_copy = pltpu.VMEM((sea_rows, width), jnp.int32)
    ocean_flags = pltpu.SemaphoreType.DMA((sea_fields,))
    near_first, near_last, far_first, far_last, first_cols, last_cols = call(
        functools.partial(edges_kernel, at),
        "edges",
        (array(at.near_rows, width),) * 2
        + (array(at.far_rows, width),) * 2
        + (array(at.col_rows, width),) * 2,
        [ANY] * 3,
        [state_copy, ocean_copy, wet_copy, pltpu.SemaphoreType.DMA((fields + 5,))],
        limit=STREAM_LIMIT,
    )(state, ocean, wet_mask)
    north = shifted(near_last, ring, 1)
    south = shifted(near_first, ring, -1)
    west = shifted(last_cols, "gy", 1)
    east = shifted(first_cols, "gy", -1)

    def weights_of(remap, transposed, name, before):
        return call(
            functools.partial(weights_kernel, transposed),
            name,
            jax.ShapeDtypeStruct((rows, 2 * width, width), BF16),
            [VMEM],
            after=(before,),
        )(remap)

    inner = call(
        functools.partial(inner_kernel, at),
        "inner",
        array(fields * rows, width),
        [ANY, SMEM],
        [pltpu.VMEM((fields, 2, rows, width), F32), pltpu.SemaphoreType.DMA],
        after=(first_cols,),
    )(atmos_state, atmos_diffusion)
    pieces = call(
        functools.partial(pieces_kernel, at, targets),
        "pieces",
        array(slots * PIECE_ROWS, width),
        [VMEM] * 6 + [SMEM] * 2,
        [pltpu.VMEM((16 * rows, width), F32), tally],
    )(
        inner,
        north,
        south,
        west,
        east,
        weights_of(remap_atmos, False, "piece_weights", first_cols),
        index,
        atmos_diffusion,
    )
    arrived = lax.all_to_all(
        pieces.reshape(targets, CAPACITY * PIECE_ROWS, width), SECTION, 0, 0, tiled=True
    )
    outgoing, gather, own_labels = call(
        functools.partial(flux_kernel, (fields, sea_fields, rows, targets, sections)),
        "fluxes",
        (
            array(devices * CAPACITY * sea_fields, width),
            array(slots, width),
            array(slots, width),
        ),
        [VMEM, VMEM, SMEM],
        [pltpu.VMEM((sea_fields * rows, width), F32), tally],
    )(
        arrived.reshape(slots * PIECE_ROWS, width),
        remap_ocean,
        index,
    )
    landed = lax.all_to_all(
        outgoing.reshape(devices, CAPACITY * sea_fields, width), EVERY, 0, 0, tiled=True
    )
    other_labels = shifted(own_labels, "comp", 1)
    to_north, to_south = call(
        functools.partial(corners_kernel, at),
        "corners",
        (array(at.far_rows, width),) * 2,
        [VMEM] * 4,
        after=(outgoing,),
    )(far_first, far_last, west, east)
    far_north = shifted(to_south, ring, 1)
    far_south = shifted(to_north, ring, -1)

    sea_base = call(
        functools.partial(ocean_kernel, at, sea_levels),
        "sea_base",
        array(sea_blocks * sea_rows, width),
        [ANY] + [VMEM] * 5 + [SMEM],
        [ocean_copy] * 2 + [pltpu.VMEM((width, width), F32)] * 2 + [ocean_flags] * 2,
        after=(outgoing,),
        limit=STREAM_LIMIT,
        work=1_000_000_000,
        out_specs=ANY,
    )(ocean, wet_mask, north, south, west, east, ocean_mixing)

    ocean_next, answers = call(
        functools.partial(sea_kernel, (sea_fields, sea_rows, targets)),
        "sea_top",
        (
            array(sea_fields, sea_levels, sea_rows, width),
            array(slots * sea_fields, width),
        ),
        [VMEM, ANY, VMEM, VMEM, SMEM, ANY],
        [pltpu.VMEM((sea_fields * sea_rows, width), F32)] * 2
        + [wet_copy, pltpu.SemaphoreType.DMA((sea_fields + 1,)), ocean_flags],
        after=(far_north, far_south),
        out_specs=(ANY, VMEM),
        input_output_aliases={5: 0},
    )(
        landed.reshape(devices * CAPACITY * sea_fields, width),
        wet_mask,
        own_labels,
        other_labels,
        section,
        sea_base.reshape(sea_fields, sea_levels, sea_rows, width),
    )
    answered = lax.all_to_all(
        answers.reshape(targets, CAPACITY * sea_fields, width), SECTION, 0, 0, tiled=True
    )
    def both_steps(part, before, **more):
        return call(
            functools.partial(steps_kernel, at, part),
            "steps_" + "ab"[part],
            array(blocks * rows, width),
            [ANY] + [VMEM] * 10 + [SMEM] + [ANY] * part,
            [pltpu.VMEM((at.part * rows, width), F32)] * 3
            + [pltpu.VMEM((at.part_rows, width), F32)] * 2
            + [pltpu.VMEM((rows, width), F32)] * 2
            + [pltpu.SemaphoreType.DMA((at.half,))] * 2,
            after=(before,),
            limit=STREAM_LIMIT,
            work=1_000_000_000,
            out_specs=ANY,
            **more,
        )

    halos = (north, south, west, east, far_north, far_south)
    halos += (near_first, near_last, first_cols, last_cols)
    atmos_next = both_steps(0, answers)(state, *halos, atmos_diffusion)
    answered, atmos_next = lax.optimization_barrier((answered, atmos_next))

    replies = call(
        functools.partial(reply_kernel, (sea_fields, rows, targets)),
        "replies",
        array(slots * sea_fields, width),
        [VMEM, VMEM, SMEM, VMEM],
        [pltpu.VMEM((sea_fields * rows, width), F32), tally],
    )(
        answered.reshape(slots * sea_fields, width),
        remap_ocean,
        index,
        gather,
    )
    returned = lax.all_to_all(
        replies.reshape(targets, CAPACITY * sea_fields, width), SECTION, 0, 0, tiled=True
    )
    atmos_next = both_steps(1, replies, input_output_aliases={12: 0})(
        state, *halos, atmos_diffusion, atmos_next
    )
    ocean_surface = call(
        functools.partial(surface_kernel, (sea_fields, rows, targets)),
        "surface",
        array(sea_fields * rows, width),
        [VMEM, VMEM, SMEM],
        [tally],
    )(
        returned.reshape(slots * sea_fields, width),
        weights_of(remap_atmos, True, "surface_weights", replies),
        index,
    )
    return (
        atmos_next.reshape(atmos_state.shape),
        ocean_next,
        ocean_surface.reshape(sea_fields, rows, width),
    )


def solution(mesh):
    in_specs = (
        P(None, None, ("comp", "gx"), "gy"),
        P(),
        P(("comp", "gx", "gy"), None, None),
        P(("comp", "gx", "gy"), None),
        P(("comp", "gx", "gy")),
        P(("comp", "gx", "gy"), None, None),
        P(("comp", "gx", "gy"), None),
        P(("comp", "gx", "gy")),
        P(None, None, "gx", "gy"),
        P(),
        P("gx", "gy"),
    )
    out_specs = (
        P(None, None, ("comp", "gx"), "gy"),
        P(None, None, "gx", "gy"),
        P(None, ("comp", "gx"), "gy"),
    )
    return jax.shard_map(
        on_device, mesh=mesh, in_specs=in_specs, out_specs=out_specs, check_vma=False
    )
```

time: 93.7 us -> 76.6 us (0.82)
  blocking collectives: 23.8 us -> 13.9 us
  waiting for transfers between devices: 13.9 us -> 7.08 us
  starting transfers between devices: 20.1 us -> 24.3 us
  local copies, waits for them, and re-layouts: 4.71 us -> 0.88 us
  Pallas kernels: 29.9 us -> 28.8 us
    all_to_all x1 -> x0, blocking collectives: 10.1 us -> none  [on_device(): lax.all_to_all(answers.reshape(targets, CAPACITY * sea_fields, width), SE...]
    all_to_all x1 -> x2, waiting for transfers between devices: 7.89 us -> 1.92 us  [the longest x1 1.91 us: on_device(): lax.all_to_all(answers.reshape(targets, CAPACITY * sea_fields, width), SE...]
    all_to_all x1 -> x2, starting transfers between devices: 2.59 us -> 7.93 us  [the longest x1 5.21 us: on_device(): lax.all_to_all(answers.reshape(targets, CAPACITY * sea_fields, width), SE...]
    unnamed x30 -> x36, local copies, waits for them, and re-layouts: 4.71 us -> 0.88 us
    ppermute x8 -> x7, starting transfers between devices: 14.1 us -> 11.4 us  [shifted(): return lax.ppermute(block, axis, route)]
    ppermute x8 -> x7, waiting for transfers between devices: 5.99 us -> 3.58 us  [shifted(): return lax.ppermute(block, axis, route)]
    all_to_all x1, waiting for transfers between devices: 0.01 us -> 1.58 us  [on_device(): lax.all_to_all(replies.reshape(targets, CAPACITY * sea_fields, width), SE...]
    all_to_all x1, starting transfers between devices: 3.49 us -> 5 us  [on_device(): lax.all_to_all(replies.reshape(targets, CAPACITY * sea_fields, width), SE...]
  transfers between devices with their start and end apart: 10 -> 10, of which waited for: 5 -> 6; matrix products, arithmetic and copies ran while one was open for 0% -> 0% of each run, Pallas kernels for 19% -> 22%
where the time goes in v1:
time: 76.6 us; the launch traced here: 75.9 us
  Pallas kernels  28.8 us (38%)
  starting transfers between devices  24.3 us (32%)
  blocking collectives  13.9 us (18%)
  waiting for transfers between devices  7.08 us (9%)
  between operations  0.94 us (1%)
  local copies, waits for them, and re-layouts  0.88 us (1%)
    pallas_call x13, Pallas kernels, call(): return lambda *arguments: run(*arguments, *after)  28.8 us
    all_to_all x1, blocking collectives, on_device(): lax.all_to_all(pieces.reshape(targets, CAPACITY * PIECE_ROWS, width), SEC...  13.9 us
    ppermute x7, starting transfers between devices, shifted(): return lax.ppermute(block, axis, route)  11.4 us
    all_to_all x1, starting transfers between devices, on_device(): lax.all_to_all(answers.reshape(targets, CAPACITY * sea_fields, width), SE...  5.21 us
    all_to_all x1, starting transfers between devices, on_device(): lax.all_to_all(replies.reshape(targets, CAPACITY * sea_fields, width), SE...  5 us
    ppermute x7, waiting for transfers between devices, shifted(): return lax.ppermute(block, axis, route)  3.58 us
    all_to_all x1, starting transfers between devices, on_device(): lax.all_to_all(outgoing.reshape(devices, CAPACITY * sea_fields, width), E...  2.72 us
    all_to_all x1, waiting for transfers between devices, on_device(): lax.all_to_all(answers.reshape(targets, CAPACITY * sea_fields, width), SE...  1.91 us
  transfers between devices with their start and end apart: 10, of which 6 were waited for; matrix products, arithmetic and copies ran while one was open for 0% of the time, Pallas kernels for 22%

profile of v1, /device:TPU:0, one launch (start us, length us, event | category | flops | bytes accessed | tf_op | source)
XLA Modules:
  0.0 75.9 jit_solution(15584883604958778439)
XLA Ops:
  0.7 3.3 %edges.1 = (f32[248,128]{1,0:T(8,128)}, f32[248,128]{1,0:T(8,128)}, f32[216,128]{1,0:T(8,128)}, f32[216,128]{1,0:T(8,128)}, f32[88,128]{1,0:T(8,128)}, /*index=5*/f32[88,128]{1,0:T(8,128)}) custom-call(f32[3200,128]{1,0:T(8,128)} %bitcast.18, f32[2048,128]{1,0:T(8,128)} %bitcast.28, s32[64,128]{1,0:T(8,128)} %refs_1_.8), custom_call_target="tpu_custom_call" | custom-call | bytes 1000000 | tf_op jit(solution)/shard_map/edges/pallas_call | solution.py:646
  4.0 3.1 %collective-permute-start = (f32[248,128]{1,0:T(8,128)}, f32[248,128]{1,0:T(8,128)S(1)}, u32[]{:S(2)}, u32[]{:S(2)}) collective-permute-start(f32[248,128]{1,0:T(8,128)} %get-tuple-element.18.refs_8_), channel_id=1, source_target_pairs={{28,0},{0,4},{4,8},{8,12},{12,16},{16,20},{20,24},{24,28},{29,1},{... | collective-permute-start | bytes 380936 | tf_op jit(solution)/shard_map/ppermute | solution.py:24
  7.1 1.5 %collective-permute-start.1 = (f32[248,128]{1,0:T(8,128)}, f32[248,128]{1,0:T(8,128)S(1)}, u32[]{:S(2)}, u32[]{:S(2)}) collective-permute-start(f32[248,128]{1,0:T(8,128)} %get-tuple-element.19.refs_7_), channel_id=1, source_target_pairs={{4,0},{8,4},{12,8},{16,12},{20,16},{24,20},{28,24},{0,28},{5,1},{9... | collective-permute-start | bytes 380936 | tf_op jit(solution)/shard_map/ppermute | solution.py:24
  8.6 1.9 %collective-permute-start.2 = (f32[88,128]{1,0:T(8,128)}, f32[88,128]{1,0:T(8,128)S(1)}, u32[]{:S(2)}, u32[]{:S(2)}) collective-permute-start(f32[88,128]{1,0:T(8,128)} %get-tuple-element.20.refs_10_), channel_id=1, source_target_pairs={{3,0},{0,1},{1,2},{2,3},{7,4},{4,5},{5,6},{6,7},{11,8},{8,9},{9,10... | collective-permute-start | bytes 135176 | tf_op jit(solution)/shard_map/ppermute | solution.py:24
  10.6 1.0 %collective-permute-start.3 = (f32[88,128]{1,0:T(8,128)}, f32[88,128]{1,0:T(8,128)S(1)}, u32[]{:S(2)}, u32[]{:S(2)}) collective-permute-start(f32[88,128]{1,0:T(8,128)} %get-tuple-element.21.refs_2_.refs_1_.refs_9_), channel_id=1, source_target_pairs={{1,0},{2,1},{3,2},{0,3},{5,4},{6,5},{7,6},{4,7},{9,8},{10,9},{11,1... | collective-permute-start | bytes 135176 | tf_op jit(solution)/shard_map/ppermute | solution.py:24
  11.6 0.8 %copy-done.9 = f32[88,128]{1,0:T(8,128)S(1)} copy-done((f32[88,128]{1,0:T(8,128)S(1)}, f32[88,128]{1,0:T(8,128)}, u32[]{:S(2)}) %copy-start.9) | copy-done | bytes 45080
  14.0 1.0 %collective-permute-done.3.refs_4_.refs_3_.refs_5_ = f32[88,128]{1,0:T(8,128)S(1)} collective-permute-done((f32[88,128]{1,0:T(8,128)}, f32[88,128]{1,0:T(8,128)S(1)}, u32[]{:S(2)}, u32[]{:S(2)}) %collective-permute-start.3) | collective-permute-done | bytes 45088 | tf_op jit(solution)/shard_map/ppermute | solution.py:24
  15.0 1.2 %pieces.1 = f32[384,128]{1,0:T(8,128)S(1)} custom-call(f32[160,128]{1,0:T(8,128)S(1)} %inner.1.refs_0_, f32[248,128]{1,0:T(8,128)S(1)} %collective-permute-done.refs_1_.refs_2_, f32[248,128]{1,0:T(8,128)S(1)} %collective-permute-done.1.refs_2_.refs_3_, f32[88,128]{1,0:T(8,128)S(1)} %collective-permute-done.2.refs_3_.refs_2_.refs_4_, ...), custom_call_target="tpu_custom_call" | custom-call | bytes 1000000 | tf_op jit(solution)/shard_map/pieces/pallas_call | solution.py:646
  16.3 13.9 %all_to_all.20 = f32[16,24,128]{2,1,0:T(8,128)S(1)} all-to-all(f32[16,24,128]{2,1,0:T(8,128)S(1)} %bitcast.22), channel_id=1, replica_groups=mesh['comp'=2,'gx'=4,'gy'=4] {'gx','gy'}, dimensions={0} | all-to-all | bytes 393216 | tf_op jit(solution)/shard_map/all_to_all | solution.py:731
  30.1 1.8 %fluxes.1 = (f32[256,128]{1,0:T(8,128)}, f32[32,128]{1,0:T(8,128)S(1)}, f32[32,128]{1,0:T(8,128)S(1)}) custom-call(f32[384,128]{1,0:T(8,128)S(1)} %bitcast.21, f32[16,128,128]{2,1,0:T(8,128)S(1)} %copy-done.1, s32[4,16]{1,0:T(4,128)S(1)} %pad_add_fusion.refs_6_.refs_2_), custom_call_target="tpu_custom_call" | custom-call | bytes 1000000 | tf_op jit(solution)/shard_map/fluxes/pallas_call | solution.py:646
  32.0 2.7 %all-to-all-start.1 = ((f32[32,8,128]{2,1,0:T(8,128)}), f32[32,8,128]{2,1,0:T(8,128)S(1)}, u32[]{:S(2)}, u32[]{:S(2)}) async-start(f32[32,8,128]{2,1,0:T(8,128)} %bitcast.8), calls=%async_computation.1 | async-start | bytes 262144 | tf_op jit(solution)/shard_map/all_to_all | solution.py:749
  34.8 1.7 %collective-permute-start.4 = (f32[216,128]{1,0:T(8,128)S(1)}, f32[216,128]{1,0:T(8,128)S(1)}, u32[]{:S(2)}, u32[]{:S(2)}) collective-permute-start(f32[216,128]{1,0:T(8,128)S(1)} %get-tuple-element.25), channel_id=1, source_target_pairs={{28,0},{0,4},{4,8},{8,12},{12,16},{16,20},{20,24},{24,28},{29,1},{... | collective-permute-start | bytes 331784 | tf_op jit(solution)/shard_map/ppermute | solution.py:24
  36.5 1.9 %collective-permute-start.5 = (f32[216,128]{1,0:T(8,128)S(1)}, f32[216,128]{1,0:T(8,128)S(1)}, u32[]{:S(2)}, u32[]{:S(2)}) collective-permute-start(f32[216,128]{1,0:T(8,128)S(1)} %get-tuple-element.26), channel_id=1, source_target_pairs={{4,0},{8,4},{12,8},{16,12},{20,16},{24,20},{28,24},{0,28},{5,1},{9... | collective-permute-start | bytes 331784 | tf_op jit(solution)/shard_map/ppermute | solution.py:24
  38.6 4.3 %sea_base.1 = f32[2048,128]{1,0:T(8,128)} custom-call(f32[2048,128]{1,0:T(8,128)} %bitcast.29, s32[64,128]{1,0:T(8,128)} %refs_1_.8, f32[248,128]{1,0:T(8,128)} %copy-done.3, f32[248,128]{1,0:T(8,128)} %copy-done.4, f32[88,128]{1,0:T(8,128)} %copy-done.5, f32[88,128]{1,0:T(8,128)} %copy-done.6, f32[4]{0:T(128)} %refs_6_.1, ...), custom_call_target="tpu_custom_call" | custom-call | bytes 1000000000 | tf_op jit(solution)/shard_map/sea_base/pallas_call | solution.py:646
  43.5 1.3 %collective-permute-done.5.refs_7_.refs_6_ = f32[216,128]{1,0:T(8,128)S(1)} collective-permute-done((f32[216,128]{1,0:T(8,128)S(1)}, f32[216,128]{1,0:T(8,128)S(1)}, u32[]{:S(2)}, u32[]{:S(2)}) %collective-permute-start.5) | collective-permute-done | bytes 110624 | tf_op jit(solution)/shard_map/ppermute | solution.py:24
  44.9 2.2 %sea_top.1 = (f32[4,8,64,128]{3,2,1,0:T(8,128)}, f32[128,128]{1,0:T(8,128)}) custom-call(f32[256,128]{1,0:T(8,128)S(1)} %bitcast.23, s32[64,128]{1,0:T(8,128)S(1)} %copy-done.10, f32[32,128]{1,0:T(8,128)S(1)} %get-tuple-element.27.refs_2_, f32[32,128]{1,0:T(8,128)S(1)} %collective-permute-done.6.refs_3_, ...), custom_call_target="tpu_custom_call", output_to_operand_aliasing={{0}: (5, {})} | custom-call | bytes 1000000 | tf_op jit(solution)/shard_map/sea_top/pallas_call | solution.py:646
  47.1 5.2 %all-to-all-start.2 = ((f32[16,8,128]{2,1,0:T(8,128)}), f32[16,8,128]{2,1,0:T(8,128)S(1)}, u32[]{:S(2)}, u32[]{:S(2)}) async-start(f32[16,8,128]{2,1,0:T(8,128)} %bitcast.12), calls=%async_computation.2 | async-start | bytes 131072 | tf_op jit(solution)/shard_map/all_to_all | solution.py:796
  52.3 5.6 %steps_a.1.refs_12_ = f32[3200,128]{1,0:T(8,128)} custom-call(f32[3200,128]{1,0:T(8,128)} %bitcast.19, f32[248,128]{1,0:T(8,128)} %copy-done.3, f32[248,128]{1,0:T(8,128)} %copy-done.4, f32[88,128]{1,0:T(8,128)} %copy-done.5, f32[88,128]{1,0:T(8,128)} %copy-done.6, f32[216,128]{1,0:T(8,128)} %copy-done.7, f32[216,128]{1,0:T(8,128)} %copy-done.8, ...), custom_call_target="tpu_custom_call" | custom-call | bytes 1000000000 | tf_op jit(solution)/shard_map/steps_a/pallas_call | solution.py:646
  57.9 1.9 %all-to-all-done.2 = f32[16,8,128]{2,1,0:T(8,128)S(1)} async-done(((f32[16,8,128]{2,1,0:T(8,128)}), f32[16,8,128]{2,1,0:T(8,128)S(1)}, u32[]{:S(2)}, u32[]{:S(2)}) %all-to-all-start.2) | async-done | bytes 65568 | tf_op jit(solution)/shard_map/all_to_all | solution.py:796
  59.8 2.0 %replies.1.refs_13_.refs_1_ = f32[128,128]{1,0:T(8,128)} custom-call(f32[128,128]{1,0:T(8,128)S(1)} %bitcast.25, f32[16,128,128]{2,1,0:T(8,128)S(1)} %copy-done.1, s32[4,16]{1,0:T(4,128)S(1)} %pad_add_fusion.refs_6_.refs_2_, f32[32,128]{1,0:T(8,128)S(1)} %get-tuple-element.31.refs_3_), custom_call_target="tpu_custom_call" | custom-call | bytes 1000000 | tf_op jit(solution)/shard_map/replies/pallas_call | solution.py:646
  61.8 5.0 %all-to-all-start.3 = ((f32[16,8,128]{2,1,0:T(8,128)}), f32[16,8,128]{2,1,0:T(8,128)S(1)}, u32[]{:S(2)}, u32[]{:S(2)}) async-start(f32[16,8,128]{2,1,0:T(8,128)} %bitcast.15), calls=%async_computation.3 | async-start | bytes 131072 | tf_op jit(solution)/shard_map/all_to_all | solution.py:833
  67.2 5.6 %steps_b.1 = f32[3200,128]{1,0:T(8,128)} custom-call(f32[3200,128]{1,0:T(8,128)} %bitcast.20, f32[248,128]{1,0:T(8,128)} %copy-done.3, f32[248,128]{1,0:T(8,128)} %copy-done.4, f32[88,128]{1,0:T(8,128)} %copy-done.5, f32[88,128]{1,0:T(8,128)} %copy-done.6, f32[216,128]{1,0:T(8,128)} %copy-done.7, ...), custom_call_target="tpu_custom_call", output_to_operand_aliasing={{}: (12, {})} | custom-call | bytes 1000000000 | tf_op jit(solution)/shard_map/steps_b/pallas_call | solution.py:646
  72.8 1.6 %all-to-all-done.3 = f32[16,8,128]{2,1,0:T(8,128)S(1)} async-done(((f32[16,8,128]{2,1,0:T(8,128)}), f32[16,8,128]{2,1,0:T(8,128)S(1)}, u32[]{:S(2)}, u32[]{:S(2)}) %all-to-all-start.3) | async-done | bytes 65568 | tf_op jit(solution)/shard_map/all_to_all | solution.py:833
  74.4 1.6 %surface.1 = f32[64,128]{1,0:T(8,128)} custom-call(f32[128,128]{1,0:T(8,128)S(1)} %bitcast.24, bf16[16,256,128]{2,1,0:T(8,128)(2,1)S(1)} %surface_weights.1.refs_1_, s32[4,16]{1,0:T(4,128)S(1)} %pad_add_fusion.refs_6_.refs_2_), custom_call_target="tpu_custom_call" | custom-call | bytes 1000000 | tf_op jit(solution)/shard_map/surface/pallas_call | solution.py:646
  (47 shorter events, 2.7 us)
Async XLA Ops:
  0.6 11.0 %copy-start = (f32[10,20,16,128]{3,2,1,0:T(8,128)S(1)}, f32[10,20,16,128]{3,2,1,0:T(8,128)}, u32[]{:S(2)}) copy-start(f32[10,20,16,128]{3,2,1,0:T(8,128)} %refs_0_.3) | copy-start | bytes 4915204
  0.6 10.9 %copy-start.14 = (s32[16]{0:T(128)S(1)}, s32[16]{0:T(128)}, u32[]{:S(2)}) copy-start(s32[16]{0:T(128)} %param.18) | copy-start | bytes 196
  0.7 10.9 %copy-start.15 = (s32[16,1]{0,1:T(1,128)S(1)}, s32[16,1]{0,1:T(1,128)}, u32[]{:S(2)}) copy-start(s32[16,1]{0,1:T(1,128)} %param.17) | copy-start | bytes 196
  0.7 10.9 %copy-start.16 = (s32[16]{0:T(128)S(1)}, s32[16]{0:T(128)}, u32[]{:S(2)}) copy-start(s32[16]{0:T(128)} %param.15) | copy-start | bytes 196
  0.7 10.9 %copy-start.13 = (f32[10]{0:T(128)S(1)}, f32[10]{0:T(128)}, u32[]{:S(2)}) copy-start(f32[10]{0:T(128)} %refs_11_.3) | copy-start | bytes 124
  0.7 12.4 %copy-start.2 = (f32[16,128,128]{2,1,0:T(8,128)S(1)}, f32[16,128,128]{2,1,0:T(8,128)}, u32[]{:S(2)}) copy-start(f32[16,128,128]{2,1,0:T(8,128)} %refs_0_.5) | copy-start | bytes 3145732
  4.0 11.0 %collective-permute-start = (f32[248,128]{1,0:T(8,128)}, f32[248,128]{1,0:T(8,128)S(1)}, u32[]{:S(2)}, u32[]{:S(2)}) collective-permute-start(f32[248,128]{1,0:T(8,128)} %get-tuple-element.18.refs_8_), channel_id=1, source_target_pairs={{28,0},{0,4},{4,8},{8,12},{12,16},{16,20},{20,24},{24,28},{29,1},{... | collective-permute-start | bytes 380936 | tf_op jit(solution)/shard_map/ppermute | solution.py:24
  7.1 7.9 %collective-permute-start.1 = (f32[248,128]{1,0:T(8,128)}, f32[248,128]{1,0:T(8,128)S(1)}, u32[]{:S(2)}, u32[]{:S(2)}) collective-permute-start(f32[248,128]{1,0:T(8,128)} %get-tuple-element.19.refs_7_), channel_id=1, source_target_pairs={{4,0},{8,4},{12,8},{16,12},{20,16},{24,20},{28,24},{0,28},{5,1},{9... | collective-permute-start | bytes 380936 | tf_op jit(solution)/shard_map/ppermute | solution.py:24
  8.6 5.3 %collective-permute-start.2 = (f32[88,128]{1,0:T(8,128)}, f32[88,128]{1,0:T(8,128)S(1)}, u32[]{:S(2)}, u32[]{:S(2)}) collective-permute-start(f32[88,128]{1,0:T(8,128)} %get-tuple-element.20.refs_10_), channel_id=1, source_target_pairs={{3,0},{0,1},{1,2},{2,3},{7,4},{4,5},{5,6},{6,7},{11,8},{8,9},{9,10... | collective-permute-start | bytes 135176 | tf_op jit(solution)/shard_map/ppermute | solution.py:24
  10.6 4.4 %collective-permute-start.3 = (f32[88,128]{1,0:T(8,128)}, f32[88,128]{1,0:T(8,128)S(1)}, u32[]{:S(2)}, u32[]{:S(2)}) collective-permute-start(f32[88,128]{1,0:T(8,128)} %get-tuple-element.21.refs_2_.refs_1_.refs_9_), channel_id=1, source_target_pairs={{1,0},{2,1},{3,2},{0,3},{5,4},{6,5},{7,6},{4,7},{9,8},{10,9},{11,1... | collective-permute-start | bytes 135176 | tf_op jit(solution)/shard_map/ppermute | solution.py:24
  13.1 17.0 %copy-start.1 = (f32[16,128,128]{2,1,0:T(8,128)S(1)}, f32[16,128,128]{2,1,0:T(8,128)}, u32[]{:S(2)}) copy-start(f32[16,128,128]{2,1,0:T(8,128)} %refs_1_.9) | copy-start | bytes 3145732
  13.3 21.5 %copy-start.11 = (f32[216,128]{1,0:T(8,128)S(1)}, f32[216,128]{1,0:T(8,128)}, u32[]{:S(2)}) copy-start(f32[216,128]{1,0:T(8,128)} %get-tuple-element.22.refs_0_) | copy-start | bytes 331780
  13.3 21.5 %copy-start.12 = (f32[216,128]{1,0:T(8,128)S(1)}, f32[216,128]{1,0:T(8,128)}, u32[]{:S(2)}) copy-start(f32[216,128]{1,0:T(8,128)} %get-tuple-element.23.refs_1_) | copy-start | bytes 331780
  14.0 20.7 %copy-start.5 = (f32[88,128]{1,0:T(8,128)}, f32[88,128]{1,0:T(8,128)S(1)}, u32[]{:S(2)}) copy-start(f32[88,128]{1,0:T(8,128)S(1)} %collective-permute-done.2.refs_3_.refs_2_.refs_4_) | copy-start | bytes 135172
  15.0 19.7 %copy-start.6 = (f32[88,128]{1,0:T(8,128)}, f32[88,128]{1,0:T(8,128)S(1)}, u32[]{:S(2)}) copy-start(f32[88,128]{1,0:T(8,128)S(1)} %collective-permute-done.3.refs_4_.refs_3_.refs_5_) | copy-start | bytes 135172
  15.0 17.0 %copy-start.3 = (f32[248,128]{1,0:T(8,128)}, f32[248,128]{1,0:T(8,128)S(1)}, u32[]{:S(2)}) copy-start(f32[248,128]{1,0:T(8,128)S(1)} %collective-permute-done.refs_1_.refs_2_) | copy-start | bytes 380932
  15.0 17.0 %copy-start.4 = (f32[248,128]{1,0:T(8,128)}, f32[248,128]{1,0:T(8,128)S(1)}, u32[]{:S(2)}) copy-start(f32[248,128]{1,0:T(8,128)S(1)} %collective-permute-done.1.refs_2_.refs_3_) | copy-start | bytes 380932
  32.0 12.9 %copy-start.10 = (s32[64,128]{1,0:T(8,128)S(1)}, s32[64,128]{1,0:T(8,128)}, u32[]{:S(2)}) copy-start(s32[64,128]{1,0:T(8,128)} %refs_1_.8) | copy-start | bytes 98308
  32.0 12.9 %all-to-all-start.1 = ((f32[32,8,128]{2,1,0:T(8,128)}), f32[32,8,128]{2,1,0:T(8,128)S(1)}, u32[]{:S(2)}, u32[]{:S(2)}) async-start(f32[32,8,128]{2,1,0:T(8,128)} %bitcast.8), calls=%async_computation.1 | async-start | bytes 262144 | tf_op jit(solution)/shard_map/all_to_all | solution.py:749
  34.8 8.8 %collective-permute-start.4 = (f32[216,128]{1,0:T(8,128)S(1)}, f32[216,128]{1,0:T(8,128)S(1)}, u32[]{:S(2)}, u32[]{:S(2)}) collective-permute-start(f32[216,128]{1,0:T(8,128)S(1)} %get-tuple-element.25), channel_id=1, source_target_pairs={{28,0},{0,4},{4,8},{8,12},{12,16},{16,20},{20,24},{24,28},{29,1},{... | collective-permute-start | bytes 331784 | tf_op jit(solution)/shard_map/ppermute | solution.py:24
  36.5 8.3 %collective-permute-start.5 = (f32[216,128]{1,0:T(8,128)S(1)}, f32[216,128]{1,0:T(8,128)S(1)}, u32[]{:S(2)}, u32[]{:S(2)}) collective-permute-start(f32[216,128]{1,0:T(8,128)S(1)} %get-tuple-element.26), channel_id=1, source_target_pairs={{4,0},{8,4},{12,8},{16,12},{20,16},{24,20},{28,24},{0,28},{5,1},{9... | collective-permute-start | bytes 331784 | tf_op jit(solution)/shard_map/ppermute | solution.py:24
  38.4 4.6 %collective-permute-start.6 = (f32[32,128]{1,0:T(8,128)S(1)}, f32[32,128]{1,0:T(8,128)S(1)}, u32[]{:S(2)}, u32[]{:S(2)}) collective-permute-start(f32[32,128]{1,0:T(8,128)S(1)} %get-tuple-element.27.refs_2_), channel_id=1, source_target_pairs={{16,0},{0,16},{17,1},{1,17},{18,2},{2,18},{19,3},{3,19},{20,4},{4,... | collective-permute-start | bytes 49160 | tf_op jit(solution)/shard_map/ppermute | solution.py:24
  47.1 12.7 %all-to-all-start.2 = ((f32[16,8,128]{2,1,0:T(8,128)}), f32[16,8,128]{2,1,0:T(8,128)S(1)}, u32[]{:S(2)}, u32[]{:S(2)}) async-start(f32[16,8,128]{2,1,0:T(8,128)} %bitcast.12), calls=%async_computation.2 | async-start | bytes 131072 | tf_op jit(solution)/shard_map/all_to_all | solution.py:796
  61.8 12.5 %all-to-all-start.3 = ((f32[16,8,128]{2,1,0:T(8,128)}), f32[16,8,128]{2,1,0:T(8,128)S(1)}, u32[]{:S(2)}, u32[]{:S(2)}) async-start(f32[16,8,128]{2,1,0:T(8,128)} %bitcast.15), calls=%async_computation.3 | async-start | bytes 131072 | tf_op jit(solution)/shard_map/all_to_all | solution.py:833
  (4 other events, 27.9 us)

commit v2 on v1

--- a/solution.py
+++ b/solution.py
@@ -15,7 +15,9 @@
 CAPACITY = 2
 PIECE_ROWS = 12
 VMEM_LIMIT = 8 * 1024 * 1024
-STREAM_LIMIT = 60 * 1024 * 1024
+EDGES_LIMIT = 60 * 1024 * 1024
+SEA_LIMIT = 53 * 1024 * 1024
+STEPS_LIMIT = 53 * 1024 * 1024
 
 
 def shifted(block, axis, distance):
@@ -359,6 +361,7 @@
     east,
     mixing,
     out_far,
+    tops,
     ocean,
     out,
     wests,
@@ -414,7 +417,10 @@
             for side in range(1, 4):
                 total = total + wet_sides[side] * (sides[side] - cells)
             tendency = number * total + 0.1 * (upper + lower - 2.0 * cells)
-            out[pl.ds(start, rows), :] = cells + wet_cells * tendency
+            after = cells + wet_cells * tendency
+            out[pl.ds(start, rows), :] = after
+            if first_level:
+                tops[pl.ds(pl.multiple_of(field * rows, rows), rows), :] = after
         chunk(out, out_far, field, field_rows, departures.at[field]).start()
         return carry
 
@@ -423,26 +429,36 @@
         chunk(out, out_far, field, field_rows, departures.at[field]).wait()
 
 
-def ranks_of(index, row, count, tally):
+def routes_kernel(index, own, *rest):
+    *outs, section, tally = rest
+    lanes = lax.broadcasted_iota(jnp.int32, (1, section.shape[1]), 1)
+    section[...] = jnp.full(section.shape, own[0].astype(F32))
+
     def clear(at, carry):
         tally[at] = 0
         return carry
 
-    lax.fori_loop(0, tally.shape[0], clear, 0)
-    places = []
-    for entry in range(count):
-        owner = index[row, entry]
-        rank = tally[owner]
-        tally[owner] = rank + 1
-        places.append((owner, rank))
-    return places
-
-
-def inner_kernel(at, state_far, diffusion, out, top, arrival):
+    for row, (slots, labels, tiles) in ((0, outs[:3]), (2, outs[3:])):
+        slots[...] = jnp.zeros(slots.shape, F32)
+        labels[...] = jnp.full(labels.shape, -1.0, F32)
+        lax.fori_loop(0, tally.shape[0], clear, 0)
+        for tile in range(index.shape[1]):
+            owner = index[row, tile]
+            rank = tally[owner]
+            tally[owner] = rank + 1
+            slot = pl.ds(owner * CAPACITY + rank, 1)
+            slots[slot, :] = (lanes == tile).astype(F32)
+            labels[slot, :] = jnp.full(lanes.shape, index[row + 1, tile].astype(F32))
+        tiles[...] = jnp.transpose(slots[...])[: tiles.shape[0], :]
+
+
+def inner_kernel(at, state_far, diffusion, out, numbers, top, arrival):
     fields, rows, width = at.fields, at.rows, at.width
     copy = pltpu.make_async_copy(state_far.at[:, pl.ds(at.levels - 2, 2)], top, arrival)
     copy.start()
     lines, lanes = grid_index((rows, width))
+    for field in range(fields):
+        numbers[pl.ds(field, 1), :] = jnp.full((1, width), diffusion[field])
     copy.wait()
     for field in range(fields):
         cells = top[field, 1]
@@ -458,9 +474,11 @@
 
 
 def pieces_kernel(
-    at, targets, inner, north, south, west, east, weights, index, diffusion, out, surface, tally
+    at, inner, north, south, west, east, weights, numbers, routes, labels, sea_labels, out, *scratch
 ):
+    surface, products = scratch
     fields, levels, rows, width = at.fields, at.levels, at.rows, at.width
+    slots = routes.shape[0]
     lines, lanes = grid_index((rows, width))
     for field in range(fields):
         part = field // at.half
@@ -474,34 +492,30 @@
             + jnp.where(lanes == width - 1, pltpu.roll(east[held, :], width - 1 - lane, 1), 0.0)
         )
         here = pl.ds(field * rows, rows)
-        surface[here, :] = inner[here, :] + diffusion[field] * outside
+        surface[here, :] = inner[here, :] + numbers[pl.ds(field, 1), :] * outside
     surface[pl.ds(fields * rows, (16 - fields) * rows), :] = jnp.zeros(
         ((16 - fields) * rows, width), F32
     )
-    out[...] = jnp.zeros(out.shape, F32)
-    slots = targets * CAPACITY
-    for row in (fields, fields + 1):
-        out[pl.ds(row, slots, stride=PIECE_ROWS), :] = jnp.full((slots, width), -1.0, F32)
-    places = ranks_of(index, 2, rows, tally)
     for tile in range(rows):
-        owner, rank = places[tile]
-        start = (owner * CAPACITY + rank) * PIECE_ROWS
-        label = jnp.full((1, width), index[3, tile].astype(F32))
-        out[pl.ds(start + fields + 1, 1), :] = label
-    places = ranks_of(index, 0, rows, tally)
-    for tile in range(rows):
-        owner, rank = places[tile]
-        start = (owner * CAPACITY + rank) * PIECE_ROWS
-        piece = remapped(surface[pl.ds(tile, 16, stride=rows), :], weights[tile])[:fields, :]
-        label = jnp.full((1, width), index[1, tile].astype(F32))
-        out[pl.ds(start, fields), :] = piece
-        out[pl.ds(start + fields, 1), :] = label
-
-
-def flux_kernel(sizes, arrived, remap, index, out, gather, sea_labels, fluxes, tally):
-    fields, flux_count, rows, targets, sections = sizes
+        products[pl.ds(tile * 16, 16), :] = remapped(
+            surface[pl.ds(tile, 16, stride=rows), :], weights[tile]
+        )
+    sent = picked(
+        routes[...][:, :rows],
+        jnp.concatenate(
+            [products[pl.ds(field, rows, stride=16), :] for field in range(fields)], axis=1
+        ),
+    )
+    for field in range(fields):
+        out[pl.ds(field, slots, stride=PIECE_ROWS), :] = sent[:, field * width : (field + 1) * width]
+    out[pl.ds(fields, slots, stride=PIECE_ROWS), :] = labels[...]
+    out[pl.ds(fields + 1, slots, stride=PIECE_ROWS), :] = sea_labels[...]
+
+
+def flux_kernel(sizes, arrived, remap, routes, out, gather, sea_labels, fluxes, products):
+    fields, flux_count, rows, sections = sizes
     width = out.shape[1]
-    slots = targets * CAPACITY
+    slots = routes.shape[0]
     select = one_hot(arrived[pl.ds(fields, slots, stride=PIECE_ROWS), :])
     gather[...] = select
     sea_labels[...] = arrived[pl.ds(fields + 1, slots, stride=PIECE_ROWS), :]
@@ -515,47 +529,33 @@
     fluxes[pl.ds(rows, rows), :] = speed * a[1] + a[5] + a[8]
     fluxes[pl.ds(2 * rows, rows), :] = speed * a[2] * (1.0 + 0.2 * jnp.tanh(a[9]))
     fluxes[pl.ds(3 * rows, rows), :] = speed * a[3]
-    out[...] = jnp.zeros(out.shape, F32)
-    places = ranks_of(index, 2, rows, tally)
     for tile in range(rows):
-        owner, rank = places[tile]
-        mapped = remapped(fluxes[pl.ds(tile, flux_count, stride=rows), :], both_halves(remap[tile]))
+        products[pl.ds(tile * flux_count, flux_count), :] = remapped(
+            fluxes[pl.ds(tile, flux_count, stride=rows), :], both_halves(remap[tile])
+        )
+    sent = picked(
+        routes[...][:, :rows],
+        jnp.concatenate(
+            [products[pl.ds(flux, rows, stride=flux_count), :] for flux in range(flux_count)],
+            axis=1,
+        ),
+    )
+    for flux in range(flux_count):
         for section in range(sections):
-            start = ((section * targets + owner) * CAPACITY + rank) * flux_count
-            out[pl.ds(start, flux_count), :] = mapped
+            out[pl.ds(section * slots * flux_count + flux, slots, stride=flux_count), :] = sent[
+                :, flux * width : (flux + 1) * width
+            ]
 
 
 def sea_kernel(
-    sizes,
-    landed,
-    wet,
-    own_labels,
-    other_labels,
-    own,
-    base,
-    out,
-    answers,
-    tops,
-    before,
-    wet_here,
-    arrivals,
-    departures,
+    sizes, landed, base_tops, wet, own_labels, other_labels, section, base, out, answers, tops, leave
 ):
-    flux_count, sea_rows, targets = sizes
-    fetched = [
-        pltpu.make_async_copy(
-            out.at[flux, 0], before.at[pl.ds(flux * sea_rows, sea_rows)], arrivals.at[flux]
-        )
-        for flux in range(flux_count)
-    ]
-    fetched.append(pltpu.make_async_copy(wet, wet_here, arrivals.at[flux_count]))
-    for copy in fetched:
-        copy.start()
+    flux_count, sea_rows = sizes
     width = landed.shape[1]
-    slots = targets * CAPACITY
+    slots = own_labels.shape[0]
     mine = one_hot(own_labels[...])
     others = one_hot(other_labels[...])
-    is_first = own[0] == 0
+    is_first = section[0:1, :] == 0.0
     select = jnp.concatenate(
         [jnp.where(is_first, mine, others), jnp.where(is_first, others, mine)], axis=0
     )
@@ -563,18 +563,14 @@
         [landed[pl.ds(flux, 2 * slots, stride=flux_count), :] for flux in range(flux_count)], axis=1
     )
     forcing = picked(jnp.transpose(select)[:sea_rows, :], values)
-    for copy in fetched:
-        copy.wait()
-    wet_cells = wet_here[...].astype(F32)
+    wet_cells = wet[...].astype(F32)
     copies = []
     for flux in range(flux_count):
         held = pl.ds(flux * sea_rows, sea_rows)
-        tops[held, :] = before[held, :] + wet_cells * (
+        tops[held, :] = base_tops[held, :] + wet_cells * (
             FORCING_SCALE[flux] * forcing[:, flux * width : (flux + 1) * width]
         )
-        copies.append(
-            pltpu.make_async_copy(tops.at[held], out.at[flux, 0], departures.at[flux])
-        )
+        copies.append(pltpu.make_async_copy(tops.at[held], out.at[flux, 0], leave.at[flux]))
         copies[flux].start()
     all_tops = jnp.concatenate(
         [tops[pl.ds(flux * sea_rows, sea_rows), :] for flux in range(flux_count)], axis=1
@@ -588,16 +584,30 @@
         copy.wait()
 
 
-def reply_kernel(sizes, answered, remap, index, gather, out, on_exchange, tally):
-    flux_count, rows, targets = sizes
+def tops_of_tiles(returned, tiles, flux_count, scratch):
+    rows, slots = tiles.shape
+    width = returned.shape[1]
+    found = picked(
+        tiles[...],
+        jnp.concatenate(
+            [returned[pl.ds(flux, slots, stride=flux_count), :] for flux in range(flux_count)],
+            axis=1,
+        ),
+    )
+    for flux in range(flux_count):
+        scratch[pl.ds(flux, rows, stride=flux_count), :] = found[
+            :, flux * width : (flux + 1) * width
+        ]
+
+
+def reply_kernel(flux_count, answered, remap, tiles, gather, out, tops, on_exchange):
+    rows, slots = tiles.shape
     width = out.shape[1]
-    slots = targets * CAPACITY
-    places = ranks_of(index, 2, rows, tally)
+    tops_of_tiles(answered, tiles, flux_count, tops)
     for tile in range(rows):
-        owner, rank = places[tile]
-        start = (owner * CAPACITY + rank) * flux_count
-        on_exchange[pl.ds(tile * flux_count, flux_count), :] = remapped(
-            answered[pl.ds(start, flux_count), :], both_halves(jnp.transpose(remap[tile]))
+        held = pl.ds(tile * flux_count, flux_count)
+        on_exchange[held, :] = remapped(
+            tops[held, :], both_halves(jnp.transpose(remap[tile]))
         )
     values = jnp.concatenate(
         [on_exchange[pl.ds(flux, rows, stride=flux_count), :] for flux in range(flux_count)], axis=1
@@ -609,14 +619,12 @@
         ]
 
 
-def surface_kernel(sizes, returned, weights, index, out, tally):
-    flux_count, rows, targets = sizes
-    places = ranks_of(index, 0, rows, tally)
+def surface_kernel(flux_count, returned, weights, tiles, out, tops):
+    rows, _ = tiles.shape
+    tops_of_tiles(returned, tiles, flux_count, tops)
     for tile in range(rows):
-        owner, rank = places[tile]
-        start = (owner * CAPACITY + rank) * flux_count
         out[pl.ds(tile, flux_count, stride=rows), :] = remapped(
-            returned[pl.ds(start, flux_count), :], weights[tile]
+            tops[pl.ds(tile * flux_count, flux_count), :], weights[tile]
         )
 
 
@@ -644,6 +652,10 @@
         **more,
     )
     return lambda *arguments: run(*arguments, *after)
+
+
+def gated(values, before):
+    return lax.optimization_barrier((values, before))[0]
 
 
 def on_device(
@@ -669,7 +681,6 @@
     at = Edges(fields, levels, rows, sea_blocks, sea_rows, width)
     slots = targets * CAPACITY
     ring = ("comp", "gx")
-    tally = pltpu.SMEM((targets,), jnp.int32)
 
     index = jnp.stack([exchange_owner[:, 0], exchange_slot, ocean_owner[:, 0], ocean_slot])
     section = lax.axis_index("comp").astype(jnp.int32).reshape(1)
@@ -688,7 +699,7 @@
         + (array(at.col_rows, width),) * 2,
         [ANY] * 3,
         [state_copy, ocean_copy, wet_copy, pltpu.SemaphoreType.DMA((fields + 5,))],
-        limit=STREAM_LIMIT,
+        limit=EDGES_LIMIT,
     )(state, ocean, wet_mask)
     north = shifted(near_last, ring, 1)
     south = shifted(near_first, ring, -1)
@@ -701,23 +712,28 @@
             name,
             jax.ShapeDtypeStruct((rows, 2 * width, width), BF16),
             [VMEM],
-            after=(before,),
-        )(remap)
-
-    inner = call(
+        )(gated(remap, before))
+
+    tile_slots, piece_labels, slot_tiles, sea_slots, sea_labels, sea_tiles, here = call(
+        routes_kernel,
+        "routes",
+        ((array(slots, width),) * 2 + (array(rows, slots),)) * 2 + (array(8, width),),
+        [SMEM, SMEM],
+        [pltpu.SMEM((targets,), jnp.int32)],
+    )(gated(index, first_cols), section)
+    inner, numbers = call(
         functools.partial(inner_kernel, at),
         "inner",
-        array(fields * rows, width),
+        (array(fields * rows, width), array(-(-fields // 8) * 8, width)),
         [ANY, SMEM],
         [pltpu.VMEM((fields, 2, rows, width), F32), pltpu.SemaphoreType.DMA],
-        after=(first_cols,),
-    )(atmos_state, atmos_diffusion)
+    )(gated(atmos_state, first_cols), atmos_diffusion)
     pieces = call(
-        functools.partial(pieces_kernel, at, targets),
+        functools.partial(pieces_kernel, at),
         "pieces",
         array(slots * PIECE_ROWS, width),
-        [VMEM] * 6 + [SMEM] * 2,
-        [pltpu.VMEM((16 * rows, width), F32), tally],
+        [VMEM] * 10,
+        [pltpu.VMEM((16 * rows, width), F32)] * 2,
     )(
         inner,
         north,
@@ -725,27 +741,25 @@
         west,
         east,
         weights_of(remap_atmos, False, "piece_weights", first_cols),
-        index,
-        atmos_diffusion,
+        numbers,
+        tile_slots,
+        piece_labels,
+        sea_labels,
     )
     arrived = lax.all_to_all(
         pieces.reshape(targets, CAPACITY * PIECE_ROWS, width), SECTION, 0, 0, tiled=True
     )
     outgoing, gather, own_labels = call(
-        functools.partial(flux_kernel, (fields, sea_fields, rows, targets, sections)),
+        functools.partial(flux_kernel, (fields, sea_fields, rows, sections)),
         "fluxes",
         (
-            array(devices * CAPACITY * sea_fields, width),
+            array(sections * slots * sea_fields, width),
             array(slots, width),
             array(slots, width),
         ),
-        [VMEM, VMEM, SMEM],
-        [pltpu.VMEM((sea_fields * rows, width), F32), tally],
-    )(
-        arrived.reshape(slots * PIECE_ROWS, width),
-        remap_ocean,
-        index,
-    )
+        [VMEM] * 3,
+        [pltpu.VMEM((sea_fields * rows, width), F32)] * 2,
+    )(arrived.reshape(slots * PIECE_ROWS, width), remap_ocean, sea_slots)
     landed = lax.all_to_all(
         outgoing.reshape(devices, CAPACITY * sea_fields, width), EVERY, 0, 0, tiled=True
     )
@@ -760,37 +774,37 @@
     far_north = shifted(to_south, ring, 1)
     far_south = shifted(to_north, ring, -1)
 
-    sea_base = call(
+    sea_base, base_tops = call(
         functools.partial(ocean_kernel, at, sea_levels),
         "sea_base",
-        array(sea_blocks * sea_rows, width),
+        (array(sea_blocks * sea_rows, width), array(sea_fields * sea_rows, width)),
         [ANY] + [VMEM] * 5 + [SMEM],
         [ocean_copy] * 2 + [pltpu.VMEM((width, width), F32)] * 2 + [ocean_flags] * 2,
         after=(outgoing,),
-        limit=STREAM_LIMIT,
+        limit=SEA_LIMIT,
         work=1_000_000_000,
-        out_specs=ANY,
+        out_specs=(ANY, VMEM),
     )(ocean, wet_mask, north, south, west, east, ocean_mixing)
 
     ocean_next, answers = call(
-        functools.partial(sea_kernel, (sea_fields, sea_rows, targets)),
+        functools.partial(sea_kernel, (sea_fields, sea_rows)),
         "sea_top",
         (
             array(sea_fields, sea_levels, sea_rows, width),
             array(slots * sea_fields, width),
         ),
-        [VMEM, ANY, VMEM, VMEM, SMEM, ANY],
-        [pltpu.VMEM((sea_fields * sea_rows, width), F32)] * 2
-        + [wet_copy, pltpu.SemaphoreType.DMA((sea_fields + 1,)), ocean_flags],
+        [VMEM] * 6 + [ANY],
+        [pltpu.VMEM((sea_fields * sea_rows, width), F32), ocean_flags],
         after=(far_north, far_south),
         out_specs=(ANY, VMEM),
-        input_output_aliases={5: 0},
+        input_output_aliases={6: 0},
     )(
         landed.reshape(devices * CAPACITY * sea_fields, width),
+        base_tops,
         wet_mask,
         own_labels,
         other_labels,
-        section,
+        here,
         sea_base.reshape(sea_fields, sea_levels, sea_rows, width),
     )
     answered = lax.all_to_all(
@@ -807,7 +821,7 @@
             + [pltpu.VMEM((rows, width), F32)] * 2
             + [pltpu.SemaphoreType.DMA((at.half,))] * 2,
             after=(before,),
-            limit=STREAM_LIMIT,
+            limit=STEPS_LIMIT,
             work=1_000_000_000,
             out_specs=ANY,
             **more,
@@ -819,17 +833,12 @@
     answered, atmos_next = lax.optimization_barrier((answered, atmos_next))
 
     replies = call(
-        functools.partial(reply_kernel, (sea_fields, rows, targets)),
+        functools.partial(reply_kernel, sea_fields),
         "replies",
         array(slots * sea_fields, width),
-        [VMEM, VMEM, SMEM, VMEM],
-        [pltpu.VMEM((sea_fields * rows, width), F32), tally],
-    )(
-        answered.reshape(slots * sea_fields, width),
-        remap_ocean,
-        index,
-        gather,
-    )
+        [VMEM] * 4,
+        [pltpu.VMEM((sea_fields * rows, width), F32)] * 2,
+    )(answered.reshape(slots * sea_fields, width), remap_ocean, sea_tiles, gather)
     returned = lax.all_to_all(
         replies.reshape(targets, CAPACITY * sea_fields, width), SECTION, 0, 0, tiled=True
     )
@@ -837,15 +846,15 @@
         state, *halos, atmos_diffusion, atmos_next
     )
     ocean_surface = call(
-        functools.partial(surface_kernel, (sea_fields, rows, targets)),
+        functools.partial(surface_kernel, sea_fields),
         "surface",
         array(sea_fields * rows, width),
-        [VMEM, VMEM, SMEM],
-        [tally],
+        [VMEM] * 3,
+        [pltpu.VMEM((sea_fields * rows, width), F32)],
     )(
         returned.reshape(slots * sea_fields, width),
         weights_of(remap_atmos, True, "surface_weights", replies),
-        index,
+        slot_tiles,
     )
     return (
         atmos_next.reshape(atmos_state.shape),

time: 76.6 us -> 72.8 us (0.950)
  Pallas kernels: 28.8 us -> 25 us
  waiting for transfers between devices: 7.08 us -> 8.05 us
    pallas_call x13 -> x14, Pallas kernels: 28.8 us -> 25 us  [call(): return lambda *arguments: run(*arguments, *after)]
  transfers between devices with their start and end apart: 10 -> 10, of which waited for: 6 -> 5; matrix products, arithmetic and copies ran while one was open for 0% -> 0% of each run, Pallas kernels for 22% -> 22%
where the time goes in v2:
time: 72.8 us; the launch traced here: 72.3 us
  Pallas kernels  25 us (34%)
  starting transfers between devices  23.7 us (33%)
  blocking collectives  13.9 us (19%)
  waiting for transfers between devices  8.05 us (11%)
  between operations  0.99 us (1%)
    pallas_call x14, Pallas kernels, call(): return lambda *arguments: run(*arguments, *after)  25 us
    all_to_all x1, blocking collectives, on_device(): lax.all_to_all(pieces.reshape(targets, CAPACITY * PIECE_ROWS, width), SEC...  13.9 us
    ppermute x7, starting transfers between devices, shifted(): return lax.ppermute(block, axis, route)  11.5 us
    all_to_all x1, starting transfers between devices, on_device(): lax.all_to_all(answers.reshape(targets, CAPACITY * sea_fields, width), SE...  5.21 us
    all_to_all x1, starting transfers between devices, on_device(): lax.all_to_all(replies.reshape(targets, CAPACITY * sea_fields, width), SE...  4.5 us
    ppermute x7, waiting for transfers between devices, shifted(): return lax.ppermute(block, axis, route)  3.23 us
    all_to_all x1, starting transfers between devices, on_device(): lax.all_to_all(outgoing.reshape(devices, CAPACITY * sea_fields, width), E...  2.58 us
    all_to_all x1, waiting for transfers between devices, on_device(): lax.all_to_all(answers.reshape(targets, CAPACITY * sea_fields, width), SE...  2.57 us
  transfers between devices with their start and end apart: 10, of which 5 were waited for; matrix products, arithmetic and copies ran while one was open for 0% of the time, Pallas kernels for 22%

profile of v2, /device:TPU:0, one launch (start us, length us, event | category | flops | bytes accessed | tf_op | source)
XLA Modules:
  0.0 72.3 jit_solution(1321898879112017276)
XLA Ops:
  0.7 3.2 %edges.1 = (f32[248,128]{1,0:T(8,128)}, f32[248,128]{1,0:T(8,128)}, f32[216,128]{1,0:T(8,128)}, f32[216,128]{1,0:T(8,128)}, f32[88,128]{1,0:T(8,128)}, /*index=5*/f32[88,128]{1,0:T(8,128)}) custom-call(f32[3200,128]{1,0:T(8,128)} %bitcast.18, f32[2048,128]{1,0:T(8,128)} %bitcast.27, s32[64,128]{1,0:T(8,128)} %refs_2_.3), custom_call_target="tpu_custom_call" | custom-call | bytes 1000000 | tf_op jit(solution)/shard_map/edges/pallas_call | solution.py:654
  4.0 3.1 %collective-permute-start = (f32[248,128]{1,0:T(8,128)}, f32[248,128]{1,0:T(8,128)S(1)}, u32[]{:S(2)}, u32[]{:S(2)}) collective-permute-start(f32[248,128]{1,0:T(8,128)} %get-tuple-element.33.refs_8_), channel_id=1, source_target_pairs={{28,0},{0,4},{4,8},{8,12},{12,16},{16,20},{20,24},{24,28},{29,1},{... | collective-permute-start | bytes 380936 | tf_op jit(solution)/shard_map/ppermute | solution.py:26
  7.0 1.5 %collective-permute-start.1 = (f32[248,128]{1,0:T(8,128)}, f32[248,128]{1,0:T(8,128)S(1)}, u32[]{:S(2)}, u32[]{:S(2)}) collective-permute-start(f32[248,128]{1,0:T(8,128)} %get-tuple-element.34.refs_7_), channel_id=1, source_target_pairs={{4,0},{8,4},{12,8},{16,12},{20,16},{24,20},{28,24},{0,28},{5,1},{9... | collective-permute-start | bytes 380936 | tf_op jit(solution)/shard_map/ppermute | solution.py:26
  8.6 1.9 %collective-permute-start.2 = (f32[88,128]{1,0:T(8,128)}, f32[88,128]{1,0:T(8,128)S(1)}, u32[]{:S(2)}, u32[]{:S(2)}) collective-permute-start(f32[88,128]{1,0:T(8,128)} %get-tuple-element.35.refs_10_), channel_id=1, source_target_pairs={{3,0},{0,1},{1,2},{2,3},{7,4},{4,5},{5,6},{6,7},{11,8},{8,9},{9,10... | collective-permute-start | bytes 135176 | tf_op jit(solution)/shard_map/ppermute | solution.py:26
  10.5 1.0 %collective-permute-start.3 = (f32[88,128]{1,0:T(8,128)}, f32[88,128]{1,0:T(8,128)S(1)}, u32[]{:S(2)}, u32[]{:S(2)}) collective-permute-start(f32[88,128]{1,0:T(8,128)} %get-tuple-element.36.refs_9_), channel_id=1, source_target_pairs={{1,0},{2,1},{3,2},{0,3},{5,4},{6,5},{7,6},{4,7},{9,8},{10,9},{11,1... | collective-permute-start | bytes 135176 | tf_op jit(solution)/shard_map/ppermute | solution.py:26
  11.7 1.0 %routes.1 = (f32[32,128]{1,0:T(8,128)S(1)}, f32[32,128]{1,0:T(8,128)S(1)}, f32[16,32]{1,0:T(8,128)S(1)}, f32[32,128]{1,0:T(8,128)S(1)}, f32[32,128]{1,0:T(8,128)...) custom-call(s32[4,16]{1,0:T(4,128)S(1)} %pad_add_fusion.refs_0_, s32[1]{0:T(128)} %bitcast.6.refs_1_), custom_call_target="tpu_custom_call" | custom-call | bytes 1000000 | tf_op jit(solution)/shard_map/routes/pallas_call | solution.py:654
  14.0 1.0 %collective-permute-done.3.refs_4_.refs_3_.refs_5_ = f32[88,128]{1,0:T(8,128)S(1)} collective-permute-done((f32[88,128]{1,0:T(8,128)}, f32[88,128]{1,0:T(8,128)S(1)}, u32[]{:S(2)}, u32[]{:S(2)}) %collective-permute-start.3) | collective-permute-done | bytes 45088 | tf_op jit(solution)/shard_map/ppermute | solution.py:26
  15.6 13.9 %all_to_all.20 = f32[16,24,128]{2,1,0:T(8,128)S(1)} all-to-all(f32[16,24,128]{2,1,0:T(8,128)S(1)} %bitcast.22), channel_id=1, replica_groups=mesh['comp'=2,'gx'=4,'gy'=4] {'gx','gy'}, dimensions={0} | all-to-all | bytes 393216 | tf_op jit(solution)/shard_map/all_to_all | solution.py:749
  29.5 1.4 %fluxes.1 = (f32[256,128]{1,0:T(8,128)}, f32[32,128]{1,0:T(8,128)S(1)}, f32[32,128]{1,0:T(8,128)S(1)}) custom-call(f32[384,128]{1,0:T(8,128)S(1)} %bitcast.21, f32[16,128,128]{2,1,0:T(8,128)S(1)} %copy-done.1, f32[32,128]{1,0:T(8,128)S(1)} %get-tuple-element.47.refs_2_), custom_call_target="tpu_custom_call" | custom-call | bytes 1000000 | tf_op jit(solution)/shard_map/fluxes/pallas_call | solution.py:654
  30.9 2.6 %all-to-all-start.1 = ((f32[32,8,128]{2,1,0:T(8,128)}), f32[32,8,128]{2,1,0:T(8,128)S(1)}, u32[]{:S(2)}, u32[]{:S(2)}) async-start(f32[32,8,128]{2,1,0:T(8,128)} %bitcast.9), calls=%async_computation.1 | async-start | bytes 262144 | tf_op jit(solution)/shard_map/all_to_all | solution.py:763
  33.5 1.7 %collective-permute-start.4 = (f32[216,128]{1,0:T(8,128)S(1)}, f32[216,128]{1,0:T(8,128)S(1)}, u32[]{:S(2)}, u32[]{:S(2)}) collective-permute-start(f32[216,128]{1,0:T(8,128)S(1)} %get-tuple-element.49), channel_id=1, source_target_pairs={{28,0},{0,4},{4,8},{8,12},{12,16},{16,20},{20,24},{24,28},{29,1},{... | collective-permute-start | bytes 331784 | tf_op jit(solution)/shard_map/ppermute | solution.py:26
  35.2 1.9 %collective-permute-start.5 = (f32[216,128]{1,0:T(8,128)S(1)}, f32[216,128]{1,0:T(8,128)S(1)}, u32[]{:S(2)}, u32[]{:S(2)}) collective-permute-start(f32[216,128]{1,0:T(8,128)S(1)} %get-tuple-element.50), channel_id=1, source_target_pairs={{4,0},{8,4},{12,8},{16,12},{20,16},{24,20},{28,24},{0,28},{5,1},{9... | collective-permute-start | bytes 331784 | tf_op jit(solution)/shard_map/ppermute | solution.py:26
  37.4 3.9 %sea_base.1 = (f32[2048,128]{1,0:T(8,128)}, f32[256,128]{1,0:T(8,128)S(1)}) custom-call(f32[2048,128]{1,0:T(8,128)} %bitcast.28, s32[64,128]{1,0:T(8,128)S(1)} %copy-done.6, f32[248,128]{1,0:T(8,128)S(1)} %collective-permute-done.refs_1_.refs_2_, f32[248,128]{1,0:T(8,128)S(1)} %collective-permute-done.1.refs_2_.refs_3_, ...), custom_call_target="tpu_custom_call" | custom-call | bytes 1000000000 | tf_op jit(solution)/shard_map/sea_base/pallas_call | solution.py:654
  41.3 0.9 %collective-permute-done.4.refs_7_.refs_5_ = f32[216,128]{1,0:T(8,128)S(1)} collective-permute-done((f32[216,128]{1,0:T(8,128)S(1)}, f32[216,128]{1,0:T(8,128)S(1)}, u32[]{:S(2)}, u32[]{:S(2)}) %collective-permute-start.4) | collective-permute-done | bytes 110624 | tf_op jit(solution)/shard_map/ppermute | solution.py:26
  42.3 1.3 %collective-permute-done.5.refs_8_.refs_6_ = f32[216,128]{1,0:T(8,128)S(1)} collective-permute-done((f32[216,128]{1,0:T(8,128)S(1)}, f32[216,128]{1,0:T(8,128)S(1)}, u32[]{:S(2)}, u32[]{:S(2)}) %collective-permute-start.5) | collective-permute-done | bytes 110624 | tf_op jit(solution)/shard_map/ppermute | solution.py:26
  43.6 1.6 %sea_top.1 = (f32[4,8,64,128]{3,2,1,0:T(8,128)}, f32[128,128]{1,0:T(8,128)}) custom-call(f32[256,128]{1,0:T(8,128)S(1)} %bitcast.23, f32[256,128]{1,0:T(8,128)S(1)} %get-tuple-element.51.refs_1_, s32[64,128]{1,0:T(8,128)S(1)} %copy-done.6, f32[32,128]{1,0:T(8,128)S(1)} %get-tuple-element.52.refs_3_, ...), custom_call_target="tpu_custom_call", output_to_operand_aliasing={{0}: (6, {})} | custom-call | bytes 1000000 | tf_op jit(solution)/shard_map/sea_top/pallas_call | solution.py:654
  45.2 5.2 %all-to-all-start.2 = ((f32[16,8,128]{2,1,0:T(8,128)}), f32[16,8,128]{2,1,0:T(8,128)S(1)}, u32[]{:S(2)}, u32[]{:S(2)}) async-start(f32[16,8,128]{2,1,0:T(8,128)} %bitcast.12), calls=%async_computation.2 | async-start | bytes 131072 | tf_op jit(solution)/shard_map/all_to_all | solution.py:810
  50.5 4.9 %steps_a.1.refs_12_ = f32[3200,128]{1,0:T(8,128)} custom-call(f32[3200,128]{1,0:T(8,128)} %bitcast.19, f32[248,128]{1,0:T(8,128)S(1)} %collective-permute-done.refs_1_.refs_2_, f32[248,128]{1,0:T(8,128)S(1)} %collective-permute-done.1.refs_2_.refs_3_, f32[88,128]{1,0:T(8,128)S(1)} %collective-permute-done.2.refs_3_.refs_2_.refs_4_, ...), custom_call_target="tpu_custom_call" | custom-call | bytes 1000000000 | tf_op jit(solution)/shard_map/steps_a/pallas_call | solution.py:654
  55.4 2.6 %all-to-all-done.2 = f32[16,8,128]{2,1,0:T(8,128)S(1)} async-done(((f32[16,8,128]{2,1,0:T(8,128)}), f32[16,8,128]{2,1,0:T(8,128)S(1)}, u32[]{:S(2)}, u32[]{:S(2)}) %all-to-all-start.2) | async-done | bytes 65568 | tf_op jit(solution)/shard_map/all_to_all | solution.py:810
  57.9 1.3 %replies.1.refs_13_ = f32[128,128]{1,0:T(8,128)} custom-call(f32[128,128]{1,0:T(8,128)S(1)} %bitcast.25, f32[16,128,128]{2,1,0:T(8,128)S(1)} %copy-done.1, f32[16,32]{1,0:T(8,128)S(1)} %copy-done.15, f32[32,128]{1,0:T(8,128)S(1)} %get-tuple-element.59.refs_3_), custom_call_target="tpu_custom_call" | custom-call | bytes 1000000 | tf_op jit(solution)/shard_map/replies/pallas_call | solution.py:654
  59.2 4.5 %all-to-all-start.3 = ((f32[16,8,128]{2,1,0:T(8,128)}), f32[16,8,128]{2,1,0:T(8,128)S(1)}, u32[]{:S(2)}, u32[]{:S(2)}) async-start(f32[16,8,128]{2,1,0:T(8,128)} %bitcast.15), calls=%async_computation.3 | async-start | bytes 131072 | tf_op jit(solution)/shard_map/all_to_all | solution.py:842
  64.1 4.9 %steps_b.1 = f32[3200,128]{1,0:T(8,128)} custom-call(f32[3200,128]{1,0:T(8,128)} %bitcast.20, f32[248,128]{1,0:T(8,128)S(1)} %collective-permute-done.refs_1_.refs_2_, f32[248,128]{1,0:T(8,128)S(1)} %collective-permute-done.1.refs_2_.refs_3_, f32[88,128]{1,0:T(8,128)S(1)} %collective-permute-done.2.refs_3_.refs_2_.refs_4_, ...), custom_call_target="tpu_custom_call", output_to_operand_aliasing={{}: (12, {})} | custom-call | bytes 1000000000 | tf_op jit(solution)/shard_map/steps_b/pallas_call | solution.py:654
  69.0 2.2 %all-to-all-done.3 = f32[16,8,128]{2,1,0:T(8,128)S(1)} async-done(((f32[16,8,128]{2,1,0:T(8,128)}), f32[16,8,128]{2,1,0:T(8,128)S(1)}, u32[]{:S(2)}, u32[]{:S(2)}) %all-to-all-start.3) | async-done | bytes 65568 | tf_op jit(solution)/shard_map/all_to_all | solution.py:842
  71.3 1.0 %surface.1 = f32[64,128]{1,0:T(8,128)} custom-call(f32[128,128]{1,0:T(8,128)S(1)} %bitcast.24, bf16[16,256,128]{2,1,0:T(8,128)(2,1)S(1)} %surface_weights.1.refs_1_, f32[16,32]{1,0:T(8,128)S(1)} %copy-done.13), custom_call_target="tpu_custom_call" | custom-call | bytes 1000000 | tf_op jit(solution)/shard_map/surface/pallas_call | solution.py:654
  (60 shorter events, 2.8 us)
Async XLA Ops:
  0.6 10.9 %copy-start.20 = (s32[16]{0:T(128)S(1)}, s32[16]{0:T(128)}, u32[]{:S(2)}) copy-start(s32[16]{0:T(128)} %param.18) | copy-start | bytes 196
  0.6 10.9 %copy-start.21 = (s32[16,1]{0,1:T(1,128)S(1)}, s32[16,1]{0,1:T(1,128)}, u32[]{:S(2)}) copy-start(s32[16,1]{0,1:T(1,128)} %param.17) | copy-start | bytes 196
  0.7 10.9 %copy-start.22 = (s32[16]{0:T(128)S(1)}, s32[16]{0:T(128)}, u32[]{:S(2)}) copy-start(s32[16]{0:T(128)} %param.15) | copy-start | bytes 196
  0.7 10.9 %copy-start.2 = (f32[16,128,128]{2,1,0:T(8,128)S(1)}, f32[16,128,128]{2,1,0:T(8,128)}, u32[]{:S(2)}) copy-start(f32[16,128,128]{2,1,0:T(8,128)} %refs_0_.2) | copy-start | bytes 3145732
  4.0 11.0 %collective-permute-start = (f32[248,128]{1,0:T(8,128)}, f32[248,128]{1,0:T(8,128)S(1)}, u32[]{:S(2)}, u32[]{:S(2)}) collective-permute-start(f32[248,128]{1,0:T(8,128)} %get-tuple-element.33.refs_8_), channel_id=1, source_target_pairs={{28,0},{0,4},{4,8},{8,12},{12,16},{16,20},{20,24},{24,28},{29,1},{... | collective-permute-start | bytes 380936 | tf_op jit(solution)/shard_map/ppermute | solution.py:26
  7.0 7.9 %collective-permute-start.1 = (f32[248,128]{1,0:T(8,128)}, f32[248,128]{1,0:T(8,128)S(1)}, u32[]{:S(2)}, u32[]{:S(2)}) collective-permute-start(f32[248,128]{1,0:T(8,128)} %get-tuple-element.34.refs_7_), channel_id=1, source_target_pairs={{4,0},{8,4},{12,8},{16,12},{20,16},{24,20},{28,24},{0,28},{5,1},{9... | collective-permute-start | bytes 380936 | tf_op jit(solution)/shard_map/ppermute | solution.py:26
  8.6 5.4 %collective-permute-start.2 = (f32[88,128]{1,0:T(8,128)}, f32[88,128]{1,0:T(8,128)S(1)}, u32[]{:S(2)}, u32[]{:S(2)}) collective-permute-start(f32[88,128]{1,0:T(8,128)} %get-tuple-element.35.refs_10_), channel_id=1, source_target_pairs={{3,0},{0,1},{1,2},{2,3},{7,4},{4,5},{5,6},{6,7},{11,8},{8,9},{9,10... | collective-permute-start | bytes 135176 | tf_op jit(solution)/shard_map/ppermute | solution.py:26
  10.5 4.4 %collective-permute-start.3 = (f32[88,128]{1,0:T(8,128)}, f32[88,128]{1,0:T(8,128)S(1)}, u32[]{:S(2)}, u32[]{:S(2)}) collective-permute-start(f32[88,128]{1,0:T(8,128)} %get-tuple-element.36.refs_9_), channel_id=1, source_target_pairs={{1,0},{2,1},{3,2},{0,3},{5,4},{6,5},{7,6},{4,7},{9,8},{10,9},{11,1... | collective-permute-start | bytes 135176 | tf_op jit(solution)/shard_map/ppermute | solution.py:26
  13.2 16.2 %copy-start.1 = (f32[16,128,128]{2,1,0:T(8,128)S(1)}, f32[16,128,128]{2,1,0:T(8,128)}, u32[]{:S(2)}) copy-start(f32[16,128,128]{2,1,0:T(8,128)} %refs_1_.7) | copy-start | bytes 3145732
  14.9 18.5 %copy-start.10 = (f32[216,128]{1,0:T(8,128)S(1)}, f32[216,128]{1,0:T(8,128)}, u32[]{:S(2)}) copy-start(f32[216,128]{1,0:T(8,128)} %get-tuple-element.37.refs_0_) | copy-start | bytes 331780
  14.9 18.5 %copy-start.11 = (f32[216,128]{1,0:T(8,128)S(1)}, f32[216,128]{1,0:T(8,128)}, u32[]{:S(2)}) copy-start(f32[216,128]{1,0:T(8,128)} %get-tuple-element.38.refs_1_) | copy-start | bytes 331780
  15.0 22.5 %copy-start.6 = (s32[64,128]{1,0:T(8,128)S(1)}, s32[64,128]{1,0:T(8,128)}, u32[]{:S(2)}) copy-start(s32[64,128]{1,0:T(8,128)} %refs_2_.3) | copy-start | bytes 98308
  15.0 22.5 %copy-start.19 = (f32[4]{0:T(128)S(1)}, f32[4]{0:T(128)}, u32[]{:S(2)}) copy-start(f32[4]{0:T(128)} %refs_6_.1) | copy-start | bytes 52
  29.5 14.1 %copy-start.18 = (f32[8,128]{1,0:T(8,128)S(1)}, f32[8,128]{1,0:T(8,128)}, u32[]{:S(2)}) copy-start(f32[8,128]{1,0:T(8,128)} %copy-done.17) | copy-start | bytes 12292
  30.9 12.7 %all-to-all-start.1 = ((f32[32,8,128]{2,1,0:T(8,128)}), f32[32,8,128]{2,1,0:T(8,128)S(1)}, u32[]{:S(2)}, u32[]{:S(2)}) async-start(f32[32,8,128]{2,1,0:T(8,128)} %bitcast.9), calls=%async_computation.1 | async-start | bytes 262144 | tf_op jit(solution)/shard_map/all_to_all | solution.py:763
  33.5 8.8 %collective-permute-start.4 = (f32[216,128]{1,0:T(8,128)S(1)}, f32[216,128]{1,0:T(8,128)S(1)}, u32[]{:S(2)}, u32[]{:S(2)}) collective-permute-start(f32[216,128]{1,0:T(8,128)S(1)} %get-tuple-element.49), channel_id=1, source_target_pairs={{28,0},{0,4},{4,8},{8,12},{12,16},{16,20},{20,24},{24,28},{29,1},{... | collective-permute-start | bytes 331784 | tf_op jit(solution)/shard_map/ppermute | solution.py:26
  35.2 8.4 %collective-permute-start.5 = (f32[216,128]{1,0:T(8,128)S(1)}, f32[216,128]{1,0:T(8,128)S(1)}, u32[]{:S(2)}, u32[]{:S(2)}) collective-permute-start(f32[216,128]{1,0:T(8,128)S(1)} %get-tuple-element.50), channel_id=1, source_target_pairs={{4,0},{8,4},{12,8},{16,12},{20,16},{24,20},{28,24},{0,28},{5,1},{9... | collective-permute-start | bytes 331784 | tf_op jit(solution)/shard_map/ppermute | solution.py:26
  37.1 13.3 %copy-start.4 = (f32[248,128]{1,0:T(8,128)S(1)}, f32[248,128]{1,0:T(8,128)}, u32[]{:S(2)}) copy-start(f32[248,128]{1,0:T(8,128)} %get-tuple-element.34.refs_7_) | copy-start | bytes 380932
  37.1 13.3 %copy-start.5 = (f32[248,128]{1,0:T(8,128)S(1)}, f32[248,128]{1,0:T(8,128)}, u32[]{:S(2)}) copy-start(f32[248,128]{1,0:T(8,128)} %get-tuple-element.33.refs_8_) | copy-start | bytes 380932
  37.1 13.3 %copy-start.7 = (f32[88,128]{1,0:T(8,128)S(1)}, f32[88,128]{1,0:T(8,128)}, u32[]{:S(2)}) copy-start(f32[88,128]{1,0:T(8,128)} %get-tuple-element.36.refs_9_) | copy-start | bytes 135172
  37.1 13.3 %copy-start.8 = (f32[88,128]{1,0:T(8,128)S(1)}, f32[88,128]{1,0:T(8,128)}, u32[]{:S(2)}) copy-start(f32[88,128]{1,0:T(8,128)} %get-tuple-element.35.refs_10_) | copy-start | bytes 135172
  37.1 4.2 %collective-permute-start.6 = (f32[32,128]{1,0:T(8,128)S(1)}, f32[32,128]{1,0:T(8,128)S(1)}, u32[]{:S(2)}, u32[]{:S(2)}) collective-permute-start(f32[32,128]{1,0:T(8,128)S(1)} %get-tuple-element.52.refs_3_), channel_id=1, source_target_pairs={{16,0},{0,16},{17,1},{1,17},{18,2},{2,18},{19,3},{3,19},{20,4},{4,... | collective-permute-start | bytes 49160 | tf_op jit(solution)/shard_map/ppermute | solution.py:26
  45.2 12.7 %all-to-all-start.2 = ((f32[16,8,128]{2,1,0:T(8,128)}), f32[16,8,128]{2,1,0:T(8,128)S(1)}, u32[]{:S(2)}, u32[]{:S(2)}) async-start(f32[16,8,128]{2,1,0:T(8,128)} %bitcast.12), calls=%async_computation.2 | async-start | bytes 131072 | tf_op jit(solution)/shard_map/all_to_all | solution.py:810
  59.2 12.0 %all-to-all-start.3 = ((f32[16,8,128]{2,1,0:T(8,128)}), f32[16,8,128]{2,1,0:T(8,128)S(1)}, u32[]{:S(2)}, u32[]{:S(2)}) async-start(f32[16,8,128]{2,1,0:T(8,128)} %bitcast.15), calls=%async_computation.3 | async-start | bytes 131072 | tf_op jit(solution)/shard_map/all_to_all | solution.py:842
  (10 other events, 62.7 us)

commit v3 on v2

--- a/solution.py
+++ b/solution.py
@@ -13,7 +13,7 @@
 SECTION = ("gx", "gy")
 EVERY = ("comp", "gx", "gy")
 CAPACITY = 2
-PIECE_ROWS = 12
+PIECE_ROWS = 8
 VMEM_LIMIT = 8 * 1024 * 1024
 EDGES_LIMIT = 60 * 1024 * 1024
 SEA_LIMIT = 53 * 1024 * 1024
@@ -429,16 +429,22 @@
         chunk(out, out_far, field, field_rows, departures.at[field]).wait()
 
 
-def routes_kernel(index, own, *rest):
-    *outs, section, tally = rest
+def label_base(rows):
+    return 2.0 * rows
+
+
+def routes_kernel(index, own, diffusion, *rest):
+    *outs, labels_out, section, numbers, tally, piece_labels, sea_labels = rest
     lanes = lax.broadcasted_iota(jnp.int32, (1, section.shape[1]), 1)
     section[...] = jnp.full(section.shape, own[0].astype(F32))
+    for field in range(diffusion.shape[0]):
+        numbers[pl.ds(field, 1), :] = jnp.full(lanes.shape, diffusion[field])
 
     def clear(at, carry):
         tally[at] = 0
         return carry
 
-    for row, (slots, labels, tiles) in ((0, outs[:3]), (2, outs[3:])):
+    for row, slots, labels in ((0, outs[0], piece_labels), (2, outs[1], sea_labels)):
         slots[...] = jnp.zeros(slots.shape, F32)
         labels[...] = jnp.full(labels.shape, -1.0, F32)
         lax.fori_loop(0, tally.shape[0], clear, 0)
@@ -449,16 +455,15 @@
             slot = pl.ds(owner * CAPACITY + rank, 1)
             slots[slot, :] = (lanes == tile).astype(F32)
             labels[slot, :] = jnp.full(lanes.shape, index[row + 1, tile].astype(F32))
-        tiles[...] = jnp.transpose(slots[...])[: tiles.shape[0], :]
-
-
-def inner_kernel(at, state_far, diffusion, out, numbers, top, arrival):
+    base = label_base(index.shape[1])
+    labels_out[...] = (piece_labels[...] + 1.0) + base * (sea_labels[...] + 1.0)
+
+
+def inner_kernel(at, state_far, numbers, out, top, arrival):
     fields, rows, width = at.fields, at.rows, at.width
     copy = pltpu.make_async_copy(state_far.at[:, pl.ds(at.levels - 2, 2)], top, arrival)
     copy.start()
     lines, lanes = grid_index((rows, width))
-    for field in range(fields):
-        numbers[pl.ds(field, 1), :] = jnp.full((1, width), diffusion[field])
     copy.wait()
     for field in range(fields):
         cells = top[field, 1]
@@ -469,17 +474,17 @@
             jnp.where(lanes == width - 1, 0.0, pltpu.roll(cells, width - 1, 1)),
         )
         out[pl.ds(field * rows, rows), :] = diffused(
-            cells, top[field, 0], cells, sides, diffusion[field]
+            cells, top[field, 0], cells, sides, numbers[pl.ds(field, 1), :]
         )
 
 
 def pieces_kernel(
-    at, inner, north, south, west, east, weights, numbers, routes, labels, sea_labels, out, *scratch
+    at, inner, north, south, west, east, weights, numbers, routes, labels, out, surface, products
 ):
-    surface, products = scratch
     fields, levels, rows, width = at.fields, at.levels, at.rows, at.width
     slots = routes.shape[0]
     lines, lanes = grid_index((rows, width))
+    a = []
     for field in range(fields):
         part = field // at.half
         held = pl.ds(part * rows, rows)
@@ -491,44 +496,50 @@
             + jnp.where(lanes == 0, pltpu.roll(west[held, :], (width - lane) % width, 1), 0.0)
             + jnp.where(lanes == width - 1, pltpu.roll(east[held, :], width - 1 - lane, 1), 0.0)
         )
-        here = pl.ds(field * rows, rows)
-        surface[here, :] = inner[here, :] + numbers[pl.ds(field, 1), :] * outside
-    surface[pl.ds(fields * rows, (16 - fields) * rows), :] = jnp.zeros(
-        ((16 - fields) * rows, width), F32
-    )
+        a.append(inner[pl.ds(field * rows, rows), :] + numbers[pl.ds(field, 1), :] * outside)
+    sums = (a[0] - a[4], a[1], a[2], a[3], a[6] + a[7], a[5] + a[8], a[9])
+    for place in range(16):
+        surface[pl.ds(place * rows, rows), :] = (
+            sums[place] if place < len(sums) else jnp.zeros((rows, width), F32)
+        )
     for tile in range(rows):
         products[pl.ds(tile * 16, 16), :] = remapped(
             surface[pl.ds(tile, 16, stride=rows), :], weights[tile]
         )
+    count = PIECE_ROWS - 1
     sent = picked(
         routes[...][:, :rows],
         jnp.concatenate(
-            [products[pl.ds(field, rows, stride=16), :] for field in range(fields)], axis=1
+            [products[pl.ds(place, rows, stride=16), :] for place in range(count)], axis=1
         ),
     )
-    for field in range(fields):
-        out[pl.ds(field, slots, stride=PIECE_ROWS), :] = sent[:, field * width : (field + 1) * width]
-    out[pl.ds(fields, slots, stride=PIECE_ROWS), :] = labels[...]
-    out[pl.ds(fields + 1, slots, stride=PIECE_ROWS), :] = sea_labels[...]
+    for place in range(count):
+        out[pl.ds(place, slots, stride=PIECE_ROWS), :] = sent[:, place * width : (place + 1) * width]
+    out[pl.ds(count, slots, stride=PIECE_ROWS), :] = labels[...]
 
 
 def flux_kernel(sizes, arrived, remap, routes, out, gather, sea_labels, fluxes, products):
-    fields, flux_count, rows, sections = sizes
+    flux_count, rows, sections = sizes
     width = out.shape[1]
     slots = routes.shape[0]
-    select = one_hot(arrived[pl.ds(fields, slots, stride=PIECE_ROWS), :])
+    count = PIECE_ROWS - 1
+    labels = arrived[pl.ds(count, slots, stride=PIECE_ROWS), :]
+    upper = jnp.floor(labels * (1.0 / label_base(rows)))
+    select = one_hot(labels - label_base(rows) * upper - 1.0)
     gather[...] = select
-    sea_labels[...] = arrived[pl.ds(fields + 1, slots, stride=PIECE_ROWS), :]
+    sea_labels[...] = upper - 1.0
     values = jnp.concatenate(
-        [arrived[pl.ds(field, slots, stride=PIECE_ROWS), :] for field in range(fields)], axis=1
+        [arrived[pl.ds(place, slots, stride=PIECE_ROWS), :] for place in range(count)], axis=1
     )
     exchange = picked(jnp.transpose(select)[:rows, :], values)
-    a = [exchange[:, field * width : (field + 1) * width] for field in range(fields)]
-    speed = jnp.sqrt(a[2] * a[2] + a[3] * a[3] + 0.5)
-    fluxes[pl.ds(0, rows), :] = speed * (a[0] - a[4]) + a[6] + a[7]
-    fluxes[pl.ds(rows, rows), :] = speed * a[1] + a[5] + a[8]
-    fluxes[pl.ds(2 * rows, rows), :] = speed * a[2] * (1.0 + 0.2 * jnp.tanh(a[9]))
-    fluxes[pl.ds(3 * rows, rows), :] = speed * a[3]
+    a04, a1, a2, a3, a67, a58, a9 = (
+        exchange[:, place * width : (place + 1) * width] for place in range(count)
+    )
+    speed = jnp.sqrt(a2 * a2 + a3 * a3 + 0.5)
+    fluxes[pl.ds(0, rows), :] = speed * a04 + a67
+    fluxes[pl.ds(rows, rows), :] = speed * a1 + a58
+    fluxes[pl.ds(2 * rows, rows), :] = speed * a2 * (1.0 + 0.2 * jnp.tanh(a9))
+    fluxes[pl.ds(3 * rows, rows), :] = speed * a3
     for tile in range(rows):
         products[pl.ds(tile * flux_count, flux_count), :] = remapped(
             fluxes[pl.ds(tile, flux_count, stride=rows), :], both_halves(remap[tile])
@@ -584,11 +595,11 @@
         copy.wait()
 
 
-def tops_of_tiles(returned, tiles, flux_count, scratch):
-    rows, slots = tiles.shape
-    width = returned.shape[1]
+def tops_of_tiles(returned, routes, flux_count, scratch):
+    slots, width = routes.shape
+    rows = scratch.shape[0] // flux_count
     found = picked(
-        tiles[...],
+        jnp.transpose(routes[...])[:rows, :],
         jnp.concatenate(
             [returned[pl.ds(flux, slots, stride=flux_count), :] for flux in range(flux_count)],
             axis=1,
@@ -600,10 +611,10 @@
         ]
 
 
-def reply_kernel(flux_count, answered, remap, tiles, gather, out, tops, on_exchange):
-    rows, slots = tiles.shape
-    width = out.shape[1]
-    tops_of_tiles(answered, tiles, flux_count, tops)
+def reply_kernel(flux_count, answered, remap, routes, gather, out, tops, on_exchange):
+    slots, width = routes.shape
+    rows = remap.shape[0]
+    tops_of_tiles(answered, routes, flux_count, tops)
     for tile in range(rows):
         held = pl.ds(tile * flux_count, flux_count)
         on_exchange[held, :] = remapped(
@@ -619,9 +630,9 @@
         ]
 
 
-def surface_kernel(flux_count, returned, weights, tiles, out, tops):
-    rows, _ = tiles.shape
-    tops_of_tiles(returned, tiles, flux_count, tops)
+def surface_kernel(flux_count, returned, weights, routes, out, tops):
+    rows = weights.shape[0]
+    tops_of_tiles(returned, routes, flux_count, tops)
     for tile in range(rows):
         out[pl.ds(tile, flux_count, stride=rows), :] = remapped(
             tops[pl.ds(tile * flux_count, flux_count), :], weights[tile]
@@ -714,25 +725,25 @@
             [VMEM],
         )(gated(remap, before))
 
-    tile_slots, piece_labels, slot_tiles, sea_slots, sea_labels, sea_tiles, here = call(
+    tile_slots, sea_slots, labels, here, numbers = call(
         routes_kernel,
         "routes",
-        ((array(slots, width),) * 2 + (array(rows, slots),)) * 2 + (array(8, width),),
-        [SMEM, SMEM],
-        [pltpu.SMEM((targets,), jnp.int32)],
-    )(gated(index, first_cols), section)
-    inner, numbers = call(
+        (array(slots, width),) * 3 + (array(8, width), array(-(-fields // 8) * 8, width)),
+        [SMEM] * 3,
+        [pltpu.SMEM((targets,), jnp.int32)] + [pltpu.VMEM((slots, width), F32)] * 2,
+    )(gated(index, first_cols), section, atmos_diffusion)
+    inner = call(
         functools.partial(inner_kernel, at),
         "inner",
-        (array(fields * rows, width), array(-(-fields // 8) * 8, width)),
-        [ANY, SMEM],
+        array(fields * rows, width),
+        [ANY, VMEM],
         [pltpu.VMEM((fields, 2, rows, width), F32), pltpu.SemaphoreType.DMA],
-    )(gated(atmos_state, first_cols), atmos_diffusion)
+    )(gated(atmos_state, first_cols), numbers)
     pieces = call(
         functools.partial(pieces_kernel, at),
         "pieces",
         array(slots * PIECE_ROWS, width),
-        [VMEM] * 10,
+        [VMEM] * 9,
         [pltpu.VMEM((16 * rows, width), F32)] * 2,
     )(
         inner,
@@ -743,14 +754,13 @@
         weights_of(remap_atmos, False, "piece_weights", first_cols),
         numbers,
         tile_slots,
-        piece_labels,
-        sea_labels,
+        labels,
     )
     arrived = lax.all_to_all(
         pieces.reshape(targets, CAPACITY * PIECE_ROWS, width), SECTION, 0, 0, tiled=True
     )
     outgoing, gather, own_labels = call(
-        functools.partial(flux_kernel, (fields, sea_fields, rows, sections)),
+        functools.partial(flux_kernel, (sea_fields, rows, sections)),
         "fluxes",
         (
             array(sections * slots * sea_fields, width),
@@ -838,7 +848,7 @@
         array(slots * sea_fields, width),
         [VMEM] * 4,
         [pltpu.VMEM((sea_fields * rows, width), F32)] * 2,
-    )(answered.reshape(slots * sea_fields, width), remap_ocean, sea_tiles, gather)
+    )(answered.reshape(slots * sea_fields, width), remap_ocean, sea_slots, gather)
     returned = lax.all_to_all(
         replies.reshape(targets, CAPACITY * sea_fields, width), SECTION, 0, 0, tiled=True
     )
@@ -854,7 +864,7 @@
     )(
         returned.reshape(slots * sea_fields, width),
         weights_of(remap_atmos, True, "surface_weights", replies),
-        slot_tiles,
+        tile_slots,
     )
     return (
         atmos_next.reshape(atmos_state.shape),

time: 72.8 us -> 71.9 us (0.988)
  waiting for transfers between devices: 8.05 us -> 9.21 us
  blocking collectives: 13.9 us -> 13 us
    ppermute x7, waiting for transfers between devices: 3.23 us -> 4.39 us  [shifted(): return lax.ppermute(block, axis, route)]
    all_to_all x1, blocking collectives: 13.9 us -> 13 us  [on_device(): lax.all_to_all(pieces.reshape(targets, CAPACITY * PIECE_ROWS, width), SEC...]
  transfers between devices with their start and end apart: 10 -> 10, of which waited for: 5 -> 6; matrix products, arithmetic and copies ran while one was open for 0% -> 0% of each run, Pallas kernels for 22% -> 21%
where the time goes in v3:
time: 71.9 us; the launch traced here: 71.4 us
  Pallas kernels  24.3 us (34%)
  starting transfers between devices  23.7 us (33%)
  blocking collectives  13 us (18%)
  waiting for transfers between devices  9.21 us (13%)
  between operations  1.02 us (1%)
    pallas_call x14, Pallas kernels, call(): return lambda *arguments: run(*arguments, *after)  24.3 us
    all_to_all x1, blocking collectives, on_device(): lax.all_to_all(pieces.reshape(targets, CAPACITY * PIECE_ROWS, width), SEC...  13 us
    ppermute x7, starting transfers between devices, shifted(): return lax.ppermute(block, axis, route)  11.5 us
    all_to_all x1, starting transfers between devices, on_device(): lax.all_to_all(answers.reshape(targets, CAPACITY * sea_fields, width), SE...  5.21 us
    all_to_all x1, starting transfers between devices, on_device(): lax.all_to_all(replies.reshape(targets, CAPACITY * sea_fields, width), SE...  4.49 us
    ppermute x7, waiting for transfers between devices, shifted(): return lax.ppermute(block, axis, route)  4.39 us
    all_to_all x1, starting transfers between devices, on_device(): lax.all_to_all(outgoing.reshape(devices, CAPACITY * sea_fields, width), E...  2.58 us
    all_to_all x1, waiting for transfers between devices, on_device(): lax.all_to_all(answers.reshape(targets, CAPACITY * sea_fields, width), SE...  2.57 us
  transfers between devices with their start and end apart: 10, of which 6 were waited for; matrix products, arithmetic and copies ran while one was open for 0% of the time, Pallas kernels for 21%

profile of v3, /device:TPU:0, one launch (start us, length us, event | category | flops | bytes accessed | tf_op | source)
XLA Modules:
  0.0 71.4 jit_solution(5885229250491418543)
XLA Ops:
  0.7 3.2 %edges.1 = (f32[248,128]{1,0:T(8,128)}, f32[248,128]{1,0:T(8,128)}, f32[216,128]{1,0:T(8,128)}, f32[216,128]{1,0:T(8,128)}, f32[88,128]{1,0:T(8,128)}, /*index=5*/f32[88,128]{1,0:T(8,128)}) custom-call(f32[3200,128]{1,0:T(8,128)} %bitcast.18, f32[2048,128]{1,0:T(8,128)} %bitcast.27, s32[64,128]{1,0:T(8,128)} %refs_2_.5), custom_call_target="tpu_custom_call" | custom-call | bytes 1000000 | tf_op jit(solution)/shard_map/edges/pallas_call | solution.py:665
  4.0 3.1 %collective-permute-start = (f32[248,128]{1,0:T(8,128)}, f32[248,128]{1,0:T(8,128)S(1)}, u32[]{:S(2)}, u32[]{:S(2)}) collective-permute-start(f32[248,128]{1,0:T(8,128)} %get-tuple-element.29.refs_8_), channel_id=1, source_target_pairs={{28,0},{0,4},{4,8},{8,12},{12,16},{16,20},{20,24},{24,28},{29,1},{... | collective-permute-start | bytes 380936 | tf_op jit(solution)/shard_map/ppermute | solution.py:26
  7.0 1.5 %collective-permute-start.1 = (f32[248,128]{1,0:T(8,128)}, f32[248,128]{1,0:T(8,128)S(1)}, u32[]{:S(2)}, u32[]{:S(2)}) collective-permute-start(f32[248,128]{1,0:T(8,128)} %get-tuple-element.30.refs_7_), channel_id=1, source_target_pairs={{4,0},{8,4},{12,8},{16,12},{20,16},{24,20},{28,24},{0,28},{5,1},{9... | collective-permute-start | bytes 380936 | tf_op jit(solution)/shard_map/ppermute | solution.py:26
  8.6 1.9 %collective-permute-start.2 = (f32[88,128]{1,0:T(8,128)}, f32[88,128]{1,0:T(8,128)S(1)}, u32[]{:S(2)}, u32[]{:S(2)}) collective-permute-start(f32[88,128]{1,0:T(8,128)} %get-tuple-element.31.refs_10_), channel_id=1, source_target_pairs={{3,0},{0,1},{1,2},{2,3},{7,4},{4,5},{5,6},{6,7},{11,8},{8,9},{9,10... | collective-permute-start | bytes 135176 | tf_op jit(solution)/shard_map/ppermute | solution.py:26
  10.5 1.0 %collective-permute-start.3 = (f32[88,128]{1,0:T(8,128)}, f32[88,128]{1,0:T(8,128)S(1)}, u32[]{:S(2)}, u32[]{:S(2)}) collective-permute-start(f32[88,128]{1,0:T(8,128)} %get-tuple-element.32.refs_9_), channel_id=1, source_target_pairs={{1,0},{2,1},{3,2},{0,3},{5,4},{6,5},{7,6},{4,7},{9,8},{10,9},{11,1... | collective-permute-start | bytes 135176 | tf_op jit(solution)/shard_map/ppermute | solution.py:26
  12.8 1.1 %collective-permute-done.2.refs_3_.refs_2_.refs_4_ = f32[88,128]{1,0:T(8,128)S(1)} collective-permute-done((f32[88,128]{1,0:T(8,128)}, f32[88,128]{1,0:T(8,128)S(1)}, u32[]{:S(2)}, u32[]{:S(2)}) %collective-permute-start.2) | collective-permute-done | bytes 45088 | tf_op jit(solution)/shard_map/ppermute | solution.py:26
  13.9 1.0 %collective-permute-done.3.refs_4_.refs_3_.refs_5_ = f32[88,128]{1,0:T(8,128)S(1)} collective-permute-done((f32[88,128]{1,0:T(8,128)}, f32[88,128]{1,0:T(8,128)S(1)}, u32[]{:S(2)}, u32[]{:S(2)}) %collective-permute-start.3) | collective-permute-done | bytes 45088 | tf_op jit(solution)/shard_map/ppermute | solution.py:26
  15.6 13.0 %all_to_all.20 = f32[16,16,128]{2,1,0:T(8,128)S(1)} all-to-all(f32[16,16,128]{2,1,0:T(8,128)S(1)} %bitcast.22), channel_id=1, replica_groups=mesh['comp'=2,'gx'=4,'gy'=4] {'gx','gy'}, dimensions={0} | all-to-all | bytes 262144 | tf_op jit(solution)/shard_map/all_to_all | solution.py:759
  28.6 1.3 %fluxes.1 = (f32[256,128]{1,0:T(8,128)}, f32[32,128]{1,0:T(8,128)S(1)}, f32[32,128]{1,0:T(8,128)S(1)}) custom-call(f32[256,128]{1,0:T(8,128)S(1)} %bitcast.23, f32[16,128,128]{2,1,0:T(8,128)S(1)} %copy-done.1, f32[32,128]{1,0:T(8,128)S(1)} %get-tuple-element.41.refs_2_), custom_call_target="tpu_custom_call" | custom-call | bytes 1000000 | tf_op jit(solution)/shard_map/fluxes/pallas_call | solution.py:665
  30.0 2.6 %all-to-all-start.1 = ((f32[32,8,128]{2,1,0:T(8,128)}), f32[32,8,128]{2,1,0:T(8,128)S(1)}, u32[]{:S(2)}, u32[]{:S(2)}) async-start(f32[32,8,128]{2,1,0:T(8,128)} %bitcast.9), calls=%async_computation.1 | async-start | bytes 262144 | tf_op jit(solution)/shard_map/all_to_all | solution.py:773
  32.6 1.7 %collective-permute-start.4 = (f32[216,128]{1,0:T(8,128)S(1)}, f32[216,128]{1,0:T(8,128)S(1)}, u32[]{:S(2)}, u32[]{:S(2)}) collective-permute-start(f32[216,128]{1,0:T(8,128)S(1)} %get-tuple-element.43), channel_id=1, source_target_pairs={{28,0},{0,4},{4,8},{8,12},{12,16},{16,20},{20,24},{24,28},{29,1},{... | collective-permute-start | bytes 331784 | tf_op jit(solution)/shard_map/ppermute | solution.py:26
  34.3 1.9 %collective-permute-start.5 = (f32[216,128]{1,0:T(8,128)S(1)}, f32[216,128]{1,0:T(8,128)S(1)}, u32[]{:S(2)}, u32[]{:S(2)}) collective-permute-start(f32[216,128]{1,0:T(8,128)S(1)} %get-tuple-element.44), channel_id=1, source_target_pairs={{4,0},{8,4},{12,8},{16,12},{20,16},{24,20},{28,24},{0,28},{5,1},{9... | collective-permute-start | bytes 331784 | tf_op jit(solution)/shard_map/ppermute | solution.py:26
  36.5 3.9 %sea_base.1 = (f32[2048,128]{1,0:T(8,128)}, f32[256,128]{1,0:T(8,128)S(1)}) custom-call(f32[2048,128]{1,0:T(8,128)} %bitcast.28, s32[64,128]{1,0:T(8,128)S(1)} %copy-done.6, f32[248,128]{1,0:T(8,128)S(1)} %collective-permute-done.refs_1_.refs_2_, f32[248,128]{1,0:T(8,128)S(1)} %collective-permute-done.1.refs_2_.refs_3_, ...), custom_call_target="tpu_custom_call" | custom-call | bytes 1000000000 | tf_op jit(solution)/shard_map/sea_base/pallas_call | solution.py:665
  40.4 0.9 %collective-permute-done.4.refs_7_.refs_5_ = f32[216,128]{1,0:T(8,128)S(1)} collective-permute-done((f32[216,128]{1,0:T(8,128)S(1)}, f32[216,128]{1,0:T(8,128)S(1)}, u32[]{:S(2)}, u32[]{:S(2)}) %collective-permute-start.4) | collective-permute-done | bytes 110624 | tf_op jit(solution)/shard_map/ppermute | solution.py:26
  41.4 1.3 %collective-permute-done.5.refs_8_.refs_6_ = f32[216,128]{1,0:T(8,128)S(1)} collective-permute-done((f32[216,128]{1,0:T(8,128)S(1)}, f32[216,128]{1,0:T(8,128)S(1)}, u32[]{:S(2)}, u32[]{:S(2)}) %collective-permute-start.5) | collective-permute-done | bytes 110624 | tf_op jit(solution)/shard_map/ppermute | solution.py:26
  42.7 1.6 %sea_top.1 = (f32[4,8,64,128]{3,2,1,0:T(8,128)}, f32[128,128]{1,0:T(8,128)}) custom-call(f32[256,128]{1,0:T(8,128)S(1)} %bitcast.21, f32[256,128]{1,0:T(8,128)S(1)} %get-tuple-element.45.refs_1_, s32[64,128]{1,0:T(8,128)S(1)} %copy-done.6, f32[32,128]{1,0:T(8,128)S(1)} %get-tuple-element.46.refs_3_, ...), custom_call_target="tpu_custom_call", output_to_operand_aliasing={{0}: (6, {})} | custom-call | bytes 1000000 | tf_op jit(solution)/shard_map/sea_top/pallas_call | solution.py:665
  44.3 5.2 %all-to-all-start.2 = ((f32[16,8,128]{2,1,0:T(8,128)}), f32[16,8,128]{2,1,0:T(8,128)S(1)}, u32[]{:S(2)}, u32[]{:S(2)}) async-start(f32[16,8,128]{2,1,0:T(8,128)} %bitcast.12), calls=%async_computation.2 | async-start | bytes 131072 | tf_op jit(solution)/shard_map/all_to_all | solution.py:820
  49.5 4.9 %steps_a.1.refs_12_ = f32[3200,128]{1,0:T(8,128)} custom-call(f32[3200,128]{1,0:T(8,128)} %bitcast.19, f32[248,128]{1,0:T(8,128)S(1)} %collective-permute-done.refs_1_.refs_2_, f32[248,128]{1,0:T(8,128)S(1)} %collective-permute-done.1.refs_2_.refs_3_, f32[88,128]{1,0:T(8,128)S(1)} %collective-permute-done.2.refs_3_.refs_2_.refs_4_, ...), custom_call_target="tpu_custom_call" | custom-call | bytes 1000000000 | tf_op jit(solution)/shard_map/steps_a/pallas_call | solution.py:665
  54.5 2.6 %all-to-all-done.2 = f32[16,8,128]{2,1,0:T(8,128)S(1)} async-done(((f32[16,8,128]{2,1,0:T(8,128)}), f32[16,8,128]{2,1,0:T(8,128)S(1)}, u32[]{:S(2)}, u32[]{:S(2)}) %all-to-all-start.2) | async-done | bytes 65568 | tf_op jit(solution)/shard_map/all_to_all | solution.py:820
  57.0 1.3 %replies.1.refs_13_ = f32[128,128]{1,0:T(8,128)} custom-call(f32[128,128]{1,0:T(8,128)S(1)} %bitcast.25, f32[16,128,128]{2,1,0:T(8,128)S(1)} %copy-done.1, f32[32,128]{1,0:T(8,128)S(1)} %copy-done.15, f32[32,128]{1,0:T(8,128)S(1)} %get-tuple-element.52.refs_3_), custom_call_target="tpu_custom_call" | custom-call | bytes 1000000 | tf_op jit(solution)/shard_map/replies/pallas_call | solution.py:665
  58.3 4.5 %all-to-all-start.3 = ((f32[16,8,128]{2,1,0:T(8,128)}), f32[16,8,128]{2,1,0:T(8,128)S(1)}, u32[]{:S(2)}, u32[]{:S(2)}) async-start(f32[16,8,128]{2,1,0:T(8,128)} %bitcast.15), calls=%async_computation.3 | async-start | bytes 131072 | tf_op jit(solution)/shard_map/all_to_all | solution.py:852
  63.2 4.9 %steps_b.1 = f32[3200,128]{1,0:T(8,128)} custom-call(f32[3200,128]{1,0:T(8,128)} %bitcast.20, f32[248,128]{1,0:T(8,128)S(1)} %collective-permute-done.refs_1_.refs_2_, f32[248,128]{1,0:T(8,128)S(1)} %collective-permute-done.1.refs_2_.refs_3_, f32[88,128]{1,0:T(8,128)S(1)} %collective-permute-done.2.refs_3_.refs_2_.refs_4_, ...), custom_call_target="tpu_custom_call", output_to_operand_aliasing={{}: (12, {})} | custom-call | bytes 1000000000 | tf_op jit(solution)/shard_map/steps_b/pallas_call | solution.py:665
  68.1 2.2 %all-to-all-done.3 = f32[16,8,128]{2,1,0:T(8,128)S(1)} async-done(((f32[16,8,128]{2,1,0:T(8,128)}), f32[16,8,128]{2,1,0:T(8,128)S(1)}, u32[]{:S(2)}, u32[]{:S(2)}) %all-to-all-start.3) | async-done | bytes 65568 | tf_op jit(solution)/shard_map/all_to_all | solution.py:852
  70.4 1.1 %surface.1 = f32[64,128]{1,0:T(8,128)} custom-call(f32[128,128]{1,0:T(8,128)S(1)} %bitcast.24, bf16[16,256,128]{2,1,0:T(8,128)(2,1)S(1)} %surface_weights.1.refs_1_, f32[32,128]{1,0:T(8,128)S(1)} %copy-done.13), custom_call_target="tpu_custom_call" | custom-call | bytes 1000000 | tf_op jit(solution)/shard_map/surface/pallas_call | solution.py:665
  (60 shorter events, 2.6 us)
Async XLA Ops:
  0.6 10.9 %copy-start.20 = (s32[16]{0:T(128)S(1)}, s32[16]{0:T(128)}, u32[]{:S(2)}) copy-start(s32[16]{0:T(128)} %param.18) | copy-start | bytes 196
  0.6 10.9 %copy-start.21 = (s32[16,1]{0,1:T(1,128)S(1)}, s32[16,1]{0,1:T(1,128)}, u32[]{:S(2)}) copy-start(s32[16,1]{0,1:T(1,128)} %param.17) | copy-start | bytes 196
  0.7 10.9 %copy-start.2 = (f32[16,128,128]{2,1,0:T(8,128)S(1)}, f32[16,128,128]{2,1,0:T(8,128)}, u32[]{:S(2)}) copy-start(f32[16,128,128]{2,1,0:T(8,128)} %refs_0_.2) | copy-start | bytes 3145732
  4.0 11.0 %collective-permute-start = (f32[248,128]{1,0:T(8,128)}, f32[248,128]{1,0:T(8,128)S(1)}, u32[]{:S(2)}, u32[]{:S(2)}) collective-permute-start(f32[248,128]{1,0:T(8,128)} %get-tuple-element.29.refs_8_), channel_id=1, source_target_pairs={{28,0},{0,4},{4,8},{8,12},{12,16},{16,20},{20,24},{24,28},{29,1},{... | collective-permute-start | bytes 380936 | tf_op jit(solution)/shard_map/ppermute | solution.py:26
  7.0 7.9 %collective-permute-start.1 = (f32[248,128]{1,0:T(8,128)}, f32[248,128]{1,0:T(8,128)S(1)}, u32[]{:S(2)}, u32[]{:S(2)}) collective-permute-start(f32[248,128]{1,0:T(8,128)} %get-tuple-element.30.refs_7_), channel_id=1, source_target_pairs={{4,0},{8,4},{12,8},{16,12},{20,16},{24,20},{28,24},{0,28},{5,1},{9... | collective-permute-start | bytes 380936 | tf_op jit(solution)/shard_map/ppermute | solution.py:26
  8.6 5.3 %collective-permute-start.2 = (f32[88,128]{1,0:T(8,128)}, f32[88,128]{1,0:T(8,128)S(1)}, u32[]{:S(2)}, u32[]{:S(2)}) collective-permute-start(f32[88,128]{1,0:T(8,128)} %get-tuple-element.31.refs_10_), channel_id=1, source_target_pairs={{3,0},{0,1},{1,2},{2,3},{7,4},{4,5},{5,6},{6,7},{11,8},{8,9},{9,10... | collective-permute-start | bytes 135176 | tf_op jit(solution)/shard_map/ppermute | solution.py:26
  10.5 4.4 %collective-permute-start.3 = (f32[88,128]{1,0:T(8,128)}, f32[88,128]{1,0:T(8,128)S(1)}, u32[]{:S(2)}, u32[]{:S(2)}) collective-permute-start(f32[88,128]{1,0:T(8,128)} %get-tuple-element.32.refs_9_), channel_id=1, source_target_pairs={{1,0},{2,1},{3,2},{0,3},{5,4},{6,5},{7,6},{4,7},{9,8},{10,9},{11,1... | collective-permute-start | bytes 135176 | tf_op jit(solution)/shard_map/ppermute | solution.py:26
  12.6 16.0 %copy-start.14 = (f32[32,128]{1,0:T(8,128)}, f32[32,128]{1,0:T(8,128)S(1)}, u32[]{:S(2)}) copy-start(f32[32,128]{1,0:T(8,128)S(1)} %get-tuple-element.41.refs_2_) | copy-start | bytes 49156
  12.6 16.0 %copy-start.1 = (f32[16,128,128]{2,1,0:T(8,128)S(1)}, f32[16,128,128]{2,1,0:T(8,128)}, u32[]{:S(2)}) copy-start(f32[16,128,128]{2,1,0:T(8,128)} %refs_1_.5) | copy-start | bytes 3145732
  15.0 17.6 %copy-start.10 = (f32[216,128]{1,0:T(8,128)S(1)}, f32[216,128]{1,0:T(8,128)}, u32[]{:S(2)}) copy-start(f32[216,128]{1,0:T(8,128)} %get-tuple-element.33.refs_0_) | copy-start | bytes 331780
  15.0 17.6 %copy-start.11 = (f32[216,128]{1,0:T(8,128)S(1)}, f32[216,128]{1,0:T(8,128)}, u32[]{:S(2)}) copy-start(f32[216,128]{1,0:T(8,128)} %get-tuple-element.34.refs_1_) | copy-start | bytes 331780
  15.0 21.6 %copy-start.6 = (s32[64,128]{1,0:T(8,128)S(1)}, s32[64,128]{1,0:T(8,128)}, u32[]{:S(2)}) copy-start(s32[64,128]{1,0:T(8,128)} %refs_2_.5) | copy-start | bytes 98308
  15.0 21.6 %copy-start.19 = (f32[4]{0:T(128)S(1)}, f32[4]{0:T(128)}, u32[]{:S(2)}) copy-start(f32[4]{0:T(128)} %refs_6_.1) | copy-start | bytes 52
  28.6 14.1 %copy-start.18 = (f32[8,128]{1,0:T(8,128)S(1)}, f32[8,128]{1,0:T(8,128)}, u32[]{:S(2)}) copy-start(f32[8,128]{1,0:T(8,128)} %copy-done.17) | copy-start | bytes 12292
  30.0 12.7 %all-to-all-start.1 = ((f32[32,8,128]{2,1,0:T(8,128)}), f32[32,8,128]{2,1,0:T(8,128)S(1)}, u32[]{:S(2)}, u32[]{:S(2)}) async-start(f32[32,8,128]{2,1,0:T(8,128)} %bitcast.9), calls=%async_computation.1 | async-start | bytes 262144 | tf_op jit(solution)/shard_map/all_to_all | solution.py:773
  32.6 8.8 %collective-permute-start.4 = (f32[216,128]{1,0:T(8,128)S(1)}, f32[216,128]{1,0:T(8,128)S(1)}, u32[]{:S(2)}, u32[]{:S(2)}) collective-permute-start(f32[216,128]{1,0:T(8,128)S(1)} %get-tuple-element.43), channel_id=1, source_target_pairs={{28,0},{0,4},{4,8},{8,12},{12,16},{16,20},{20,24},{24,28},{29,1},{... | collective-permute-start | bytes 331784 | tf_op jit(solution)/shard_map/ppermute | solution.py:26
  34.3 8.4 %collective-permute-start.5 = (f32[216,128]{1,0:T(8,128)S(1)}, f32[216,128]{1,0:T(8,128)S(1)}, u32[]{:S(2)}, u32[]{:S(2)}) collective-permute-start(f32[216,128]{1,0:T(8,128)S(1)} %get-tuple-element.44), channel_id=1, source_target_pairs={{4,0},{8,4},{12,8},{16,12},{20,16},{24,20},{28,24},{0,28},{5,1},{9... | collective-permute-start | bytes 331784 | tf_op jit(solution)/shard_map/ppermute | solution.py:26
  36.2 13.3 %copy-start.4 = (f32[248,128]{1,0:T(8,128)S(1)}, f32[248,128]{1,0:T(8,128)}, u32[]{:S(2)}) copy-start(f32[248,128]{1,0:T(8,128)} %get-tuple-element.30.refs_7_) | copy-start | bytes 380932
  36.2 13.3 %copy-start.5 = (f32[248,128]{1,0:T(8,128)S(1)}, f32[248,128]{1,0:T(8,128)}, u32[]{:S(2)}) copy-start(f32[248,128]{1,0:T(8,128)} %get-tuple-element.29.refs_8_) | copy-start | bytes 380932
  36.2 13.3 %copy-start.7 = (f32[88,128]{1,0:T(8,128)S(1)}, f32[88,128]{1,0:T(8,128)}, u32[]{:S(2)}) copy-start(f32[88,128]{1,0:T(8,128)} %get-tuple-element.32.refs_9_) | copy-start | bytes 135172
  36.2 13.3 %copy-start.8 = (f32[88,128]{1,0:T(8,128)S(1)}, f32[88,128]{1,0:T(8,128)}, u32[]{:S(2)}) copy-start(f32[88,128]{1,0:T(8,128)} %get-tuple-element.31.refs_10_) | copy-start | bytes 135172
  36.2 4.2 %collective-permute-start.6 = (f32[32,128]{1,0:T(8,128)S(1)}, f32[32,128]{1,0:T(8,128)S(1)}, u32[]{:S(2)}, u32[]{:S(2)}) collective-permute-start(f32[32,128]{1,0:T(8,128)S(1)} %get-tuple-element.46.refs_3_), channel_id=1, source_target_pairs={{16,0},{0,16},{17,1},{1,17},{18,2},{2,18},{19,3},{3,19},{20,4},{4,... | collective-permute-start | bytes 49160 | tf_op jit(solution)/shard_map/ppermute | solution.py:26
  44.3 12.8 %all-to-all-start.2 = ((f32[16,8,128]{2,1,0:T(8,128)}), f32[16,8,128]{2,1,0:T(8,128)S(1)}, u32[]{:S(2)}, u32[]{:S(2)}) async-start(f32[16,8,128]{2,1,0:T(8,128)} %bitcast.12), calls=%async_computation.2 | async-start | bytes 131072 | tf_op jit(solution)/shard_map/all_to_all | solution.py:820
  58.3 12.0 %all-to-all-start.3 = ((f32[16,8,128]{2,1,0:T(8,128)}), f32[16,8,128]{2,1,0:T(8,128)S(1)}, u32[]{:S(2)}, u32[]{:S(2)}) async-start(f32[16,8,128]{2,1,0:T(8,128)} %bitcast.15), calls=%async_computation.3 | async-start | bytes 131072 | tf_op jit(solution)/shard_map/all_to_all | solution.py:852
  (10 other events, 71.9 us)

commit v4 on v3

--- a/solution.py
+++ b/solution.py
@@ -70,6 +70,15 @@
     middle = rest.astype(BF16)
     low = (rest - middle.astype(F32)).astype(BF16)
     return dot(chosen, high) + dot(chosen, middle) + dot(chosen, low)
+
+
+def placed(values, selection):
+    chosen = selection.astype(BF16)
+    high = values.astype(BF16)
+    rest = values - high.astype(F32)
+    middle = rest.astype(BF16)
+    low = (rest - middle.astype(F32)).astype(BF16)
+    return dot(high, chosen) + dot(middle, chosen) + dot(low, chosen)
 
 
 def one_hot(labels):
@@ -262,27 +271,39 @@
         out[...] = diffused(cells, upper, lower, sides, numbers)
 
 
-def field_step(at, field, state, out, north, south, first_line, west_cols, east_cols, number):
+def interleaved(at, west, east):
+    width = at.width
+    fields_each = width // 2 // at.levels
+    columns = jnp.concatenate([east, west], axis=1)
+    source, target = grid_index((2 * width, width))
+    out = []
+    for first in range(0, at.half, fields_each):
+        block = jnp.where(source < width, source, source - width) - first * at.levels
+        lane = 2 * block + jnp.where(source < width, 0, 1)
+        out.append(placed(columns, (lane == target).astype(F32)))
+    return out
+
+
+def field_step(at, field, state, out, north, south, first_line, beside, number):
     levels, rows, width = at.levels, at.rows, at.width
+    fields_each = width // 2 // levels
     lines, lanes = grid_index((rows, width))
     for level in range(levels):
         line = first_line + field * levels + level
-        start = pl.multiple_of((field * levels + level) * rows, rows)
+        start = (field * levels + level) * rows
         cells = state[pl.ds(start, rows), :]
         first_level, last_level = level == 0, level == levels - 1
         upper = cells if first_level else state[pl.ds(start - rows, rows), :]
         lower = cells if last_level else state[pl.ds(start + rows, rows), :]
+        lane = 2 * ((field % fields_each) * levels + level) + 1
+        edge = pltpu.roll(beside[field // fields_each], width - lane, 1)
         sides = (
             jnp.where(lines == 0, north[pl.ds(line, 1), :], pltpu.roll(cells, 1, 0)),
             jnp.where(
                 lines == rows - 1, south[pl.ds(line, 1), :], pltpu.roll(cells, rows - 1, 0)
             ),
-            jnp.where(lanes == 0, pltpu.roll(west_cols, (width - level) % width, 1), pltpu.roll(cells, 1, 1)),
-            jnp.where(
-                lanes == width - 1,
-                pltpu.roll(east_cols, width - 1 - level, 1),
-                pltpu.roll(cells, width - 1, 1),
-            ),
+            jnp.where(lanes == 0, edge, pltpu.roll(cells, 1, 1)),
+            jnp.where(lanes == width - 1, edge, pltpu.roll(cells, width - 1, 1)),
         )
         out[pl.ds(start, rows), :] = diffused(cells, upper, lower, sides, number)
 
@@ -313,15 +334,15 @@
 
     def coming(field):
         return pltpu.make_async_copy(
-            state_far.at[pl.ds(pl.multiple_of((whole + field) * field_rows, 8), field_rows)],
-            state.at[pl.ds(pl.multiple_of(field * field_rows, 8), field_rows)],
+            state_far.at[pl.ds((whole + field) * field_rows, field_rows)],
+            state.at[pl.ds(field * field_rows, field_rows)],
             arrivals.at[field],
         )
 
     def going(field):
         return pltpu.make_async_copy(
-            out.at[pl.ds(pl.multiple_of(field * field_rows, 8), field_rows)],
-            out_far.at[pl.ds(pl.multiple_of((whole + field) * field_rows, 8), field_rows)],
+            out.at[pl.ds(field * field_rows, field_rows)],
+            out_far.at[pl.ds((whole + field) * field_rows, field_rows)],
             departures.at[field],
         )
 
@@ -330,22 +351,16 @@
     halos = (north, south, west, east, far_north, far_south)
     ring_step(at, part, halos, (near_first, near_last, first, last), diffusion, ring)
     held = pl.ds(part * rows, rows)
-
-    def both_steps(field, carry):
-        back = lax.rem(width - field * levels, width)
+    outer = interleaved(at, west[held, :], east[held, :])
+    inner = interleaved(at, ring[2][...], ring[3][...])
+    for field in range(at.half):
         number = diffusion[whole + field]
-        west_cols = pltpu.roll(west[held, :], back, 1)
-        east_cols = pltpu.roll(east[held, :], back, 1)
         coming(field).wait()
-        line = part * at.part_rows
-        field_step(at, field, state, middle, north, south, line, west_cols, east_cols, number)
-        west_cols = pltpu.roll(ring[2][...], back, 1)
-        east_cols = pltpu.roll(ring[3][...], back, 1)
-        field_step(at, field, middle, out, ring[0], ring[1], 0, west_cols, east_cols, number)
+        field_step(
+            at, field, state, middle, north, south, part * at.part_rows, outer, number
+        )
+        field_step(at, field, middle, out, ring[0], ring[1], 0, inner, number)
         going(field).start()
-        return carry
-
-    lax.fori_loop(0, at.half, both_steps, 0)
     for field in range(at.half):
         going(field).wait()
 
@@ -559,7 +574,7 @@
 
 
 def sea_kernel(
-    sizes, landed, base_tops, wet, own_labels, other_labels, section, base, out, answers, tops, leave
+    sizes, landed, base_tops, wet, own_labels, other_labels, section, tops, answers
 ):
     flux_count, sea_rows = sizes
     width = landed.shape[1]
@@ -575,14 +590,11 @@
     )
     forcing = picked(jnp.transpose(select)[:sea_rows, :], values)
     wet_cells = wet[...].astype(F32)
-    copies = []
     for flux in range(flux_count):
         held = pl.ds(flux * sea_rows, sea_rows)
         tops[held, :] = base_tops[held, :] + wet_cells * (
             FORCING_SCALE[flux] * forcing[:, flux * width : (flux + 1) * width]
         )
-        copies.append(pltpu.make_async_copy(tops.at[held], out.at[flux, 0], leave.at[flux]))
-        copies[flux].start()
     all_tops = jnp.concatenate(
         [tops[pl.ds(flux * sea_rows, sea_rows), :] for flux in range(flux_count)], axis=1
     )
@@ -591,6 +603,17 @@
         answers[pl.ds(flux, slots, stride=flux_count), :] = reply[
             :, flux * width : (flux + 1) * width
         ]
+
+
+def store_kernel(sea_rows, tops, base, out, leave):
+    copies = [
+        pltpu.make_async_copy(
+            tops.at[pl.ds(flux * sea_rows, sea_rows)], out.at[flux, 0], leave.at[flux]
+        )
+        for flux in range(out.shape[0])
+    ]
+    for copy in copies:
+        copy.start()
     for copy in copies:
         copy.wait()
 
@@ -796,18 +819,12 @@
         out_specs=(ANY, VMEM),
     )(ocean, wet_mask, north, south, west, east, ocean_mixing)
 
-    ocean_next, answers = call(
+    tops, answers = call(
         functools.partial(sea_kernel, (sea_fields, sea_rows)),
         "sea_top",
-        (
-            array(sea_fields, sea_levels, sea_rows, width),
-            array(slots * sea_fields, width),
-        ),
-        [VMEM] * 6 + [ANY],
-        [pltpu.VMEM((sea_fields * sea_rows, width), F32), ocean_flags],
+        (array(sea_fields * sea_rows, width), array(slots * sea_fields, width)),
+        [VMEM] * 6,
         after=(far_north, far_south),
-        out_specs=(ANY, VMEM),
-        input_output_aliases={6: 0},
     )(
         landed.reshape(devices * CAPACITY * sea_fields, width),
         base_tops,
@@ -815,8 +832,16 @@
         own_labels,
         other_labels,
         here,
-        sea_base.reshape(sea_fields, sea_levels, sea_rows, width),
-    )
+    )
+    ocean_next = call(
+        functools.partial(store_kernel, sea_rows),
+        "store",
+        array(sea_fields, sea_levels, sea_rows, width),
+        [VMEM, ANY],
+        [ocean_flags],
+        out_specs=ANY,
+        input_output_aliases={1: 0},
+    )(tops, sea_base.reshape(sea_fields, sea_levels, sea_rows, width))
     answered = lax.all_to_all(
         answers.reshape(targets, CAPACITY * sea_fields, width), SECTION, 0, 0, tiled=True
     )
@@ -840,7 +865,7 @@
     halos = (north, south, west, east, far_north, far_south)
     halos += (near_first, near_last, first_cols, last_cols)
     atmos_next = both_steps(0, answers)(state, *halos, atmos_diffusion)
-    answered, atmos_next = lax.optimization_barrier((answered, atmos_next))
+    answered, atmos_next, ocean_next = lax.optimization_barrier((answered, atmos_next, ocean_next))
 
     replies = call(
         functools.partial(reply_kernel, sea_fields),

time: 71.9 us -> 71.2 us (level)
  Pallas kernels: 24.3 us -> 22.9 us
  waiting for transfers between devices: 9.21 us -> 10.1 us
    pallas_call x14 -> x15, Pallas kernels: 24.3 us -> 22.9 us  [call(): return lambda *arguments: run(*arguments, *after)]
    all_to_all x1, waiting for transfers between devices: 2.25 us -> 2.98 us  [on_device(): lax.all_to_all(replies.reshape(targets, CAPACITY * sea_fields, width), SE...]
  transfers between devices with their start and end apart: 10 -> 10, of which waited for: 6 -> 6; matrix products, arithmetic and copies ran while one was open for 0% -> 0% of each run, Pallas kernels for 21% -> 20%
where the time goes in v4:
time: 71.2 us; the launch traced here: 70.7 us
  starting transfers between devices  23.5 us (33%)
  Pallas kernels  22.9 us (32%)
  blocking collectives  13 us (18%)
  waiting for transfers between devices  10.1 us (14%)
  between operations  1.05 us (1%)
    pallas_call x15, Pallas kernels, call(): return lambda *arguments: run(*arguments, *after)  22.9 us
    all_to_all x1, blocking collectives, on_device(): lax.all_to_all(pieces.reshape(targets, CAPACITY * PIECE_ROWS, width), SEC...  13 us
    ppermute x7, starting transfers between devices, shifted(): return lax.ppermute(block, axis, route)  11.4 us
    all_to_all x1, starting transfers between devices, on_device(): lax.all_to_all(answers.reshape(targets, CAPACITY * sea_fields, width), SE...  5.2 us
    ppermute x7, waiting for transfers between devices, shifted(): return lax.ppermute(block, axis, route)  4.43 us
    all_to_all x1, starting transfers between devices, on_device(): lax.all_to_all(replies.reshape(targets, CAPACITY * sea_fields, width), SE...  4.32 us
    all_to_all x1, waiting for transfers between devices, on_device(): lax.all_to_all(replies.reshape(targets, CAPACITY * sea_fields, width), SE...  2.98 us
    all_to_all x1, waiting for transfers between devices, on_device(): lax.all_to_all(answers.reshape(targets, CAPACITY * sea_fields, width), SE...  2.73 us
  transfers between devices with their start and end apart: 10, of which 6 were waited for; matrix products, arithmetic and copies ran while one was open for 0% of the time, Pallas kernels for 20%

profile of v4, /device:TPU:0, one launch (start us, length us, event | category | flops | bytes accessed | tf_op | source)
XLA Modules:
  0.0 70.7 jit_solution(10599113657946474010)
XLA Ops:
  0.7 3.2 %edges.1 = (f32[248,128]{1,0:T(8,128)}, f32[248,128]{1,0:T(8,128)}, f32[216,128]{1,0:T(8,128)}, f32[216,128]{1,0:T(8,128)}, f32[88,128]{1,0:T(8,128)}, /*index=5*/f32[88,128]{1,0:T(8,128)}) custom-call(f32[3200,128]{1,0:T(8,128)} %bitcast.18, f32[2048,128]{1,0:T(8,128)} %bitcast.27, s32[64,128]{1,0:T(8,128)} %refs_2_.5), custom_call_target="tpu_custom_call" | custom-call | bytes 1000000 | tf_op jit(solution)/shard_map/edges/pallas_call | solution.py:688
  4.0 3.1 %collective-permute-start = (f32[248,128]{1,0:T(8,128)}, f32[248,128]{1,0:T(8,128)S(1)}, u32[]{:S(2)}, u32[]{:S(2)}) collective-permute-start(f32[248,128]{1,0:T(8,128)} %get-tuple-element.30.refs_8_), channel_id=1, source_target_pairs={{28,0},{0,4},{4,8},{8,12},{12,16},{16,20},{20,24},{24,28},{29,1},{... | collective-permute-start | bytes 380936 | tf_op jit(solution)/shard_map/ppermute | solution.py:26
  7.0 1.5 %collective-permute-start.1 = (f32[248,128]{1,0:T(8,128)}, f32[248,128]{1,0:T(8,128)S(1)}, u32[]{:S(2)}, u32[]{:S(2)}) collective-permute-start(f32[248,128]{1,0:T(8,128)} %get-tuple-element.31.refs_7_), channel_id=1, source_target_pairs={{4,0},{8,4},{12,8},{16,12},{20,16},{24,20},{28,24},{0,28},{5,1},{9... | collective-permute-start | bytes 380936 | tf_op jit(solution)/shard_map/ppermute | solution.py:26
  8.6 1.9 %collective-permute-start.2 = (f32[88,128]{1,0:T(8,128)}, f32[88,128]{1,0:T(8,128)S(1)}, u32[]{:S(2)}, u32[]{:S(2)}) collective-permute-start(f32[88,128]{1,0:T(8,128)} %get-tuple-element.32.refs_10_), channel_id=1, source_target_pairs={{3,0},{0,1},{1,2},{2,3},{7,4},{4,5},{5,6},{6,7},{11,8},{8,9},{9,10... | collective-permute-start | bytes 135176 | tf_op jit(solution)/shard_map/ppermute | solution.py:26
  10.5 1.0 %collective-permute-start.3 = (f32[88,128]{1,0:T(8,128)}, f32[88,128]{1,0:T(8,128)S(1)}, u32[]{:S(2)}, u32[]{:S(2)}) collective-permute-start(f32[88,128]{1,0:T(8,128)} %get-tuple-element.33.refs_9_), channel_id=1, source_target_pairs={{1,0},{2,1},{3,2},{0,3},{5,4},{6,5},{7,6},{4,7},{9,8},{10,9},{11,1... | collective-permute-start | bytes 135176 | tf_op jit(solution)/shard_map/ppermute | solution.py:26
  12.8 1.1 %collective-permute-done.2.refs_3_.refs_2_.refs_4_ = f32[88,128]{1,0:T(8,128)S(1)} collective-permute-done((f32[88,128]{1,0:T(8,128)}, f32[88,128]{1,0:T(8,128)S(1)}, u32[]{:S(2)}, u32[]{:S(2)}) %collective-permute-start.2) | collective-permute-done | bytes 45088 | tf_op jit(solution)/shard_map/ppermute | solution.py:26
  13.9 1.0 %collective-permute-done.3.refs_4_.refs_3_.refs_5_ = f32[88,128]{1,0:T(8,128)S(1)} collective-permute-done((f32[88,128]{1,0:T(8,128)}, f32[88,128]{1,0:T(8,128)S(1)}, u32[]{:S(2)}, u32[]{:S(2)}) %collective-permute-start.3) | collective-permute-done | bytes 45088 | tf_op jit(solution)/shard_map/ppermute | solution.py:26
  15.6 13.0 %all_to_all.20 = f32[16,16,128]{2,1,0:T(8,128)S(1)} all-to-all(f32[16,16,128]{2,1,0:T(8,128)S(1)} %bitcast.21), channel_id=1, replica_groups=mesh['comp'=2,'gx'=4,'gy'=4] {'gx','gy'}, dimensions={0} | all-to-all | bytes 262144 | tf_op jit(solution)/shard_map/all_to_all | solution.py:782
  28.6 1.3 %fluxes.1 = (f32[256,128]{1,0:T(8,128)}, f32[32,128]{1,0:T(8,128)S(1)}, f32[32,128]{1,0:T(8,128)S(1)}) custom-call(f32[256,128]{1,0:T(8,128)S(1)} %bitcast.22, f32[16,128,128]{2,1,0:T(8,128)S(1)} %copy-done.1, f32[32,128]{1,0:T(8,128)S(1)} %get-tuple-element.42.refs_2_), custom_call_target="tpu_custom_call" | custom-call | bytes 1000000 | tf_op jit(solution)/shard_map/fluxes/pallas_call | solution.py:688
  30.0 2.6 %all-to-all-start.1 = ((f32[32,8,128]{2,1,0:T(8,128)}), f32[32,8,128]{2,1,0:T(8,128)S(1)}, u32[]{:S(2)}, u32[]{:S(2)}) async-start(f32[32,8,128]{2,1,0:T(8,128)} %bitcast.9), calls=%async_computation.1 | async-start | bytes 262144 | tf_op jit(solution)/shard_map/all_to_all | solution.py:796
  32.6 1.7 %collective-permute-start.4 = (f32[216,128]{1,0:T(8,128)S(1)}, f32[216,128]{1,0:T(8,128)S(1)}, u32[]{:S(2)}, u32[]{:S(2)}) collective-permute-start(f32[216,128]{1,0:T(8,128)S(1)} %get-tuple-element.44), channel_id=1, source_target_pairs={{28,0},{0,4},{4,8},{8,12},{12,16},{16,20},{20,24},{24,28},{29,1},{... | collective-permute-start | bytes 331784 | tf_op jit(solution)/shard_map/ppermute | solution.py:26
  34.3 1.9 %collective-permute-start.5 = (f32[216,128]{1,0:T(8,128)S(1)}, f32[216,128]{1,0:T(8,128)S(1)}, u32[]{:S(2)}, u32[]{:S(2)}) collective-permute-start(f32[216,128]{1,0:T(8,128)S(1)} %get-tuple-element.45), channel_id=1, source_target_pairs={{4,0},{8,4},{12,8},{16,12},{20,16},{24,20},{28,24},{0,28},{5,1},{9... | collective-permute-start | bytes 331784 | tf_op jit(solution)/shard_map/ppermute | solution.py:26
  36.5 3.9 %sea_base.1 = (f32[2048,128]{1,0:T(8,128)}, f32[256,128]{1,0:T(8,128)S(1)}) custom-call(f32[2048,128]{1,0:T(8,128)} %bitcast.28, s32[64,128]{1,0:T(8,128)S(1)} %copy-done.6, f32[248,128]{1,0:T(8,128)S(1)} %collective-permute-done.refs_1_.refs_2_, f32[248,128]{1,0:T(8,128)S(1)} %collective-permute-done.1.refs_2_.refs_3_, ...), custom_call_target="tpu_custom_call" | custom-call | bytes 1000000000 | tf_op jit(solution)/shard_map/sea_base/pallas_call | solution.py:688
  40.4 1.0 %collective-permute-done.4.refs_6_.refs_5_ = f32[216,128]{1,0:T(8,128)S(1)} collective-permute-done((f32[216,128]{1,0:T(8,128)S(1)}, f32[216,128]{1,0:T(8,128)S(1)}, u32[]{:S(2)}, u32[]{:S(2)}) %collective-permute-start.4) | collective-permute-done | bytes 110624 | tf_op jit(solution)/shard_map/ppermute | solution.py:26
  41.4 1.3 %collective-permute-done.5.refs_7_.refs_6_ = f32[216,128]{1,0:T(8,128)S(1)} collective-permute-done((f32[216,128]{1,0:T(8,128)S(1)}, f32[216,128]{1,0:T(8,128)S(1)}, u32[]{:S(2)}, u32[]{:S(2)}) %collective-permute-start.5) | collective-permute-done | bytes 110624 | tf_op jit(solution)/shard_map/ppermute | solution.py:26
  42.7 1.1 %sea_top.1 = (f32[256,128]{1,0:T(8,128)S(1)}, f32[128,128]{1,0:T(8,128)}) custom-call(f32[256,128]{1,0:T(8,128)S(1)} %bitcast.23, f32[256,128]{1,0:T(8,128)S(1)} %get-tuple-element.46.refs_1_, s32[64,128]{1,0:T(8,128)S(1)} %copy-done.6, f32[32,128]{1,0:T(8,128)S(1)} %get-tuple-element.47.refs_3_, f32[32,128]{1,0:T(8,128)S(1)} %collective-permute-done.6.refs_4_, ...), custom_call_target="tpu_custom_call" | custom-call | bytes 1000000 | tf_op jit(solution)/shard_map/sea_top/pallas_call | solution.py:688
  43.8 5.2 %all-to-all-start.2 = ((f32[16,8,128]{2,1,0:T(8,128)}), f32[16,8,128]{2,1,0:T(8,128)S(1)}, u32[]{:S(2)}, u32[]{:S(2)}) async-start(f32[16,8,128]{2,1,0:T(8,128)} %bitcast.11), calls=%async_computation.2 | async-start | bytes 131072 | tf_op jit(solution)/shard_map/all_to_all | solution.py:845
  49.7 4.0 %steps_a.1.refs_12_ = f32[3200,128]{1,0:T(8,128)} custom-call(f32[3200,128]{1,0:T(8,128)} %bitcast.19, f32[248,128]{1,0:T(8,128)S(1)} %collective-permute-done.refs_1_.refs_2_, f32[248,128]{1,0:T(8,128)S(1)} %collective-permute-done.1.refs_2_.refs_3_, f32[88,128]{1,0:T(8,128)S(1)} %collective-permute-done.2.refs_3_.refs_2_.refs_4_, ...), custom_call_target="tpu_custom_call" | custom-call | bytes 1000000000 | tf_op jit(solution)/shard_map/steps_a/pallas_call | solution.py:688
  53.8 2.7 %all-to-all-done.2 = f32[16,8,128]{2,1,0:T(8,128)S(1)} async-done(((f32[16,8,128]{2,1,0:T(8,128)}), f32[16,8,128]{2,1,0:T(8,128)S(1)}, u32[]{:S(2)}, u32[]{:S(2)}) %all-to-all-start.2) | async-done | bytes 65568 | tf_op jit(solution)/shard_map/all_to_all | solution.py:845
  56.5 1.3 %replies.1.refs_13_ = f32[128,128]{1,0:T(8,128)} custom-call(f32[128,128]{1,0:T(8,128)S(1)} %bitcast.25, f32[16,128,128]{2,1,0:T(8,128)S(1)} %copy-done.1, f32[32,128]{1,0:T(8,128)S(1)} %copy-done.15, f32[32,128]{1,0:T(8,128)S(1)} %get-tuple-element.54.refs_3_), custom_call_target="tpu_custom_call" | custom-call | bytes 1000000 | tf_op jit(solution)/shard_map/replies/pallas_call | solution.py:688
  57.8 4.3 %all-to-all-start.3 = ((f32[16,8,128]{2,1,0:T(8,128)}), f32[16,8,128]{2,1,0:T(8,128)S(1)}, u32[]{:S(2)}, u32[]{:S(2)}) async-start(f32[16,8,128]{2,1,0:T(8,128)} %bitcast.15), calls=%async_computation.3 | async-start | bytes 131072 | tf_op jit(solution)/shard_map/all_to_all | solution.py:877
  62.5 4.2 %steps_b.1 = f32[3200,128]{1,0:T(8,128)} custom-call(f32[3200,128]{1,0:T(8,128)} %bitcast.20, f32[248,128]{1,0:T(8,128)S(1)} %collective-permute-done.refs_1_.refs_2_, f32[248,128]{1,0:T(8,128)S(1)} %collective-permute-done.1.refs_2_.refs_3_, f32[88,128]{1,0:T(8,128)S(1)} %collective-permute-done.2.refs_3_.refs_2_.refs_4_, ...), custom_call_target="tpu_custom_call", output_to_operand_aliasing={{}: (12, {})} | custom-call | bytes 1000000000 | tf_op jit(solution)/shard_map/steps_b/pallas_call | solution.py:688
  66.7 3.0 %all-to-all-done.3 = f32[16,8,128]{2,1,0:T(8,128)S(1)} async-done(((f32[16,8,128]{2,1,0:T(8,128)}), f32[16,8,128]{2,1,0:T(8,128)S(1)}, u32[]{:S(2)}, u32[]{:S(2)}) %all-to-all-start.3) | async-done | bytes 65568 | tf_op jit(solution)/shard_map/all_to_all | solution.py:877
  69.7 1.1 %surface.1 = f32[64,128]{1,0:T(8,128)} custom-call(f32[128,128]{1,0:T(8,128)S(1)} %bitcast.24, bf16[16,256,128]{2,1,0:T(8,128)(2,1)S(1)} %surface_weights.1.refs_1_, f32[32,128]{1,0:T(8,128)S(1)} %copy-done.13), custom_call_target="tpu_custom_call" | custom-call | bytes 1000000 | tf_op jit(solution)/shard_map/surface/pallas_call | solution.py:688
  (61 shorter events, 3.2 us)
Async XLA Ops:
  0.6 10.9 %copy-start.20 = (s32[16]{0:T(128)S(1)}, s32[16]{0:T(128)}, u32[]{:S(2)}) copy-start(s32[16]{0:T(128)} %param.18) | copy-start | bytes 196
  0.6 10.9 %copy-start.21 = (s32[16,1]{0,1:T(1,128)S(1)}, s32[16,1]{0,1:T(1,128)}, u32[]{:S(2)}) copy-start(s32[16,1]{0,1:T(1,128)} %param.17) | copy-start | bytes 196
  0.7 10.9 %copy-start.22 = (s32[16]{0:T(128)S(1)}, s32[16]{0:T(128)}, u32[]{:S(2)}) copy-start(s32[16]{0:T(128)} %param.15) | copy-start | bytes 196
  0.7 10.9 %copy-start.23 = (s32[16,1]{0,1:T(1,128)S(1)}, s32[16,1]{0,1:T(1,128)}, u32[]{:S(2)}) copy-start(s32[16,1]{0,1:T(1,128)} %param.14) | copy-start | bytes 196
  0.7 10.9 %copy-start.2 = (f32[16,128,128]{2,1,0:T(8,128)S(1)}, f32[16,128,128]{2,1,0:T(8,128)}, u32[]{:S(2)}) copy-start(f32[16,128,128]{2,1,0:T(8,128)} %refs_0_.2) | copy-start | bytes 3145732
  4.0 11.0 %collective-permute-start = (f32[248,128]{1,0:T(8,128)}, f32[248,128]{1,0:T(8,128)S(1)}, u32[]{:S(2)}, u32[]{:S(2)}) collective-permute-start(f32[248,128]{1,0:T(8,128)} %get-tuple-element.30.refs_8_), channel_id=1, source_target_pairs={{28,0},{0,4},{4,8},{8,12},{12,16},{16,20},{20,24},{24,28},{29,1},{... | collective-permute-start | bytes 380936 | tf_op jit(solution)/shard_map/ppermute | solution.py:26
  7.0 7.9 %collective-permute-start.1 = (f32[248,128]{1,0:T(8,128)}, f32[248,128]{1,0:T(8,128)S(1)}, u32[]{:S(2)}, u32[]{:S(2)}) collective-permute-start(f32[248,128]{1,0:T(8,128)} %get-tuple-element.31.refs_7_), channel_id=1, source_target_pairs={{4,0},{8,4},{12,8},{16,12},{20,16},{24,20},{28,24},{0,28},{5,1},{9... | collective-permute-start | bytes 380936 | tf_op jit(solution)/shard_map/ppermute | solution.py:26
  8.6 5.3 %collective-permute-start.2 = (f32[88,128]{1,0:T(8,128)}, f32[88,128]{1,0:T(8,128)S(1)}, u32[]{:S(2)}, u32[]{:S(2)}) collective-permute-start(f32[88,128]{1,0:T(8,128)} %get-tuple-element.32.refs_10_), channel_id=1, source_target_pairs={{3,0},{0,1},{1,2},{2,3},{7,4},{4,5},{5,6},{6,7},{11,8},{8,9},{9,10... | collective-permute-start | bytes 135176 | tf_op jit(solution)/shard_map/ppermute | solution.py:26
  10.5 4.4 %collective-permute-start.3 = (f32[88,128]{1,0:T(8,128)}, f32[88,128]{1,0:T(8,128)S(1)}, u32[]{:S(2)}, u32[]{:S(2)}) collective-permute-start(f32[88,128]{1,0:T(8,128)} %get-tuple-element.33.refs_9_), channel_id=1, source_target_pairs={{1,0},{2,1},{3,2},{0,3},{5,4},{6,5},{7,6},{4,7},{9,8},{10,9},{11,1... | collective-permute-start | bytes 135176 | tf_op jit(solution)/shard_map/ppermute | solution.py:26
  12.6 16.0 %copy-start.14 = (f32[32,128]{1,0:T(8,128)}, f32[32,128]{1,0:T(8,128)S(1)}, u32[]{:S(2)}) copy-start(f32[32,128]{1,0:T(8,128)S(1)} %get-tuple-element.42.refs_2_) | copy-start | bytes 49156
  12.6 16.0 %copy-start.1 = (f32[16,128,128]{2,1,0:T(8,128)S(1)}, f32[16,128,128]{2,1,0:T(8,128)}, u32[]{:S(2)}) copy-start(f32[16,128,128]{2,1,0:T(8,128)} %refs_1_.5) | copy-start | bytes 3145732
  15.0 17.6 %copy-start.10 = (f32[216,128]{1,0:T(8,128)S(1)}, f32[216,128]{1,0:T(8,128)}, u32[]{:S(2)}) copy-start(f32[216,128]{1,0:T(8,128)} %get-tuple-element.34.refs_0_) | copy-start | bytes 331780
  15.0 17.6 %copy-start.11 = (f32[216,128]{1,0:T(8,128)S(1)}, f32[216,128]{1,0:T(8,128)}, u32[]{:S(2)}) copy-start(f32[216,128]{1,0:T(8,128)} %get-tuple-element.35.refs_1_) | copy-start | bytes 331780
  15.0 21.5 %copy-start.6 = (s32[64,128]{1,0:T(8,128)S(1)}, s32[64,128]{1,0:T(8,128)}, u32[]{:S(2)}) copy-start(s32[64,128]{1,0:T(8,128)} %refs_2_.5) | copy-start | bytes 98308
  15.0 21.5 %copy-start.19 = (f32[4]{0:T(128)S(1)}, f32[4]{0:T(128)}, u32[]{:S(2)}) copy-start(f32[4]{0:T(128)} %refs_6_.1) | copy-start | bytes 52
  28.6 14.1 %copy-start.18 = (f32[8,128]{1,0:T(8,128)S(1)}, f32[8,128]{1,0:T(8,128)}, u32[]{:S(2)}) copy-start(f32[8,128]{1,0:T(8,128)} %copy-done.17) | copy-start | bytes 12292
  30.0 12.7 %all-to-all-start.1 = ((f32[32,8,128]{2,1,0:T(8,128)}), f32[32,8,128]{2,1,0:T(8,128)S(1)}, u32[]{:S(2)}, u32[]{:S(2)}) async-start(f32[32,8,128]{2,1,0:T(8,128)} %bitcast.9), calls=%async_computation.1 | async-start | bytes 262144 | tf_op jit(solution)/shard_map/all_to_all | solution.py:796
  32.6 8.8 %collective-permute-start.4 = (f32[216,128]{1,0:T(8,128)S(1)}, f32[216,128]{1,0:T(8,128)S(1)}, u32[]{:S(2)}, u32[]{:S(2)}) collective-permute-start(f32[216,128]{1,0:T(8,128)S(1)} %get-tuple-element.44), channel_id=1, source_target_pairs={{28,0},{0,4},{4,8},{8,12},{12,16},{16,20},{20,24},{24,28},{29,1},{... | collective-permute-start | bytes 331784 | tf_op jit(solution)/shard_map/ppermute | solution.py:26
  34.3 8.4 %collective-permute-start.5 = (f32[216,128]{1,0:T(8,128)S(1)}, f32[216,128]{1,0:T(8,128)S(1)}, u32[]{:S(2)}, u32[]{:S(2)}) collective-permute-start(f32[216,128]{1,0:T(8,128)S(1)} %get-tuple-element.45), channel_id=1, source_target_pairs={{4,0},{8,4},{12,8},{16,12},{20,16},{24,20},{28,24},{0,28},{5,1},{9... | collective-permute-start | bytes 331784 | tf_op jit(solution)/shard_map/ppermute | solution.py:26
  36.2 4.2 %collective-permute-start.6 = (f32[32,128]{1,0:T(8,128)S(1)}, f32[32,128]{1,0:T(8,128)S(1)}, u32[]{:S(2)}, u32[]{:S(2)}) collective-permute-start(f32[32,128]{1,0:T(8,128)S(1)} %get-tuple-element.47.refs_3_), channel_id=1, source_target_pairs={{16,0},{0,16},{17,1},{1,17},{18,2},{2,18},{19,3},{3,19},{20,4},{4,... | collective-permute-start | bytes 49160 | tf_op jit(solution)/shard_map/ppermute | solution.py:26
  40.3 9.3 %copy-start.4 = (f32[248,128]{1,0:T(8,128)S(1)}, f32[248,128]{1,0:T(8,128)}, u32[]{:S(2)}) copy-start(f32[248,128]{1,0:T(8,128)} %get-tuple-element.31.refs_7_) | copy-start | bytes 380932
  40.3 9.3 %copy-start.5 = (f32[248,128]{1,0:T(8,128)S(1)}, f32[248,128]{1,0:T(8,128)}, u32[]{:S(2)}) copy-start(f32[248,128]{1,0:T(8,128)} %get-tuple-element.30.refs_8_) | copy-start | bytes 380932
  43.8 12.7 %all-to-all-start.2 = ((f32[16,8,128]{2,1,0:T(8,128)}), f32[16,8,128]{2,1,0:T(8,128)S(1)}, u32[]{:S(2)}, u32[]{:S(2)}) async-start(f32[16,8,128]{2,1,0:T(8,128)} %bitcast.11), calls=%async_computation.2 | async-start | bytes 131072 | tf_op jit(solution)/shard_map/all_to_all | solution.py:845
  57.8 11.9 %all-to-all-start.3 = ((f32[16,8,128]{2,1,0:T(8,128)}), f32[16,8,128]{2,1,0:T(8,128)S(1)}, u32[]{:S(2)}, u32[]{:S(2)}) async-start(f32[16,8,128]{2,1,0:T(8,128)} %bitcast.15), calls=%async_computation.3 | async-start | bytes 131072 | tf_op jit(solution)/shard_map/all_to_all | solution.py:877
  (10 other events, 68.0 us)

commit v5 on v4

--- a/solution.py
+++ b/solution.py
@@ -15,7 +15,7 @@
 CAPACITY = 2
 PIECE_ROWS = 8
 VMEM_LIMIT = 8 * 1024 * 1024
-EDGES_LIMIT = 60 * 1024 * 1024
+EDGES_LIMIT = 52 * 1024 * 1024
 SEA_LIMIT = 53 * 1024 * 1024
 STEPS_LIMIT = 53 * 1024 * 1024
 
@@ -112,12 +112,12 @@
         self.sea_blocks, self.sea_rows = sea_blocks, sea_rows
         self.half = fields // 2
         self.part = self.half * levels
-        self.part_rows = -(-self.part // 8) * 8
-        self.atmos_rows = 2 * self.part_rows
+        self.ring_rows = -(-self.part // 8) * 8
+        self.atmos_rows = 2 * self.part
         self.wet_row = self.atmos_rows + sea_blocks
         self.near_rows = -(-(self.wet_row + 1) // 8) * 8
         self.corner_row = self.atmos_rows
-        self.far_rows = self.atmos_rows + 8
+        self.far_rows = -(-(self.atmos_rows + 4) // 8) * 8
         self.sea_tiles = sea_blocks * sea_rows // width
         self.sea_cols = 4 * rows
         self.sea_col_rows = -(-(self.sea_tiles + 1) // 8) * 8
@@ -137,33 +137,14 @@
 
 
 def edges_kernel(
-    at,
-    state_far,
-    ocean_far,
-    wet_far,
-    near_first,
-    near_last,
-    far_first,
-    far_last,
-    first,
-    last,
-    state,
-    ocean,
-    wet,
-    arrivals,
+    at, state_far, near_first, near_last, far_first, far_last, first, last, state, arrivals
 ):
     rows, part, width = at.rows, at.part, at.width
     field_rows = at.levels * rows
-    sea_parts = 4
     copies = [
         chunk(state_far, state, field, field_rows, arrivals.at[field])
         for field in range(at.fields)
     ]
-    copies += [
-        chunk(ocean_far, ocean, field, ocean.shape[0] // sea_parts, arrivals.at[at.fields + field])
-        for field in range(sea_parts)
-    ]
-    copies.append(pltpu.make_async_copy(wet_far, wet, arrivals.at[at.fields + sea_parts]))
     for copy in copies:
         copy.start()
     for out in (near_first, near_last, far_first, far_last):
@@ -175,7 +156,7 @@
             copies[field].wait()
         for row in range(rows):
             lines = state[pl.ds(half * part * rows + row, part, stride=rows), :]
-            held = pl.ds(half * at.part_rows, part)
+            held = pl.ds(half * at.part, part)
             if row < 2:
                 (near_first, far_first)[row][held, :] = lines
             if row >= rows - 2:
@@ -186,9 +167,13 @@
             first[pl.ds(far, 1), :] = turned[1:2, :]
             last[pl.ds(near, 1), :] = turned[width - 1 : width, :]
             last[pl.ds(far, 1), :] = turned[width - 2 : width - 1, :]
-    for copy in copies[at.fields :]:
-        copy.wait()
-    for out, sea_row in ((near_first, 0), (near_last, at.sea_rows - 1)):
+
+
+def sea_edges_kernel(at, ocean, wet, near_first, near_last, first, last, *outs):
+    width = at.width
+    for out, rows in zip(outs, (near_first, near_last, first, last)):
+        out[...] = rows[...]
+    for out, sea_row in ((outs[0], 0), (outs[1], at.sea_rows - 1)):
         out[pl.ds(at.atmos_rows, at.sea_blocks), :] = ocean[
             pl.ds(sea_row, at.sea_blocks, stride=at.sea_rows), :
         ]
@@ -199,8 +184,8 @@
         else:
             lines = squared(wet[...].astype(F32))
         turned = jnp.transpose(lines)
-        first[pl.ds(at.sea_cols + tile, 1), :] = turned[0:1, :]
-        last[pl.ds(at.sea_cols + tile, 1), :] = turned[width - 1 : width, :]
+        outs[2][pl.ds(at.sea_cols + tile, 1), :] = turned[0:1, :]
+        outs[3][pl.ds(at.sea_cols + tile, 1), :] = turned[width - 1 : width, :]
 
 
 def corners_kernel(at, far_first, far_last, west, east, to_north, to_south):
@@ -226,8 +211,8 @@
     north, south, west, east, far_north, far_south = halos
     near_first, near_last, first, last = edges
     rows, width = at.rows, at.width
-    shape = (at.part_rows, width)
-    held = pl.ds(part * at.part_rows, shape[0])
+    shape = (at.ring_rows, width)
+    held = pl.ds(part * at.part, shape[0])
     lines, lanes = grid_index(shape)
     numbers, is_first, is_last = spread(at, diffusion, part, lines)
     for out, outside, further, own, is_north in (
@@ -357,7 +342,7 @@
         number = diffusion[whole + field]
         coming(field).wait()
         field_step(
-            at, field, state, middle, north, south, part * at.part_rows, outer, number
+            at, field, state, middle, north, south, part * at.part, outer, number
         )
         field_step(at, field, middle, out, ring[0], ring[1], 0, inner, number)
         going(field).start()
@@ -504,7 +489,7 @@
         part = field // at.half
         held = pl.ds(part * rows, rows)
         lane = (field % at.half) * levels + levels - 1
-        line = pl.ds(part * at.part_rows + lane, 1)
+        line = pl.ds(part * at.part + lane, 1)
         outside = (
             jnp.where(lines == 0, north[line, :], 0.0)
             + jnp.where(lines == rows - 1, south[line, :], 0.0)
@@ -723,7 +708,6 @@
 
     state_copy = pltpu.VMEM((blocks * rows, width), F32)
     ocean_copy = pltpu.VMEM((sea_blocks * sea_rows, width), F32)
-    wet_copy = pltpu.VMEM((sea_rows, width), jnp.int32)
     ocean_flags = pltpu.SemaphoreType.DMA((sea_fields,))
     near_first, near_last, far_first, far_last, first_cols, last_cols = call(
         functools.partial(edges_kernel, at),
@@ -731,10 +715,16 @@
         (array(at.near_rows, width),) * 2
         + (array(at.far_rows, width),) * 2
         + (array(at.col_rows, width),) * 2,
-        [ANY] * 3,
-        [state_copy, ocean_copy, wet_copy, pltpu.SemaphoreType.DMA((fields + 5,))],
+        [ANY],
+        [state_copy, pltpu.SemaphoreType.DMA((fields,))],
         limit=EDGES_LIMIT,
-    )(state, ocean, wet_mask)
+    )(state)
+    near_first, near_last, first_cols, last_cols = call(
+        functools.partial(sea_edges_kernel, at),
+        "sea_edges",
+        (array(at.near_rows, width),) * 2 + (array(at.col_rows, width),) * 2,
+        [VMEM] * 6,
+    )(ocean, wet_mask, near_first, near_last, first_cols, last_cols)
     north = shifted(near_last, ring, 1)
     south = shifted(near_first, ring, -1)
     west = shifted(last_cols, "gy", 1)
@@ -852,7 +842,7 @@
             array(blocks * rows, width),
             [ANY] + [VMEM] * 10 + [SMEM] + [ANY] * part,
             [pltpu.VMEM((at.part * rows, width), F32)] * 3
-            + [pltpu.VMEM((at.part_rows, width), F32)] * 2
+            + [pltpu.VMEM((at.ring_rows, width), F32)] * 2
             + [pltpu.VMEM((rows, width), F32)] * 2
             + [pltpu.SemaphoreType.DMA((at.half,))] * 2,
             after=(before,),

time: 71.2 us -> 69.9 us (0.982)
  Pallas kernels: 22.9 us -> 22.1 us
    pallas_call x15 -> x16, Pallas kernels: 22.9 us -> 22.1 us  [call(): return lambda *arguments: run(*arguments, *after)]
  transfers between devices with their start and end apart: 10 -> 10, of which waited for: 6 -> 6; matrix products, arithmetic and copies ran while one was open for 0% -> 0% of each run, Pallas kernels for 20% -> 21%
where the time goes in v5:
time: 69.9 us; the launch traced here: 69.5 us
  starting transfers between devices  23.5 us (34%)
  Pallas kernels  22.1 us (32%)
  blocking collectives  12.9 us (18%)
  waiting for transfers between devices  9.82 us (14%)
  between operations  1.04 us (1%)
    pallas_call x16, Pallas kernels, call(): return lambda *arguments: run(*arguments, *after)  22.1 us
    all_to_all x1, blocking collectives, on_device(): lax.all_to_all(pieces.reshape(targets, CAPACITY * PIECE_ROWS, width), SEC...  12.9 us
    ppermute x7, starting transfers between devices, shifted(): return lax.ppermute(block, axis, route)  11.4 us
    all_to_all x1, starting transfers between devices, on_device(): lax.all_to_all(answers.reshape(targets, CAPACITY * sea_fields, width), SE...  5.2 us
    all_to_all x1, starting transfers between devices, on_device(): lax.all_to_all(replies.reshape(targets, CAPACITY * sea_fields, width), SE...  4.31 us
    ppermute x7, waiting for transfers between devices, shifted(): return lax.ppermute(block, axis, route)  4.08 us
    all_to_all x1, waiting for transfers between devices, on_device(): lax.all_to_all(replies.reshape(targets, CAPACITY * sea_fields, width), SE...  2.99 us
    all_to_all x1, waiting for transfers between devices, on_device(): lax.all_to_all(answers.reshape(targets, CAPACITY * sea_fields, width), SE...  2.75 us
  transfers between devices with their start and end apart: 10, of which 6 were waited for; matrix products, arithmetic and copies ran while one was open for 0% of the time, Pallas kernels for 21%

profile of v5, /device:TPU:0, one launch (start us, length us, event | category | flops | bytes accessed | tf_op | source)
XLA Modules:
  0.0 69.5 jit_solution(3699982941447644354)
XLA Ops:
  0.7 2.2 %edges.1 = (f32[240,128]{1,0:T(8,128)S(1)}, f32[240,128]{1,0:T(8,128)S(1)}, f32[208,128]{1,0:T(8,128)S(1)}, f32[208,128]{1,0:T(8,128)S(1)}, f32[88,128]{1,0:T(8,128)S(1)}, /*index=5*/f32[88,128]{1,0:T(8,128)S(1)}) custom-call(f32[3200,128]{1,0:T(8,128)} %bitcast.18), custom_call_target="tpu_custom_call" | custom-call | bytes 1000000 | tf_op jit(solution)/shard_map/edges/pallas_call | solution.py:673
  3.3 3.1 %collective-permute-start = (f32[240,128]{1,0:T(8,128)S(1)}, f32[240,128]{1,0:T(8,128)S(1)}, u32[]{:S(2)}, u32[]{:S(2)}) collective-permute-start(f32[240,128]{1,0:T(8,128)S(1)} %get-tuple-element.38.refs_8_), channel_id=1, source_target_pairs={{28,0},{0,4},{4,8},{8,12},{12,16},{16,20},{20,24},{24,28},{29,1},{... | collective-permute-start | bytes 368648 | tf_op jit(solution)/shard_map/ppermute | solution.py:26
  6.4 1.5 %collective-permute-start.1 = (f32[240,128]{1,0:T(8,128)S(1)}, f32[240,128]{1,0:T(8,128)S(1)}, u32[]{:S(2)}, u32[]{:S(2)}) collective-permute-start(f32[240,128]{1,0:T(8,128)S(1)} %get-tuple-element.39.refs_7_), channel_id=1, source_target_pairs={{4,0},{8,4},{12,8},{16,12},{20,16},{24,20},{28,24},{0,28},{5,1},{9... | collective-permute-start | bytes 368648 | tf_op jit(solution)/shard_map/ppermute | solution.py:26
  7.9 1.9 %collective-permute-start.2 = (f32[88,128]{1,0:T(8,128)S(1)}, f32[88,128]{1,0:T(8,128)S(1)}, u32[]{:S(2)}, u32[]{:S(2)}) collective-permute-start(f32[88,128]{1,0:T(8,128)S(1)} %get-tuple-element.40.refs_10_), channel_id=1, source_target_pairs={{3,0},{0,1},{1,2},{2,3},{7,4},{4,5},{5,6},{6,7},{11,8},{8,9},{9,10... | collective-permute-start | bytes 135176 | tf_op jit(solution)/shard_map/ppermute | solution.py:26
  9.9 1.0 %collective-permute-start.3 = (f32[88,128]{1,0:T(8,128)S(1)}, f32[88,128]{1,0:T(8,128)S(1)}, u32[]{:S(2)}, u32[]{:S(2)}) collective-permute-start(f32[88,128]{1,0:T(8,128)S(1)} %get-tuple-element.41.refs_9_), channel_id=1, source_target_pairs={{1,0},{2,1},{3,2},{0,3},{5,4},{6,5},{7,6},{4,7},{9,8},{10,9},{11,1... | collective-permute-start | bytes 135176 | tf_op jit(solution)/shard_map/ppermute | solution.py:26
  11.0 0.9 %routes.1 = (f32[32,128]{1,0:T(8,128)S(1)}, f32[32,128]{1,0:T(8,128)S(1)}, f32[32,128]{1,0:T(8,128)S(1)}, f32[8,128]{1,0:T(8,128)S(1)}, f32[16,128]{1,0:T(8,128)S(1)}) custom-call(s32[4,16]{1,0:T(4,128)S(1)} %pad_add_fusion.refs_0_, s32[1]{0:T(128)} %bitcast.6.refs_1_, f32[10]{0:T(128)S(1)} %copy-done.16), custom_call_target="tpu_custom_call" | custom-call | bytes 1000000 | tf_op jit(solution)/shard_map/routes/pallas_call | solution.py:673
  13.1 1.0 %collective-permute-done.3.refs_4_.refs_3_.refs_5_ = f32[88,128]{1,0:T(8,128)S(1)} collective-permute-done((f32[88,128]{1,0:T(8,128)S(1)}, f32[88,128]{1,0:T(8,128)S(1)}, u32[]{:S(2)}, u32[]{:S(2)}) %collective-permute-start.3) | collective-permute-done | bytes 45088 | tf_op jit(solution)/shard_map/ppermute | solution.py:26
  14.7 12.9 %all_to_all.20 = f32[16,16,128]{2,1,0:T(8,128)S(1)} all-to-all(f32[16,16,128]{2,1,0:T(8,128)S(1)} %bitcast.23), channel_id=1, replica_groups=mesh['comp'=2,'gx'=4,'gy'=4] {'gx','gy'}, dimensions={0} | all-to-all | bytes 262144 | tf_op jit(solution)/shard_map/all_to_all | solution.py:772
  27.6 1.3 %fluxes.1 = (f32[256,128]{1,0:T(8,128)}, f32[32,128]{1,0:T(8,128)S(1)}, f32[32,128]{1,0:T(8,128)S(1)}) custom-call(f32[256,128]{1,0:T(8,128)S(1)} %bitcast.24, f32[16,128,128]{2,1,0:T(8,128)S(1)} %copy-done.1, f32[32,128]{1,0:T(8,128)S(1)} %get-tuple-element.50.refs_2_), custom_call_target="tpu_custom_call" | custom-call | bytes 1000000 | tf_op jit(solution)/shard_map/fluxes/pallas_call | solution.py:673
  28.9 2.6 %all-to-all-start.1 = ((f32[32,8,128]{2,1,0:T(8,128)}), f32[32,8,128]{2,1,0:T(8,128)S(1)}, u32[]{:S(2)}, u32[]{:S(2)}) async-start(f32[32,8,128]{2,1,0:T(8,128)} %bitcast.9), calls=%async_computation.1 | async-start | bytes 262144 | tf_op jit(solution)/shard_map/all_to_all | solution.py:786
  31.5 1.7 %collective-permute-start.4 = (f32[208,128]{1,0:T(8,128)S(1)}, f32[208,128]{1,0:T(8,128)S(1)}, u32[]{:S(2)}, u32[]{:S(2)}) collective-permute-start(f32[208,128]{1,0:T(8,128)S(1)} %get-tuple-element.52), channel_id=1, source_target_pairs={{28,0},{0,4},{4,8},{8,12},{12,16},{16,20},{20,24},{24,28},{29,1},{... | collective-permute-start | bytes 319496 | tf_op jit(solution)/shard_map/ppermute | solution.py:26
  33.3 1.9 %collective-permute-start.5 = (f32[208,128]{1,0:T(8,128)S(1)}, f32[208,128]{1,0:T(8,128)S(1)}, u32[]{:S(2)}, u32[]{:S(2)}) collective-permute-start(f32[208,128]{1,0:T(8,128)S(1)} %get-tuple-element.53), channel_id=1, source_target_pairs={{4,0},{8,4},{12,8},{16,12},{20,16},{24,20},{28,24},{0,28},{5,1},{9... | collective-permute-start | bytes 319496 | tf_op jit(solution)/shard_map/ppermute | solution.py:26
  35.4 3.9 %sea_base.1 = (f32[2048,128]{1,0:T(8,128)}, f32[256,128]{1,0:T(8,128)S(1)}) custom-call(f32[2048,128]{1,0:T(8,128)} %bitcast.21, s32[64,128]{1,0:T(8,128)S(1)} %copy-done.5, f32[240,128]{1,0:T(8,128)S(1)} %collective-permute-done.refs_1_.refs_2_, f32[240,128]{1,0:T(8,128)S(1)} %collective-permute-done.1.refs_2_.refs_3_, ...), custom_call_target="tpu_custom_call" | custom-call | bytes 1000000000 | tf_op jit(solution)/shard_map/sea_base/pallas_call | solution.py:673
  39.3 0.9 %collective-permute-done.4.refs_6_.refs_5_ = f32[208,128]{1,0:T(8,128)S(1)} collective-permute-done((f32[208,128]{1,0:T(8,128)S(1)}, f32[208,128]{1,0:T(8,128)S(1)}, u32[]{:S(2)}, u32[]{:S(2)}) %collective-permute-start.4) | collective-permute-done | bytes 106528 | tf_op jit(solution)/shard_map/ppermute | solution.py:26
  40.2 1.2 %collective-permute-done.5.refs_7_.refs_6_ = f32[208,128]{1,0:T(8,128)S(1)} collective-permute-done((f32[208,128]{1,0:T(8,128)S(1)}, f32[208,128]{1,0:T(8,128)S(1)}, u32[]{:S(2)}, u32[]{:S(2)}) %collective-permute-start.5) | collective-permute-done | bytes 106528 | tf_op jit(solution)/shard_map/ppermute | solution.py:26
  41.5 1.0 %sea_top.1 = (f32[256,128]{1,0:T(8,128)S(1)}, f32[128,128]{1,0:T(8,128)}) custom-call(f32[256,128]{1,0:T(8,128)S(1)} %bitcast.25, f32[256,128]{1,0:T(8,128)S(1)} %get-tuple-element.54.refs_1_, s32[64,128]{1,0:T(8,128)S(1)} %copy-done.5, f32[32,128]{1,0:T(8,128)S(1)} %get-tuple-element.55.refs_3_, f32[32,128]{1,0:T(8,128)S(1)} %collective-permute-done.6.refs_4_, ...), custom_call_target="tpu_custom_call" | custom-call | bytes 1000000 | tf_op jit(solution)/shard_map/sea_top/pallas_call | solution.py:673
  42.5 5.2 %all-to-all-start.2 = ((f32[16,8,128]{2,1,0:T(8,128)}), f32[16,8,128]{2,1,0:T(8,128)S(1)}, u32[]{:S(2)}, u32[]{:S(2)}) async-start(f32[16,8,128]{2,1,0:T(8,128)} %bitcast.11), calls=%async_computation.2 | async-start | bytes 131072 | tf_op jit(solution)/shard_map/all_to_all | solution.py:835
  48.4 4.0 %steps_a.1.refs_12_ = f32[3200,128]{1,0:T(8,128)} custom-call(f32[3200,128]{1,0:T(8,128)} %bitcast.19, f32[240,128]{1,0:T(8,128)S(1)} %collective-permute-done.refs_1_.refs_2_, f32[240,128]{1,0:T(8,128)S(1)} %collective-permute-done.1.refs_2_.refs_3_, f32[88,128]{1,0:T(8,128)S(1)} %collective-permute-done.2.refs_3_.refs_2_.refs_4_, ...), custom_call_target="tpu_custom_call" | custom-call | bytes 1000000000 | tf_op jit(solution)/shard_map/steps_a/pallas_call | solution.py:673
  52.5 2.7 %all-to-all-done.2 = f32[16,8,128]{2,1,0:T(8,128)S(1)} async-done(((f32[16,8,128]{2,1,0:T(8,128)}), f32[16,8,128]{2,1,0:T(8,128)S(1)}, u32[]{:S(2)}, u32[]{:S(2)}) %all-to-all-start.2) | async-done | bytes 65568 | tf_op jit(solution)/shard_map/all_to_all | solution.py:835
  55.3 1.3 %replies.1.refs_13_ = f32[128,128]{1,0:T(8,128)} custom-call(f32[128,128]{1,0:T(8,128)S(1)} %bitcast.27, f32[16,128,128]{2,1,0:T(8,128)S(1)} %copy-done.1, f32[32,128]{1,0:T(8,128)S(1)} %copy-done.15, f32[32,128]{1,0:T(8,128)S(1)} %get-tuple-element.62.refs_3_), custom_call_target="tpu_custom_call" | custom-call | bytes 1000000 | tf_op jit(solution)/shard_map/replies/pallas_call | solution.py:673
  56.6 4.3 %all-to-all-start.3 = ((f32[16,8,128]{2,1,0:T(8,128)}), f32[16,8,128]{2,1,0:T(8,128)S(1)}, u32[]{:S(2)}, u32[]{:S(2)}) async-start(f32[16,8,128]{2,1,0:T(8,128)} %bitcast.15), calls=%async_computation.3 | async-start | bytes 131072 | tf_op jit(solution)/shard_map/all_to_all | solution.py:867
  61.2 4.2 %steps_b.1 = f32[3200,128]{1,0:T(8,128)} custom-call(f32[3200,128]{1,0:T(8,128)} %bitcast.20, f32[240,128]{1,0:T(8,128)S(1)} %collective-permute-done.refs_1_.refs_2_, f32[240,128]{1,0:T(8,128)S(1)} %collective-permute-done.1.refs_2_.refs_3_, f32[88,128]{1,0:T(8,128)S(1)} %collective-permute-done.2.refs_3_.refs_2_.refs_4_, ...), custom_call_target="tpu_custom_call", output_to_operand_aliasing={{}: (12, {})} | custom-call | bytes 1000000000 | tf_op jit(solution)/shard_map/steps_b/pallas_call | solution.py:673
  65.4 3.0 %all-to-all-done.3 = f32[16,8,128]{2,1,0:T(8,128)S(1)} async-done(((f32[16,8,128]{2,1,0:T(8,128)}), f32[16,8,128]{2,1,0:T(8,128)S(1)}, u32[]{:S(2)}, u32[]{:S(2)}) %all-to-all-start.3) | async-done | bytes 65568 | tf_op jit(solution)/shard_map/all_to_all | solution.py:867
  68.4 1.1 %surface.1 = f32[64,128]{1,0:T(8,128)} custom-call(f32[128,128]{1,0:T(8,128)S(1)} %bitcast.26, bf16[16,256,128]{2,1,0:T(8,128)(2,1)S(1)} %surface_weights.1.refs_1_, f32[32,128]{1,0:T(8,128)S(1)} %get-tuple-element.48.refs_7_.refs_2_), custom_call_target="tpu_custom_call" | custom-call | bytes 1000000 | tf_op jit(solution)/shard_map/surface/pallas_call | solution.py:673
  (58 shorter events, 3.5 us)
Async XLA Ops:
  0.7 10.2 %copy-start.18 = (s32[16]{0:T(128)S(1)}, s32[16]{0:T(128)}, u32[]{:S(2)}) copy-start(s32[16]{0:T(128)} %param.18) | copy-start | bytes 196
  0.7 10.2 %copy-start.19 = (s32[16,1]{0,1:T(1,128)S(1)}, s32[16,1]{0,1:T(1,128)}, u32[]{:S(2)}) copy-start(s32[16,1]{0,1:T(1,128)} %param.17) | copy-start | bytes 196
  0.7 10.2 %copy-start.20 = (s32[16]{0:T(128)S(1)}, s32[16]{0:T(128)}, u32[]{:S(2)}) copy-start(s32[16]{0:T(128)} %param.15) | copy-start | bytes 196
  0.7 10.2 %copy-start.21 = (s32[16,1]{0,1:T(1,128)S(1)}, s32[16,1]{0,1:T(1,128)}, u32[]{:S(2)}) copy-start(s32[16,1]{0,1:T(1,128)} %param.14) | copy-start | bytes 196
  0.7 10.2 %copy-start.3 = (f32[16,128,128]{2,1,0:T(8,128)S(1)}, f32[16,128,128]{2,1,0:T(8,128)}, u32[]{:S(2)}) copy-start(f32[16,128,128]{2,1,0:T(8,128)} %refs_0_.2) | copy-start | bytes 3145732
  2.9 9.1 %copy-start = (f32[10,20,16,128]{3,2,1,0:T(8,128)S(1)}, f32[10,20,16,128]{3,2,1,0:T(8,128)}, u32[]{:S(2)}) copy-start(f32[10,20,16,128]{3,2,1,0:T(8,128)} %refs_0_) | copy-start | bytes 4915204
  3.3 8.9 %copy-start.6 = (f32[88,128]{1,0:T(8,128)}, f32[88,128]{1,0:T(8,128)S(1)}, u32[]{:S(2)}) copy-start(f32[88,128]{1,0:T(8,128)S(1)} %get-tuple-element.41.refs_9_) | copy-start | bytes 135172
  3.3 8.9 %copy-start.9 = (f32[88,128]{1,0:T(8,128)}, f32[88,128]{1,0:T(8,128)S(1)}, u32[]{:S(2)}) copy-start(f32[88,128]{1,0:T(8,128)S(1)} %get-tuple-element.40.refs_10_) | copy-start | bytes 135172
  3.3 10.8 %collective-permute-start = (f32[240,128]{1,0:T(8,128)S(1)}, f32[240,128]{1,0:T(8,128)S(1)}, u32[]{:S(2)}, u32[]{:S(2)}) collective-permute-start(f32[240,128]{1,0:T(8,128)S(1)} %get-tuple-element.38.refs_8_), channel_id=1, source_target_pairs={{28,0},{0,4},{4,8},{8,12},{12,16},{16,20},{20,24},{24,28},{29,1},{... | collective-permute-start | bytes 368648 | tf_op jit(solution)/shard_map/ppermute | solution.py:26
  6.4 7.7 %collective-permute-start.1 = (f32[240,128]{1,0:T(8,128)S(1)}, f32[240,128]{1,0:T(8,128)S(1)}, u32[]{:S(2)}, u32[]{:S(2)}) collective-permute-start(f32[240,128]{1,0:T(8,128)S(1)} %get-tuple-element.39.refs_7_), channel_id=1, source_target_pairs={{4,0},{8,4},{12,8},{16,12},{20,16},{24,20},{28,24},{0,28},{5,1},{9... | collective-permute-start | bytes 368648 | tf_op jit(solution)/shard_map/ppermute | solution.py:26
  7.9 5.1 %collective-permute-start.2 = (f32[88,128]{1,0:T(8,128)S(1)}, f32[88,128]{1,0:T(8,128)S(1)}, u32[]{:S(2)}, u32[]{:S(2)}) collective-permute-start(f32[88,128]{1,0:T(8,128)S(1)} %get-tuple-element.40.refs_10_), channel_id=1, source_target_pairs={{3,0},{0,1},{1,2},{2,3},{7,4},{4,5},{5,6},{6,7},{11,8},{8,9},{9,10... | collective-permute-start | bytes 135176 | tf_op jit(solution)/shard_map/ppermute | solution.py:26
  9.9 4.2 %collective-permute-start.3 = (f32[88,128]{1,0:T(8,128)S(1)}, f32[88,128]{1,0:T(8,128)S(1)}, u32[]{:S(2)}, u32[]{:S(2)}) collective-permute-start(f32[88,128]{1,0:T(8,128)S(1)} %get-tuple-element.41.refs_9_), channel_id=1, source_target_pairs={{1,0},{2,1},{3,2},{0,3},{5,4},{6,5},{7,6},{4,7},{9,8},{10,9},{11,1... | collective-permute-start | bytes 135176 | tf_op jit(solution)/shard_map/ppermute | solution.py:26
  12.0 15.6 %copy-start.14 = (f32[32,128]{1,0:T(8,128)}, f32[32,128]{1,0:T(8,128)S(1)}, u32[]{:S(2)}) copy-start(f32[32,128]{1,0:T(8,128)S(1)} %get-tuple-element.50.refs_2_) | copy-start | bytes 49156
  12.0 15.6 %copy-start.1 = (f32[16,128,128]{2,1,0:T(8,128)S(1)}, f32[16,128,128]{2,1,0:T(8,128)}, u32[]{:S(2)}) copy-start(f32[16,128,128]{2,1,0:T(8,128)} %refs_1_.7) | copy-start | bytes 3145732
  14.1 17.4 %copy-start.13 = (f32[208,128]{1,0:T(8,128)S(1)}, f32[208,128]{1,0:T(8,128)}, u32[]{:S(2)}) copy-start(f32[208,128]{1,0:T(8,128)} %copy-done.12) | copy-start | bytes 319492
  14.1 21.3 %copy-start.17 = (f32[4]{0:T(128)S(1)}, f32[4]{0:T(128)}, u32[]{:S(2)}) copy-start(f32[4]{0:T(128)} %refs_6_.1) | copy-start | bytes 52
  28.9 12.6 %all-to-all-start.1 = ((f32[32,8,128]{2,1,0:T(8,128)}), f32[32,8,128]{2,1,0:T(8,128)S(1)}, u32[]{:S(2)}, u32[]{:S(2)}) async-start(f32[32,8,128]{2,1,0:T(8,128)} %bitcast.9), calls=%async_computation.1 | async-start | bytes 262144 | tf_op jit(solution)/shard_map/all_to_all | solution.py:786
  31.5 8.7 %collective-permute-start.4 = (f32[208,128]{1,0:T(8,128)S(1)}, f32[208,128]{1,0:T(8,128)S(1)}, u32[]{:S(2)}, u32[]{:S(2)}) collective-permute-start(f32[208,128]{1,0:T(8,128)S(1)} %get-tuple-element.52), channel_id=1, source_target_pairs={{28,0},{0,4},{4,8},{8,12},{12,16},{16,20},{20,24},{24,28},{29,1},{... | collective-permute-start | bytes 319496 | tf_op jit(solution)/shard_map/ppermute | solution.py:26
  33.3 8.2 %collective-permute-start.5 = (f32[208,128]{1,0:T(8,128)S(1)}, f32[208,128]{1,0:T(8,128)S(1)}, u32[]{:S(2)}, u32[]{:S(2)}) collective-permute-start(f32[208,128]{1,0:T(8,128)S(1)} %get-tuple-element.53), channel_id=1, source_target_pairs={{4,0},{8,4},{12,8},{16,12},{20,16},{24,20},{28,24},{0,28},{5,1},{9... | collective-permute-start | bytes 319496 | tf_op jit(solution)/shard_map/ppermute | solution.py:26
  35.1 4.2 %collective-permute-start.6 = (f32[32,128]{1,0:T(8,128)S(1)}, f32[32,128]{1,0:T(8,128)S(1)}, u32[]{:S(2)}, u32[]{:S(2)}) collective-permute-start(f32[32,128]{1,0:T(8,128)S(1)} %get-tuple-element.55.refs_3_), channel_id=1, source_target_pairs={{16,0},{0,16},{17,1},{1,17},{18,2},{2,18},{19,3},{3,19},{20,4},{4,... | collective-permute-start | bytes 49160 | tf_op jit(solution)/shard_map/ppermute | solution.py:26
  39.3 9.2 %copy-start.7 = (f32[88,128]{1,0:T(8,128)S(1)}, f32[88,128]{1,0:T(8,128)}, u32[]{:S(2)}) copy-start(f32[88,128]{1,0:T(8,128)} %copy-done.6) | copy-start | bytes 135172
  39.3 9.2 %copy-start.10 = (f32[88,128]{1,0:T(8,128)S(1)}, f32[88,128]{1,0:T(8,128)}, u32[]{:S(2)}) copy-start(f32[88,128]{1,0:T(8,128)} %copy-done.9) | copy-start | bytes 135172
  42.5 12.7 %all-to-all-start.2 = ((f32[16,8,128]{2,1,0:T(8,128)}), f32[16,8,128]{2,1,0:T(8,128)S(1)}, u32[]{:S(2)}, u32[]{:S(2)}) async-start(f32[16,8,128]{2,1,0:T(8,128)} %bitcast.11), calls=%async_computation.2 | async-start | bytes 131072 | tf_op jit(solution)/shard_map/all_to_all | solution.py:835
  56.6 11.9 %all-to-all-start.3 = ((f32[16,8,128]{2,1,0:T(8,128)}), f32[16,8,128]{2,1,0:T(8,128)S(1)}, u32[]{:S(2)}, u32[]{:S(2)}) async-start(f32[16,8,128]{2,1,0:T(8,128)} %bitcast.15), calls=%async_computation.3 | async-start | bytes 131072 | tf_op jit(solution)/shard_map/all_to_all | solution.py:867
  (8 other events, 45.5 us)

commit v6 on v5

--- a/solution.py
+++ b/solution.py
@@ -295,7 +295,6 @@
 
 def steps_kernel(
     at,
-    part,
     state_far,
     north,
     south,
@@ -308,45 +307,60 @@
     first,
     last,
     diffusion,
+    tops,
+    sea_before,
+    out_far,
+    sea_out,
+    state,
+    middle,
+    out,
     *rest,
 ):
-    if part:
-        rest = rest[1:]
-    out_far, state, middle, out, *ring, arrivals, departures = rest
-    rows, width, levels = at.rows, at.width, at.levels
+    *rings, arrivals, departures, sea_departures = rest
+    rows, levels = at.rows, at.levels
     field_rows = levels * rows
-    whole = part * at.half
 
     def coming(field):
-        return pltpu.make_async_copy(
-            state_far.at[pl.ds((whole + field) * field_rows, field_rows)],
-            state.at[pl.ds(field * field_rows, field_rows)],
-            arrivals.at[field],
-        )
+        return chunk(state_far, state, field, field_rows, arrivals.at[field])
 
     def going(field):
-        return pltpu.make_async_copy(
-            out.at[pl.ds(field * field_rows, field_rows)],
-            out_far.at[pl.ds((whole + field) * field_rows, field_rows)],
-            departures.at[field],
-        )
-
-    for field in range(at.half):
+        return chunk(out, out_far, field, field_rows, departures.at[field])
+
+    for field in range(at.fields):
         coming(field).start()
+    stored = [
+        pltpu.make_async_copy(
+            tops.at[pl.ds(flux * at.sea_rows, at.sea_rows)],
+            sea_out.at[flux, 0],
+            sea_departures.at[flux],
+        )
+        for flux in range(sea_out.shape[0])
+    ]
+    for copy in stored:
+        copy.start()
     halos = (north, south, west, east, far_north, far_south)
-    ring_step(at, part, halos, (near_first, near_last, first, last), diffusion, ring)
-    held = pl.ds(part * rows, rows)
-    outer = interleaved(at, west[held, :], east[held, :])
-    inner = interleaved(at, ring[2][...], ring[3][...])
-    for field in range(at.half):
-        number = diffusion[whole + field]
-        coming(field).wait()
-        field_step(
-            at, field, state, middle, north, south, part * at.part, outer, number
-        )
-        field_step(at, field, middle, out, ring[0], ring[1], 0, inner, number)
-        going(field).start()
-    for field in range(at.half):
+    for part in range(2):
+        ring = rings[4 * part : 4 * part + 4]
+        ring_step(at, part, halos, (near_first, near_last, first, last), diffusion, ring)
+    for part in range(2):
+        ring = rings[4 * part : 4 * part + 4]
+        held = pl.ds(part * rows, rows)
+        outer = interleaved(at, west[held, :], east[held, :])
+        inner = interleaved(at, ring[2][...], ring[3][...])
+        cells = pl.ds(part * at.part * rows, at.part * rows)
+        parts = [array.at[cells] for array in (state, middle, out)]
+        for field in range(at.half):
+            whole = part * at.half + field
+            number = diffusion[whole]
+            coming(whole).wait()
+            field_step(
+                at, field, parts[0], parts[1], north, south, part * at.part, outer, number
+            )
+            field_step(at, field, parts[1], parts[2], ring[0], ring[1], 0, inner, number)
+            going(whole).start()
+    for copy in stored:
+        copy.wait()
+    for field in range(at.fields):
         going(field).wait()
 
 
@@ -590,19 +604,6 @@
         ]
 
 
-def store_kernel(sea_rows, tops, base, out, leave):
-    copies = [
-        pltpu.make_async_copy(
-            tops.at[pl.ds(flux * sea_rows, sea_rows)], out.at[flux, 0], leave.at[flux]
-        )
-        for flux in range(out.shape[0])
-    ]
-    for copy in copies:
-        copy.start()
-    for copy in copies:
-        copy.wait()
-
-
 def tops_of_tiles(returned, routes, flux_count, scratch):
     slots, width = routes.shape
     rows = scratch.shape[0] // flux_count
@@ -823,40 +824,9 @@
         other_labels,
         here,
     )
-    ocean_next = call(
-        functools.partial(store_kernel, sea_rows),
-        "store",
-        array(sea_fields, sea_levels, sea_rows, width),
-        [VMEM, ANY],
-        [ocean_flags],
-        out_specs=ANY,
-        input_output_aliases={1: 0},
-    )(tops, sea_base.reshape(sea_fields, sea_levels, sea_rows, width))
     answered = lax.all_to_all(
         answers.reshape(targets, CAPACITY * sea_fields, width), SECTION, 0, 0, tiled=True
     )
-    def both_steps(part, before, **more):
-        return call(
-            functools.partial(steps_kernel, at, part),
-            "steps_" + "ab"[part],
-            array(blocks * rows, width),
-            [ANY] + [VMEM] * 10 + [SMEM] + [ANY] * part,
-            [pltpu.VMEM((at.part * rows, width), F32)] * 3
-            + [pltpu.VMEM((at.ring_rows, width), F32)] * 2
-            + [pltpu.VMEM((rows, width), F32)] * 2
-            + [pltpu.SemaphoreType.DMA((at.half,))] * 2,
-            after=(before,),
-            limit=STEPS_LIMIT,
-            work=1_000_000_000,
-            out_specs=ANY,
-            **more,
-        )
-
-    halos = (north, south, west, east, far_north, far_south)
-    halos += (near_first, near_last, first_cols, last_cols)
-    atmos_next = both_steps(0, answers)(state, *halos, atmos_diffusion)
-    answered, atmos_next, ocean_next = lax.optimization_barrier((answered, atmos_next, ocean_next))
-
     replies = call(
         functools.partial(reply_kernel, sea_fields),
         "replies",
@@ -867,8 +837,38 @@
     returned = lax.all_to_all(
         replies.reshape(targets, CAPACITY * sea_fields, width), SECTION, 0, 0, tiled=True
     )
-    atmos_next = both_steps(1, replies, input_output_aliases={12: 0})(
-        state, *halos, atmos_diffusion, atmos_next
+    atmos_next, ocean_next = call(
+        functools.partial(steps_kernel, at),
+        "steps",
+        (array(blocks * rows, width), array(sea_fields, sea_levels, sea_rows, width)),
+        [ANY] + [VMEM] * 10 + [SMEM, ANY, ANY],
+        [state_copy] * 3
+        + (
+            [pltpu.VMEM((at.ring_rows, width), F32)] * 2 + [pltpu.VMEM((rows, width), F32)] * 2
+        )
+        * 2
+        + [pltpu.SemaphoreType.DMA((fields,))] * 2
+        + [ocean_flags],
+        after=(replies,),
+        limit=STEPS_LIMIT,
+        work=1_000_000_000,
+        out_specs=(ANY, ANY),
+        input_output_aliases={13: 1},
+    )(
+        state,
+        north,
+        south,
+        west,
+        east,
+        far_north,
+        far_south,
+        near_first,
+        near_last,
+        first_cols,
+        last_cols,
+        atmos_diffusion,
+        tops,
+        sea_base.reshape(sea_fields, sea_levels, sea_rows, width),
     )
     ocean_surface = call(
         functools.partial(surface_kernel, sea_fields),

time: 69.9 us -> 68.7 us (0.983)
  blocking collectives: 12.9 us -> 25.3 us
  starting transfers between devices: 23.5 us -> 17.4 us
  waiting for transfers between devices: 9.82 us -> 4.66 us
  Pallas kernels: 22.1 us -> 19.4 us
    all_to_all x0 -> x1, blocking collectives: none -> 12.5 us  [on_device(): lax.all_to_all(answers.reshape(targets, CAPACITY * sea_fields, width), SE...]
    all_to_all x1 -> x0, starting transfers between devices: 5.2 us -> none  [on_device(): lax.all_to_all(answers.reshape(targets, CAPACITY * sea_fields, width), SE...]
    pallas_call x16 -> x14, Pallas kernels: 22.1 us -> 19.4 us  [call(): return lambda *arguments: run(*arguments, *after)]
    all_to_all x1 -> x0, waiting for transfers between devices: 2.75 us -> none  [on_device(): lax.all_to_all(answers.reshape(targets, CAPACITY * sea_fields, width), SE...]
    all_to_all x1, waiting for transfers between devices: 2.99 us -> 0.99 us  [on_device(): lax.all_to_all(replies.reshape(targets, CAPACITY * sea_fields, width), SE...]
    all_to_all x1, starting transfers between devices: 4.31 us -> 3.5 us  [on_device(): lax.all_to_all(replies.reshape(targets, CAPACITY * sea_fields, width), SE...]
  transfers between devices with their start and end apart: 10 -> 9, of which waited for: 6 -> 5; matrix products, arithmetic and copies ran while one was open for 0% -> 0% of each run, Pallas kernels for 21% -> 17%
where the time goes in v6:
time: 68.7 us; the launch traced here: 68.3 us
  blocking collectives  25.3 us (37%)
  Pallas kernels  19.4 us (28%)
  starting transfers between devices  17.4 us (25%)
  waiting for transfers between devices  4.66 us (7%)
  between operations  0.88 us (1%)
  local copies, waits for them, and re-layouts  0.71 us (1%)
    pallas_call x14, Pallas kernels, call(): return lambda *arguments: run(*arguments, *after)  19.4 us
    all_to_all x1, blocking collectives, on_device(): lax.all_to_all(pieces.reshape(targets, CAPACITY * PIECE_ROWS, width), SEC...  12.8 us
    all_to_all x1, blocking collectives, on_device(): lax.all_to_all(answers.reshape(targets, CAPACITY * sea_fields, width), SE...  12.5 us
    ppermute x7, starting transfers between devices, shifted(): return lax.ppermute(block, axis, route)  11.3 us
    ppermute x7, waiting for transfers between devices, shifted(): return lax.ppermute(block, axis, route)  3.67 us
    all_to_all x1, starting transfers between devices, on_device(): lax.all_to_all(replies.reshape(targets, CAPACITY * sea_fields, width), SE...  3.5 us
    all_to_all x1, starting transfers between devices, on_device(): lax.all_to_all(outgoing.reshape(devices, CAPACITY * sea_fields, width), E...  2.58 us
  transfers between devices with their start and end apart: 9, of which 5 were waited for; matrix products, arithmetic and copies ran while one was open for 0% of the time, Pallas kernels for 17%

profile of v6, /device:TPU:0, one launch (start us, length us, event | category | flops | bytes accessed | tf_op | source)
XLA Modules:
  0.0 68.3 jit_solution(4958361799072846377)
XLA Ops:
  0.7 2.2 %edges.1 = (f32[240,128]{1,0:T(8,128)S(1)}, f32[240,128]{1,0:T(8,128)S(1)}, f32[208,128]{1,0:T(8,128)S(1)}, f32[208,128]{1,0:T(8,128)S(1)}, f32[88,128]{1,0:T(8,128)S(1)}, /*index=5*/f32[88,128]{1,0:T(8,128)S(1)}) custom-call(f32[3200,128]{1,0:T(8,128)} %bitcast.18), custom_call_target="tpu_custom_call" | custom-call | bytes 1000000 | tf_op jit(solution)/shard_map/edges/pallas_call | solution.py:674
  2.9 1.0 %sea_edges.1 = (f32[240,128]{1,0:T(8,128)S(1)}, f32[240,128]{1,0:T(8,128)S(1)}, f32[88,128]{1,0:T(8,128)}, f32[88,128]{1,0:T(8,128)}) custom-call(f32[2048,128]{1,0:T(8,128)S(1)} %bitcast.21, s32[64,128]{1,0:T(8,128)S(1)} %copy-done.5, f32[240,128]{1,0:T(8,128)S(1)} %get-tuple-element.33.refs_2_, f32[240,128]{1,0:T(8,128)S(1)} %get-tuple-element.34.refs_3_, ...), custom_call_target="tpu_custom_call" | custom-call | bytes 1000000 | tf_op jit(solution)/shard_map/sea_edges/pallas_call | solution.py:674
  3.9 3.0 %collective-permute-start = (f32[240,128]{1,0:T(8,128)S(1)}, f32[240,128]{1,0:T(8,128)S(1)}, u32[]{:S(2)}, u32[]{:S(2)}) collective-permute-start(f32[240,128]{1,0:T(8,128)S(1)} %get-tuple-element.37.refs_8_), channel_id=1, source_target_pairs={{28,0},{0,4},{4,8},{8,12},{12,16},{16,20},{20,24},{24,28},{29,1},{... | collective-permute-start | bytes 368648 | tf_op jit(solution)/shard_map/ppermute | solution.py:26
  6.9 1.5 %collective-permute-start.1 = (f32[240,128]{1,0:T(8,128)S(1)}, f32[240,128]{1,0:T(8,128)S(1)}, u32[]{:S(2)}, u32[]{:S(2)}) collective-permute-start(f32[240,128]{1,0:T(8,128)S(1)} %get-tuple-element.38.refs_7_), channel_id=1, source_target_pairs={{4,0},{8,4},{12,8},{16,12},{20,16},{24,20},{28,24},{0,28},{5,1},{9... | collective-permute-start | bytes 368648 | tf_op jit(solution)/shard_map/ppermute | solution.py:26
  8.4 2.0 %collective-permute-start.2 = (f32[88,128]{1,0:T(8,128)}, f32[88,128]{1,0:T(8,128)S(1)}, u32[]{:S(2)}, u32[]{:S(2)}) collective-permute-start(f32[88,128]{1,0:T(8,128)} %get-tuple-element.39.refs_10_), channel_id=1, source_target_pairs={{3,0},{0,1},{1,2},{2,3},{7,4},{4,5},{5,6},{6,7},{11,8},{8,9},{9,10... | collective-permute-start | bytes 135176 | tf_op jit(solution)/shard_map/ppermute | solution.py:26
  10.4 1.0 %collective-permute-start.3 = (f32[88,128]{1,0:T(8,128)}, f32[88,128]{1,0:T(8,128)S(1)}, u32[]{:S(2)}, u32[]{:S(2)}) collective-permute-start(f32[88,128]{1,0:T(8,128)} %get-tuple-element.40.refs_9_), channel_id=1, source_target_pairs={{1,0},{2,1},{3,2},{0,3},{5,4},{6,5},{7,6},{4,7},{9,8},{10,9},{11,1... | collective-permute-start | bytes 135176 | tf_op jit(solution)/shard_map/ppermute | solution.py:26
  11.5 0.6 copy-done.7
  12.2 0.9 %routes.1 = (f32[32,128]{1,0:T(8,128)S(1)}, f32[32,128]{1,0:T(8,128)S(1)}, f32[32,128]{1,0:T(8,128)S(1)}, f32[8,128]{1,0:T(8,128)S(1)}, f32[16,128]{1,0:T(8,128)S(1)}) custom-call(s32[4,16]{1,0:T(4,128)S(1)} %pad_add_fusion.refs_0_, s32[1]{0:T(128)} %bitcast.6.refs_1_, f32[10]{0:T(128)S(1)} %copy-done.7), custom_call_target="tpu_custom_call" | custom-call | bytes 1000000 | tf_op jit(solution)/shard_map/routes/pallas_call | solution.py:674
  13.8 1.0 %collective-permute-done.3.refs_4_.refs_3_.refs_5_ = f32[88,128]{1,0:T(8,128)S(1)} collective-permute-done((f32[88,128]{1,0:T(8,128)}, f32[88,128]{1,0:T(8,128)S(1)}, u32[]{:S(2)}, u32[]{:S(2)}) %collective-permute-start.3) | collective-permute-done | bytes 45088 | tf_op jit(solution)/shard_map/ppermute | solution.py:26
  14.8 0.6 pieces.1
  15.4 12.8 %all_to_all.20 = f32[16,16,128]{2,1,0:T(8,128)S(1)} all-to-all(f32[16,16,128]{2,1,0:T(8,128)S(1)} %bitcast.22), channel_id=1, replica_groups=mesh['comp'=2,'gx'=4,'gy'=4] {'gx','gy'}, dimensions={0} | all-to-all | bytes 262144 | tf_op jit(solution)/shard_map/all_to_all | solution.py:773
  28.1 1.3 %fluxes.1 = (f32[256,128]{1,0:T(8,128)}, f32[32,128]{1,0:T(8,128)S(1)}, f32[32,128]{1,0:T(8,128)S(1)}) custom-call(f32[256,128]{1,0:T(8,128)S(1)} %bitcast.23, f32[16,128,128]{2,1,0:T(8,128)S(1)} %copy-done.1, f32[32,128]{1,0:T(8,128)S(1)} %get-tuple-element.49.refs_2_), custom_call_target="tpu_custom_call" | custom-call | bytes 1000000 | tf_op jit(solution)/shard_map/fluxes/pallas_call | solution.py:674
  29.4 2.6 %all-to-all-start.1 = ((f32[32,8,128]{2,1,0:T(8,128)}), f32[32,8,128]{2,1,0:T(8,128)S(1)}, u32[]{:S(2)}, u32[]{:S(2)}) async-start(f32[32,8,128]{2,1,0:T(8,128)} %bitcast.9), calls=%async_computation.1 | async-start | bytes 262144 | tf_op jit(solution)/shard_map/all_to_all | solution.py:787
  32.1 1.7 %collective-permute-start.4 = (f32[208,128]{1,0:T(8,128)S(1)}, f32[208,128]{1,0:T(8,128)S(1)}, u32[]{:S(2)}, u32[]{:S(2)}) collective-permute-start(f32[208,128]{1,0:T(8,128)S(1)} %get-tuple-element.51), channel_id=1, source_target_pairs={{28,0},{0,4},{4,8},{8,12},{12,16},{16,20},{20,24},{24,28},{29,1},{... | collective-permute-start | bytes 319496 | tf_op jit(solution)/shard_map/ppermute | solution.py:26
  33.8 1.9 %collective-permute-start.5 = (f32[208,128]{1,0:T(8,128)S(1)}, f32[208,128]{1,0:T(8,128)S(1)}, u32[]{:S(2)}, u32[]{:S(2)}) collective-permute-start(f32[208,128]{1,0:T(8,128)S(1)} %get-tuple-element.52), channel_id=1, source_target_pairs={{4,0},{8,4},{12,8},{16,12},{20,16},{24,20},{28,24},{0,28},{5,1},{9... | collective-permute-start | bytes 319496 | tf_op jit(solution)/shard_map/ppermute | solution.py:26
  35.9 3.9 %sea_base.1 = (f32[2048,128]{1,0:T(8,128)}, f32[256,128]{1,0:T(8,128)S(1)}) custom-call(f32[2048,128]{1,0:T(8,128)} %bitcast.20, s32[64,128]{1,0:T(8,128)S(1)} %copy-done.5, f32[240,128]{1,0:T(8,128)S(1)} %collective-permute-done.refs_1_.refs_2_, f32[240,128]{1,0:T(8,128)S(1)} %collective-permute-done.1.refs_2_.refs_3_, ...), custom_call_target="tpu_custom_call" | custom-call | bytes 1000000000 | tf_op jit(solution)/shard_map/sea_base/pallas_call | solution.py:674
  39.8 0.9 %collective-permute-done.4.refs_6_.refs_5_ = f32[208,128]{1,0:T(8,128)S(1)} collective-permute-done((f32[208,128]{1,0:T(8,128)S(1)}, f32[208,128]{1,0:T(8,128)S(1)}, u32[]{:S(2)}, u32[]{:S(2)}) %collective-permute-start.4) | collective-permute-done | bytes 106528 | tf_op jit(solution)/shard_map/ppermute | solution.py:26
  40.7 1.3 %collective-permute-done.5.refs_7_.refs_6_ = f32[208,128]{1,0:T(8,128)S(1)} collective-permute-done((f32[208,128]{1,0:T(8,128)S(1)}, f32[208,128]{1,0:T(8,128)S(1)}, u32[]{:S(2)}, u32[]{:S(2)}) %collective-permute-start.5) | collective-permute-done | bytes 106528 | tf_op jit(solution)/shard_map/ppermute | solution.py:26
  42.4 12.5 %all_to_all.21 = f32[16,8,128]{2,1,0:T(8,128)S(1)} all-to-all(f32[16,8,128]{2,1,0:T(8,128)S(1)} %bitcast.27), channel_id=1, replica_groups=mesh['comp'=2,'gx'=4,'gy'=4] {'gx','gy'}, dimensions={0} | all-to-all | bytes 131072 | tf_op jit(solution)/shard_map/all_to_all | solution.py:827
  55.0 1.3 %replies.1.refs_14_ = f32[128,128]{1,0:T(8,128)} custom-call(f32[128,128]{1,0:T(8,128)S(1)} %bitcast.26, f32[16,128,128]{2,1,0:T(8,128)S(1)} %copy-done.1, f32[32,128]{1,0:T(8,128)S(1)} %get-tuple-element.49.refs_2_, f32[32,128]{1,0:T(8,128)S(1)} %get-tuple-element.59.refs_3_), custom_call_target="tpu_custom_call" | custom-call | bytes 1000000 | tf_op jit(solution)/shard_map/replies/pallas_call | solution.py:674
  56.2 3.5 %all-to-all-start.3 = ((f32[16,8,128]{2,1,0:T(8,128)}), f32[16,8,128]{2,1,0:T(8,128)S(1)}, u32[]{:S(2)}, u32[]{:S(2)}) async-start(f32[16,8,128]{2,1,0:T(8,128)} %bitcast.15), calls=%async_computation.3 | async-start | bytes 131072 | tf_op jit(solution)/shard_map/all_to_all | solution.py:837
  60.1 6.1 %steps.1 = (f32[3200,128]{1,0:T(8,128)}, f32[4,8,64,128]{3,2,1,0:T(8,128)}) custom-call(f32[3200,128]{1,0:T(8,128)} %bitcast.19, f32[240,128]{1,0:T(8,128)S(1)} %collective-permute-done.refs_1_.refs_2_, f32[240,128]{1,0:T(8,128)S(1)} %collective-permute-done.1.refs_2_.refs_3_, ...), custom_call_target="tpu_custom_call", output_to_operand_aliasing={{1}: (13, {})} | custom-call | bytes 1000000000 | tf_op jit(solution)/shard_map/steps/pallas_call | solution.py:674
  66.3 1.0 %all-to-all-done.3 = f32[16,8,128]{2,1,0:T(8,128)S(1)} async-done(((f32[16,8,128]{2,1,0:T(8,128)}), f32[16,8,128]{2,1,0:T(8,128)S(1)}, u32[]{:S(2)}, u32[]{:S(2)}) %all-to-all-start.3) | async-done | bytes 65568 | tf_op jit(solution)/shard_map/all_to_all | solution.py:837
  67.3 1.1 %surface.1 = f32[64,128]{1,0:T(8,128)} custom-call(f32[128,128]{1,0:T(8,128)S(1)} %bitcast.25, bf16[16,256,128]{2,1,0:T(8,128)(2,1)S(1)} %surface_weights.1.refs_1_, f32[32,128]{1,0:T(8,128)S(1)} %get-tuple-element.47.refs_7_.refs_2_), custom_call_target="tpu_custom_call" | custom-call | bytes 1000000 | tf_op jit(solution)/shard_map/surface/pallas_call | solution.py:674
  (39 shorter events, 1.8 us)
Async XLA Ops:
  0.6 2.3 %copy-start.2 = (f32[4,8,64,128]{3,2,1,0:T(8,128)S(1)}, f32[4,8,64,128]{3,2,1,0:T(8,128)}, u32[]{:S(2)}) copy-start(f32[4,8,64,128]{3,2,1,0:T(8,128)} %param.19) | copy-start | bytes 3145732
  0.6 2.3 %copy-start.5 = (s32[64,128]{1,0:T(8,128)S(1)}, s32[64,128]{1,0:T(8,128)}, u32[]{:S(2)}) copy-start(s32[64,128]{1,0:T(8,128)} %refs_2_.3) | copy-start | bytes 98308
  0.7 10.7 %copy-start.10 = (s32[16]{0:T(128)S(1)}, s32[16]{0:T(128)}, u32[]{:S(2)}) copy-start(s32[16]{0:T(128)} %param.18) | copy-start | bytes 196
  0.7 10.7 %copy-start.11 = (s32[16,1]{0,1:T(1,128)S(1)}, s32[16,1]{0,1:T(1,128)}, u32[]{:S(2)}) copy-start(s32[16,1]{0,1:T(1,128)} %param.17) | copy-start | bytes 196
  0.7 10.7 %copy-start.12 = (s32[16]{0:T(128)S(1)}, s32[16]{0:T(128)}, u32[]{:S(2)}) copy-start(s32[16]{0:T(128)} %param.15) | copy-start | bytes 196
  0.7 10.7 %copy-start.13 = (s32[16,1]{0,1:T(1,128)S(1)}, s32[16,1]{0,1:T(1,128)}, u32[]{:S(2)}) copy-start(s32[16,1]{0,1:T(1,128)} %param.14) | copy-start | bytes 196
  0.7 10.7 %copy-start.3 = (f32[16,128,128]{2,1,0:T(8,128)S(1)}, f32[16,128,128]{2,1,0:T(8,128)}, u32[]{:S(2)}) copy-start(f32[16,128,128]{2,1,0:T(8,128)} %refs_0_.2) | copy-start | bytes 3145732
  2.9 10.2 %copy-start = (f32[10,20,16,128]{3,2,1,0:T(8,128)S(1)}, f32[10,20,16,128]{3,2,1,0:T(8,128)}, u32[]{:S(2)}) copy-start(f32[10,20,16,128]{3,2,1,0:T(8,128)} %refs_0_) | copy-start | bytes 4915204
  3.9 10.9 %collective-permute-start = (f32[240,128]{1,0:T(8,128)S(1)}, f32[240,128]{1,0:T(8,128)S(1)}, u32[]{:S(2)}, u32[]{:S(2)}) collective-permute-start(f32[240,128]{1,0:T(8,128)S(1)} %get-tuple-element.37.refs_8_), channel_id=1, source_target_pairs={{28,0},{0,4},{4,8},{8,12},{12,16},{16,20},{20,24},{24,28},{29,1},{... | collective-permute-start | bytes 368648 | tf_op jit(solution)/shard_map/ppermute | solution.py:26
  6.9 7.8 %collective-permute-start.1 = (f32[240,128]{1,0:T(8,128)S(1)}, f32[240,128]{1,0:T(8,128)S(1)}, u32[]{:S(2)}, u32[]{:S(2)}) collective-permute-start(f32[240,128]{1,0:T(8,128)S(1)} %get-tuple-element.38.refs_7_), channel_id=1, source_target_pairs={{4,0},{8,4},{12,8},{16,12},{20,16},{24,20},{28,24},{0,28},{5,1},{9... | collective-permute-start | bytes 368648 | tf_op jit(solution)/shard_map/ppermute | solution.py:26
  8.4 5.3 %collective-permute-start.2 = (f32[88,128]{1,0:T(8,128)}, f32[88,128]{1,0:T(8,128)S(1)}, u32[]{:S(2)}, u32[]{:S(2)}) collective-permute-start(f32[88,128]{1,0:T(8,128)} %get-tuple-element.39.refs_10_), channel_id=1, source_target_pairs={{3,0},{0,1},{1,2},{2,3},{7,4},{4,5},{5,6},{6,7},{11,8},{8,9},{9,10... | collective-permute-start | bytes 135176 | tf_op jit(solution)/shard_map/ppermute | solution.py:26
  10.4 4.4 %collective-permute-start.3 = (f32[88,128]{1,0:T(8,128)}, f32[88,128]{1,0:T(8,128)S(1)}, u32[]{:S(2)}, u32[]{:S(2)}) collective-permute-start(f32[88,128]{1,0:T(8,128)} %get-tuple-element.40.refs_9_), channel_id=1, source_target_pairs={{1,0},{2,1},{3,2},{0,3},{5,4},{6,5},{7,6},{4,7},{9,8},{10,9},{11,1... | collective-permute-start | bytes 135176 | tf_op jit(solution)/shard_map/ppermute | solution.py:26
  11.5 0.7 copy-start.7
  13.1 15.0 %copy-start.1 = (f32[16,128,128]{2,1,0:T(8,128)S(1)}, f32[16,128,128]{2,1,0:T(8,128)}, u32[]{:S(2)}) copy-start(f32[16,128,128]{2,1,0:T(8,128)} %refs_1_.7) | copy-start | bytes 3145732
  14.8 21.1 %copy-start.9 = (f32[4]{0:T(128)S(1)}, f32[4]{0:T(128)}, u32[]{:S(2)}) copy-start(f32[4]{0:T(128)} %refs_6_.1) | copy-start | bytes 52
  29.4 12.6 %all-to-all-start.1 = ((f32[32,8,128]{2,1,0:T(8,128)}), f32[32,8,128]{2,1,0:T(8,128)S(1)}, u32[]{:S(2)}, u32[]{:S(2)}) async-start(f32[32,8,128]{2,1,0:T(8,128)} %bitcast.9), calls=%async_computation.1 | async-start | bytes 262144 | tf_op jit(solution)/shard_map/all_to_all | solution.py:787
  32.1 8.7 %collective-permute-start.4 = (f32[208,128]{1,0:T(8,128)S(1)}, f32[208,128]{1,0:T(8,128)S(1)}, u32[]{:S(2)}, u32[]{:S(2)}) collective-permute-start(f32[208,128]{1,0:T(8,128)S(1)} %get-tuple-element.51), channel_id=1, source_target_pairs={{28,0},{0,4},{4,8},{8,12},{12,16},{16,20},{20,24},{24,28},{29,1},{... | collective-permute-start | bytes 319496 | tf_op jit(solution)/shard_map/ppermute | solution.py:26
  33.8 8.2 %collective-permute-start.5 = (f32[208,128]{1,0:T(8,128)S(1)}, f32[208,128]{1,0:T(8,128)S(1)}, u32[]{:S(2)}, u32[]{:S(2)}) collective-permute-start(f32[208,128]{1,0:T(8,128)S(1)} %get-tuple-element.52), channel_id=1, source_target_pairs={{4,0},{8,4},{12,8},{16,12},{20,16},{24,20},{28,24},{0,28},{5,1},{9... | collective-permute-start | bytes 319496 | tf_op jit(solution)/shard_map/ppermute | solution.py:26
  35.7 24.1 %copy-start.4 = (f32[16,128,128]{2,1,0:T(8,128)S(1)}, f32[16,128,128]{2,1,0:T(8,128)}, u32[]{:S(2)}) copy-start(f32[16,128,128]{2,1,0:T(8,128)} %refs_0_.2) | copy-start | bytes 3145732
  35.7 4.1 %collective-permute-start.6 = (f32[32,128]{1,0:T(8,128)S(1)}, f32[32,128]{1,0:T(8,128)S(1)}, u32[]{:S(2)}, u32[]{:S(2)}) collective-permute-start(f32[32,128]{1,0:T(8,128)S(1)} %get-tuple-element.54.refs_3_), channel_id=1, source_target_pairs={{16,0},{0,16},{17,1},{1,17},{18,2},{2,18},{19,3},{3,19},{20,4},{4,... | collective-permute-start | bytes 49160 | tf_op jit(solution)/shard_map/ppermute | solution.py:26
  42.4 13.8 %copy-start.6 = (f32[256,128]{1,0:T(8,128)}, f32[256,128]{1,0:T(8,128)S(1)}, u32[]{:S(2)}) copy-start(f32[256,128]{1,0:T(8,128)S(1)} %get-tuple-element.56.refs_12_) | copy-start | bytes 393220
  55.0 5.2 %copy-start.8 = (f32[10]{0:T(128)S(1)}, f32[10]{0:T(128)}, u32[]{:S(2)}) copy-start(f32[10]{0:T(128)} %refs_11_.1) | copy-start | bytes 124
  56.2 11.0 %all-to-all-start.3 = ((f32[16,8,128]{2,1,0:T(8,128)}), f32[16,8,128]{2,1,0:T(8,128)S(1)}, u32[]{:S(2)}, u32[]{:S(2)}) async-start(f32[16,8,128]{2,1,0:T(8,128)} %bitcast.15), calls=%async_computation.3 | async-start | bytes 131072 | tf_op jit(solution)/shard_map/all_to_all | solution.py:837

commit v7 on v6

--- a/solution.py
+++ b/solution.py
@@ -532,7 +532,12 @@
     out[pl.ds(count, slots, stride=PIECE_ROWS), :] = labels[...]
 
 
-def flux_kernel(sizes, arrived, remap, routes, out, gather, sea_labels, fluxes, products):
+def sea_labels_kernel(rows, arrived, sea_labels):
+    labels = arrived[pl.ds(PIECE_ROWS - 1, sea_labels.shape[0], stride=PIECE_ROWS), :]
+    sea_labels[...] = jnp.floor(labels * (1.0 / label_base(rows))) - 1.0
+
+
+def flux_kernel(sizes, arrived, remap, routes, out, gather, fluxes, products):
     flux_count, rows, sections = sizes
     width = out.shape[1]
     slots = routes.shape[0]
@@ -541,7 +546,6 @@
     upper = jnp.floor(labels * (1.0 / label_base(rows)))
     select = one_hot(labels - label_base(rows) * upper - 1.0)
     gather[...] = select
-    sea_labels[...] = upper - 1.0
     values = jnp.concatenate(
         [arrived[pl.ds(place, slots, stride=PIECE_ROWS), :] for place in range(count)], axis=1
     )
@@ -639,12 +643,12 @@
         ]
 
 
-def surface_kernel(flux_count, returned, weights, routes, out, tops):
-    rows = weights.shape[0]
+def surface_kernel(flux_count, returned, remap, routes, out, tops):
+    rows = remap.shape[0]
     tops_of_tiles(returned, routes, flux_count, tops)
     for tile in range(rows):
         out[pl.ds(tile, flux_count, stride=rows), :] = remapped(
-            tops[pl.ds(tile * flux_count, flux_count), :], weights[tile]
+            tops[pl.ds(tile * flux_count, flux_count), :], both_halves(jnp.transpose(remap[tile]))
         )
 
 
@@ -773,27 +777,12 @@
     arrived = lax.all_to_all(
         pieces.reshape(targets, CAPACITY * PIECE_ROWS, width), SECTION, 0, 0, tiled=True
     )
-    outgoing, gather, own_labels = call(
-        functools.partial(flux_kernel, (sea_fields, rows, sections)),
-        "fluxes",
-        (
-            array(sections * slots * sea_fields, width),
-            array(slots, width),
-            array(slots, width),
-        ),
-        [VMEM] * 3,
-        [pltpu.VMEM((sea_fields * rows, width), F32)] * 2,
-    )(arrived.reshape(slots * PIECE_ROWS, width), remap_ocean, sea_slots)
-    landed = lax.all_to_all(
-        outgoing.reshape(devices, CAPACITY * sea_fields, width), EVERY, 0, 0, tiled=True
-    )
-    other_labels = shifted(own_labels, "comp", 1)
     to_north, to_south = call(
         functools.partial(corners_kernel, at),
         "corners",
         (array(at.far_rows, width),) * 2,
         [VMEM] * 4,
-        after=(outgoing,),
+        after=(pieces,),
     )(far_first, far_last, west, east)
     far_north = shifted(to_south, ring, 1)
     far_south = shifted(to_north, ring, -1)
@@ -804,18 +793,36 @@
         (array(sea_blocks * sea_rows, width), array(sea_fields * sea_rows, width)),
         [ANY] + [VMEM] * 5 + [SMEM],
         [ocean_copy] * 2 + [pltpu.VMEM((width, width), F32)] * 2 + [ocean_flags] * 2,
-        after=(outgoing,),
+        after=(pieces,),
         limit=SEA_LIMIT,
         work=1_000_000_000,
         out_specs=(ANY, VMEM),
     )(ocean, wet_mask, north, south, west, east, ocean_mixing)
 
+    arrived, sea_base, far_north, far_south = lax.optimization_barrier(
+        (arrived, sea_base, far_north, far_south)
+    )
+    arrived = arrived.reshape(slots * PIECE_ROWS, width)
+    own_labels = call(
+        functools.partial(sea_labels_kernel, rows), "sea_labels", array(slots, width), [VMEM]
+    )(arrived)
+    other_labels = shifted(own_labels, "comp", 1)
+    outgoing, gather = call(
+        functools.partial(flux_kernel, (sea_fields, rows, sections)),
+        "fluxes",
+        (array(sections * slots * sea_fields, width), array(slots, width)),
+        [VMEM] * 3,
+        [pltpu.VMEM((sea_fields * rows, width), F32)] * 2,
+    )(arrived, remap_ocean, sea_slots)
+    outgoing, other_labels = lax.optimization_barrier((outgoing, other_labels))
+    landed = lax.all_to_all(
+        outgoing.reshape(devices, CAPACITY * sea_fields, width), EVERY, 0, 0, tiled=True
+    )
     tops, answers = call(
         functools.partial(sea_kernel, (sea_fields, sea_rows)),
         "sea_top",
         (array(sea_fields * sea_rows, width), array(slots * sea_fields, width)),
         [VMEM] * 6,
-        after=(far_north, far_south),
     )(
         landed.reshape(devices * CAPACITY * sea_fields, width),
         base_tops,
@@ -878,7 +885,7 @@
         [pltpu.VMEM((sea_fields * rows, width), F32)],
     )(
         returned.reshape(slots * sea_fields, width),
-        weights_of(remap_atmos, True, "surface_weights", replies),
+        remap_atmos,
         tile_slots,
     )
     return (

time: 68.7 us -> 68 us (0.990)
  blocking collectives: 25.3 us -> 22.4 us
  waiting for transfers between devices: 4.66 us -> 6.62 us
  Pallas kernels: 19.4 us -> 18.1 us
  starting transfers between devices: 17.4 us -> 18.3 us
    all_to_all x1, blocking collectives: 12.5 us -> 10.6 us  [on_device(): lax.all_to_all(answers.reshape(targets, CAPACITY * sea_fields, width), SE...]
    ppermute x7, waiting for transfers between devices: 3.67 us -> 5 us  [shifted(): return lax.ppermute(block, axis, route)]
    pallas_call x14, Pallas kernels: 19.4 us -> 18.1 us  [call(): return lambda *arguments: run(*arguments, *after)]
    all_to_all x1, starting transfers between devices: 2.58 us -> 3.61 us  [on_device(): lax.all_to_all(pieces.reshape(targets, CAPACITY * PIECE_ROWS, width), SEC...]
    all_to_all x1, blocking collectives: 12.8 us -> 11.8 us  [on_device(): lax.all_to_all(outgoing.reshape(devices, CAPACITY * sea_fields, width), E...]
  transfers between devices with their start and end apart: 9 -> 9, of which waited for: 5 -> 4; matrix products, arithmetic and copies ran while one was open for 0% -> 0% of each run, Pallas kernels for 17% -> 17%
where the time goes in v7:
time: 68 us; the launch traced here: 67.5 us
  blocking collectives  22.4 us (33%)
  starting transfers between devices  18.3 us (27%)
  Pallas kernels  18.1 us (27%)
  waiting for transfers between devices  6.62 us (10%)
  local copies, waits for them, and re-layouts  1.28 us (2%)
  between operations  0.9 us (1%)
    pallas_call x14, Pallas kernels, call(): return lambda *arguments: run(*arguments, *after)  18.1 us
    all_to_all x1, blocking collectives, on_device(): lax.all_to_all(outgoing.reshape(devices, CAPACITY * sea_fields, width), E...  11.8 us
    ppermute x7, starting transfers between devices, shifted(): return lax.ppermute(block, axis, route)  11.2 us
    all_to_all x1, blocking collectives, on_device(): lax.all_to_all(answers.reshape(targets, CAPACITY * sea_fields, width), SE...  10.6 us
    ppermute x7, waiting for transfers between devices, shifted(): return lax.ppermute(block, axis, route)  5 us
    all_to_all x1, starting transfers between devices, on_device(): lax.all_to_all(pieces.reshape(targets, CAPACITY * PIECE_ROWS, width), SEC...  3.61 us
    all_to_all x1, starting transfers between devices, on_device(): lax.all_to_all(replies.reshape(targets, CAPACITY * sea_fields, width), SE...  3.48 us
    all_to_all x1, waiting for transfers between devices, on_device(): lax.all_to_all(replies.reshape(targets, CAPACITY * sea_fields, width), SE...  1.62 us
  transfers between devices with their start and end apart: 9, of which 4 were waited for; matrix products, arithmetic and copies ran while one was open for 0% of the time, Pallas kernels for 17%

profile of v7, /device:TPU:0, one launch (start us, length us, event | category | flops | bytes accessed | tf_op | source)
XLA Modules:
  0.0 67.5 jit_solution(1421971864629022713)
XLA Ops:
  0.7 2.1 %edges.1 = (f32[240,128]{1,0:T(8,128)S(1)}, f32[240,128]{1,0:T(8,128)S(1)}, f32[208,128]{1,0:T(8,128)S(1)}, f32[208,128]{1,0:T(8,128)S(1)}, f32[88,128]{1,0:T(8,128)S(1)}, /*index=5*/f32[88,128]{1,0:T(8,128)S(1)}) custom-call(f32[3200,128]{1,0:T(8,128)} %bitcast.18), custom_call_target="tpu_custom_call" | custom-call | bytes 1000000 | tf_op jit(solution)/shard_map/edges/pallas_call | solution.py:678
  2.9 0.4 sea_edges.1
  3.2 3.1 %collective-permute-start = (f32[240,128]{1,0:T(8,128)S(1)}, f32[240,128]{1,0:T(8,128)S(1)}, u32[]{:S(2)}, u32[]{:S(2)}) collective-permute-start(f32[240,128]{1,0:T(8,128)S(1)} %get-tuple-element.41.refs_8_), channel_id=1, source_target_pairs={{28,0},{0,4},{4,8},{8,12},{12,16},{16,20},{20,24},{24,28},{29,1},{... | collective-permute-start | bytes 368648 | tf_op jit(solution)/shard_map/ppermute | solution.py:26
  6.3 1.5 %collective-permute-start.1 = (f32[240,128]{1,0:T(8,128)S(1)}, f32[240,128]{1,0:T(8,128)S(1)}, u32[]{:S(2)}, u32[]{:S(2)}) collective-permute-start(f32[240,128]{1,0:T(8,128)S(1)} %get-tuple-element.42.refs_7_), channel_id=1, source_target_pairs={{4,0},{8,4},{12,8},{16,12},{20,16},{24,20},{28,24},{0,28},{5,1},{9... | collective-permute-start | bytes 368648 | tf_op jit(solution)/shard_map/ppermute | solution.py:26
  7.8 2.9 %collective-permute-start.3 = (f32[88,128]{1,0:T(8,128)S(1)}, f32[88,128]{1,0:T(8,128)S(1)}, u32[]{:S(2)}, u32[]{:S(2)}) collective-permute-start(f32[88,128]{1,0:T(8,128)S(1)} %get-tuple-element.44.refs_9_), channel_id=1, source_target_pairs={{1,0},{2,1},{3,2},{0,3},{5,4},{6,5},{7,6},{4,7},{9,8},{10,9},{11,1... | collective-permute-start | bytes 135176 | tf_op jit(solution)/shard_map/ppermute | solution.py:26
  10.8 1.2 %copy-done.3 = f32[16,128,128]{2,1,0:T(8,128)S(1)} copy-done((f32[16,128,128]{2,1,0:T(8,128)S(1)}, f32[16,128,128]{2,1,0:T(8,128)}, u32[]{:S(2)}) %copy-start.3) | copy-done | bytes 1048600
  12.1 0.9 %routes.1 = (f32[32,128]{1,0:T(8,128)S(1)}, f32[32,128]{1,0:T(8,128)S(1)}, f32[32,128]{1,0:T(8,128)S(1)}, f32[8,128]{1,0:T(8,128)S(1)}, f32[16,128]{1,0:T(8,128)S(1)}) custom-call(s32[4,16]{1,0:T(4,128)S(1)} %pad_add_fusion.refs_0_, s32[1]{0:T(128)} %bitcast.6.refs_1_, f32[10]{0:T(128)S(1)} %copy-done.7), custom_call_target="tpu_custom_call" | custom-call | bytes 1000000 | tf_op jit(solution)/shard_map/routes/pallas_call | solution.py:678
  13.3 2.4 %collective-permute-done.2.refs_3_.refs_4_.refs_2_ = f32[88,128]{1,0:T(8,128)S(1)} collective-permute-done((f32[88,128]{1,0:T(8,128)S(1)}, f32[88,128]{1,0:T(8,128)S(1)}, u32[]{:S(2)}, u32[]{:S(2)}) %collective-permute-start.2) | collective-permute-done | bytes 45088 | tf_op jit(solution)/shard_map/ppermute | solution.py:26
  15.7 1.2 %pieces.1.refs_7_.refs_4_ = f32[256,128]{1,0:T(8,128)} custom-call(f32[160,128]{1,0:T(8,128)S(1)} %inner.1.refs_0_, f32[240,128]{1,0:T(8,128)S(1)} %collective-permute-done.refs_1_.refs_2_, f32[240,128]{1,0:T(8,128)S(1)} %collective-permute-done.1.refs_2_.refs_3_, f32[88,128]{1,0:T(8,128)S(1)} %collective-permute-done.2.refs_3_.refs_4_.refs_2_, ...), custom_call_target="tpu_custom_call" | custom-call | bytes 1000000 | tf_op jit(solution)/shard_map/pieces/pallas_call | solution.py:678
  16.9 3.6 %all-to-all-start = ((f32[16,16,128]{2,1,0:T(8,128)}), f32[16,16,128]{2,1,0:T(8,128)S(1)}, u32[]{:S(2)}, u32[]{:S(2)}) async-start(f32[16,16,128]{2,1,0:T(8,128)} %bitcast.7), calls=%async_computation | async-start | bytes 262144 | tf_op jit(solution)/shard_map/all_to_all | solution.py:777
  20.5 2.0 %collective-permute-start.4 = (f32[208,128]{1,0:T(8,128)S(1)}, f32[208,128]{1,0:T(8,128)S(1)}, u32[]{:S(2)}, u32[]{:S(2)}) collective-permute-start(f32[208,128]{1,0:T(8,128)S(1)} %get-tuple-element.54), channel_id=1, source_target_pairs={{28,0},{0,4},{4,8},{8,12},{12,16},{16,20},{20,24},{24,28},{29,1},{... | collective-permute-start | bytes 319496 | tf_op jit(solution)/shard_map/ppermute | solution.py:26
  22.5 1.6 %collective-permute-start.5 = (f32[208,128]{1,0:T(8,128)S(1)}, f32[208,128]{1,0:T(8,128)S(1)}, u32[]{:S(2)}, u32[]{:S(2)}) collective-permute-start(f32[208,128]{1,0:T(8,128)S(1)} %get-tuple-element.55), channel_id=1, source_target_pairs={{4,0},{8,4},{12,8},{16,12},{20,16},{24,20},{28,24},{0,28},{5,1},{9... | collective-permute-start | bytes 319496 | tf_op jit(solution)/shard_map/ppermute | solution.py:26
  24.2 3.9 %sea_base.1 = (f32[2048,128]{1,0:T(8,128)}, f32[256,128]{1,0:T(8,128)S(1)}) custom-call(f32[2048,128]{1,0:T(8,128)} %bitcast.20, s32[64,128]{1,0:T(8,128)S(1)} %copy-done.5, f32[240,128]{1,0:T(8,128)S(1)} %collective-permute-done.refs_1_.refs_2_, f32[240,128]{1,0:T(8,128)S(1)} %collective-permute-done.1.refs_2_.refs_3_, ...), custom_call_target="tpu_custom_call" | custom-call | bytes 1000000000 | tf_op jit(solution)/shard_map/sea_base/pallas_call | solution.py:678
  28.0 2.1 %collective-permute-done.5.refs_6_ = f32[208,128]{1,0:T(8,128)S(1)} collective-permute-done((f32[208,128]{1,0:T(8,128)S(1)}, f32[208,128]{1,0:T(8,128)S(1)}, u32[]{:S(2)}, u32[]{:S(2)}) %collective-permute-start.5) | collective-permute-done | bytes 106528 | tf_op jit(solution)/shard_map/ppermute | solution.py:26
  30.2 0.6 fluxes.1
  30.8 0.5 collective-permute-done.6.refs_4_
  31.4 11.8 %all_to_all.20 = f32[32,8,128]{2,1,0:T(8,128)S(1)} all-to-all(f32[32,8,128]{2,1,0:T(8,128)S(1)} %bitcast.27), channel_id=1, replica_groups=mesh['comp'=2,'gx'=4,'gy'=4] {'comp','gx','gy'}, dimensions={0} | all-to-all | bytes 262144 | tf_op jit(solution)/shard_map/all_to_all | solution.py:818
  43.2 0.4 sea_top.1
  43.6 10.6 %all_to_all.21 = f32[16,8,128]{2,1,0:T(8,128)S(1)} all-to-all(f32[16,8,128]{2,1,0:T(8,128)S(1)} %bitcast.28), channel_id=1, replica_groups=mesh['comp'=2,'gx'=4,'gy'=4] {'gx','gy'}, dimensions={0} | all-to-all | bytes 131072 | tf_op jit(solution)/shard_map/all_to_all | solution.py:834
  54.1 1.3 %replies.1.refs_14_ = f32[128,128]{1,0:T(8,128)} custom-call(f32[128,128]{1,0:T(8,128)S(1)} %bitcast.26, f32[16,128,128]{2,1,0:T(8,128)S(1)} %copy-done.1, f32[32,128]{1,0:T(8,128)S(1)} %get-tuple-element.59.refs_2_, f32[32,128]{1,0:T(8,128)S(1)} %get-tuple-element.68.refs_3_), custom_call_target="tpu_custom_call" | custom-call | bytes 1000000 | tf_op jit(solution)/shard_map/replies/pallas_call | solution.py:678
  55.4 3.5 %all-to-all-start.3 = ((f32[16,8,128]{2,1,0:T(8,128)}), f32[16,8,128]{2,1,0:T(8,128)S(1)}, u32[]{:S(2)}, u32[]{:S(2)}) async-start(f32[16,8,128]{2,1,0:T(8,128)} %bitcast.15), calls=%async_computation.3 | async-start | bytes 131072 | tf_op jit(solution)/shard_map/all_to_all | solution.py:844
  58.9 5.9 %steps.1 = (f32[3200,128]{1,0:T(8,128)}, f32[4,8,64,128]{3,2,1,0:T(8,128)}) custom-call(f32[3200,128]{1,0:T(8,128)} %bitcast.19, f32[240,128]{1,0:T(8,128)S(1)} %collective-permute-done.refs_1_.refs_2_, f32[240,128]{1,0:T(8,128)S(1)} %collective-permute-done.1.refs_2_.refs_3_, ...), custom_call_target="tpu_custom_call", output_to_operand_aliasing={{1}: (13, {})} | custom-call | bytes 1000000000 | tf_op jit(solution)/shard_map/steps/pallas_call | solution.py:678
  64.8 1.6 %all-to-all-done.3 = f32[16,8,128]{2,1,0:T(8,128)S(1)} async-done(((f32[16,8,128]{2,1,0:T(8,128)}), f32[16,8,128]{2,1,0:T(8,128)S(1)}, u32[]{:S(2)}, u32[]{:S(2)}) %all-to-all-start.3) | async-done | bytes 65568 | tf_op jit(solution)/shard_map/all_to_all | solution.py:844
  66.4 1.1 %surface.1 = f32[64,128]{1,0:T(8,128)} custom-call(f32[128,128]{1,0:T(8,128)S(1)} %bitcast.25, f32[16,128,128]{2,1,0:T(8,128)S(1)} %copy-done.4, f32[32,128]{1,0:T(8,128)S(1)} %get-tuple-element.49.refs_7_.refs_2_), custom_call_target="tpu_custom_call" | custom-call | bytes 1000000 | tf_op jit(solution)/shard_map/surface/pallas_call | solution.py:678
  (37 shorter events, 0.5 us)
Async XLA Ops:
  0.6 2.2 %copy-start.2 = (f32[4,8,64,128]{3,2,1,0:T(8,128)S(1)}, f32[4,8,64,128]{3,2,1,0:T(8,128)}, u32[]{:S(2)}) copy-start(f32[4,8,64,128]{3,2,1,0:T(8,128)} %param.19) | copy-start | bytes 3145732
  0.6 2.2 %copy-start.5 = (s32[64,128]{1,0:T(8,128)S(1)}, s32[64,128]{1,0:T(8,128)}, u32[]{:S(2)}) copy-start(s32[64,128]{1,0:T(8,128)} %refs_2_.3) | copy-start | bytes 98308
  0.7 10.1 %copy-start.12 = (s32[16,1]{0,1:T(1,128)S(1)}, s32[16,1]{0,1:T(1,128)}, u32[]{:S(2)}) copy-start(s32[16,1]{0,1:T(1,128)} %param.14) | copy-start | bytes 196
  0.7 10.1 %copy-start.11 = (s32[16]{0:T(128)S(1)}, s32[16]{0:T(128)}, u32[]{:S(2)}) copy-start(s32[16]{0:T(128)} %param.15) | copy-start | bytes 196
  0.7 10.1 %copy-start.10 = (s32[16,1]{0,1:T(1,128)S(1)}, s32[16,1]{0,1:T(1,128)}, u32[]{:S(2)}) copy-start(s32[16,1]{0,1:T(1,128)} %param.17) | copy-start | bytes 196
  0.7 10.1 %copy-start.9 = (s32[16]{0:T(128)S(1)}, s32[16]{0:T(128)}, u32[]{:S(2)}) copy-start(s32[16]{0:T(128)} %param.18) | copy-start | bytes 196
  2.8 9.3 %copy-start.7 = (f32[10]{0:T(128)S(1)}, f32[10]{0:T(128)}, u32[]{:S(2)}) copy-start(f32[10]{0:T(128)} %refs_11_.1) | copy-start | bytes 124
  2.9 10.2 %copy-start = (f32[10,20,16,128]{3,2,1,0:T(8,128)S(1)}, f32[10,20,16,128]{3,2,1,0:T(8,128)}, u32[]{:S(2)}) copy-start(f32[10,20,16,128]{3,2,1,0:T(8,128)} %refs_0_) | copy-start | bytes 4915204
  3.2 12.4 %collective-permute-start = (f32[240,128]{1,0:T(8,128)S(1)}, f32[240,128]{1,0:T(8,128)S(1)}, u32[]{:S(2)}, u32[]{:S(2)}) collective-permute-start(f32[240,128]{1,0:T(8,128)S(1)} %get-tuple-element.41.refs_8_), channel_id=1, source_target_pairs={{28,0},{0,4},{4,8},{8,12},{12,16},{16,20},{20,24},{24,28},{29,1},{... | collective-permute-start | bytes 368648 | tf_op jit(solution)/shard_map/ppermute | solution.py:26
  6.3 9.4 %collective-permute-start.1 = (f32[240,128]{1,0:T(8,128)S(1)}, f32[240,128]{1,0:T(8,128)S(1)}, u32[]{:S(2)}, u32[]{:S(2)}) collective-permute-start(f32[240,128]{1,0:T(8,128)S(1)} %get-tuple-element.42.refs_7_), channel_id=1, source_target_pairs={{4,0},{8,4},{12,8},{16,12},{20,16},{24,20},{28,24},{0,28},{5,1},{9... | collective-permute-start | bytes 368648 | tf_op jit(solution)/shard_map/ppermute | solution.py:26
  7.8 5.4 %collective-permute-start.3 = (f32[88,128]{1,0:T(8,128)S(1)}, f32[88,128]{1,0:T(8,128)S(1)}, u32[]{:S(2)}, u32[]{:S(2)}) collective-permute-start(f32[88,128]{1,0:T(8,128)S(1)} %get-tuple-element.44.refs_9_), channel_id=1, source_target_pairs={{1,0},{2,1},{3,2},{0,3},{5,4},{6,5},{7,6},{4,7},{9,8},{10,9},{11,1... | collective-permute-start | bytes 135176 | tf_op jit(solution)/shard_map/ppermute | solution.py:26
  10.7 4.9 %collective-permute-start.2 = (f32[88,128]{1,0:T(8,128)S(1)}, f32[88,128]{1,0:T(8,128)S(1)}, u32[]{:S(2)}, u32[]{:S(2)}) collective-permute-start(f32[88,128]{1,0:T(8,128)S(1)} %get-tuple-element.43.refs_10_), channel_id=1, source_target_pairs={{3,0},{0,1},{1,2},{2,3},{7,4},{4,5},{5,6},{6,7},{11,8},{8,9},{9,10... | collective-permute-start | bytes 135176 | tf_op jit(solution)/shard_map/ppermute | solution.py:26
  10.8 1.2 %copy-start.3 = (f32[16,128,128]{2,1,0:T(8,128)S(1)}, f32[16,128,128]{2,1,0:T(8,128)}, u32[]{:S(2)}) copy-start(f32[16,128,128]{2,1,0:T(8,128)} %refs_1_.9) | copy-start | bytes 3145732
  13.1 11.1 %copy-start.8 = (f32[4]{0:T(128)S(1)}, f32[4]{0:T(128)}, u32[]{:S(2)}) copy-start(f32[4]{0:T(128)} %refs_6_.1) | copy-start | bytes 52
  15.7 14.5 %copy-start.1 = (f32[16,128,128]{2,1,0:T(8,128)S(1)}, f32[16,128,128]{2,1,0:T(8,128)}, u32[]{:S(2)}) copy-start(f32[16,128,128]{2,1,0:T(8,128)} %refs_1_.8) | copy-start | bytes 3145732
  16.9 13.2 %all-to-all-start = ((f32[16,16,128]{2,1,0:T(8,128)}), f32[16,16,128]{2,1,0:T(8,128)S(1)}, u32[]{:S(2)}, u32[]{:S(2)}) async-start(f32[16,16,128]{2,1,0:T(8,128)} %bitcast.7), calls=%async_computation | async-start | bytes 262144 | tf_op jit(solution)/shard_map/all_to_all | solution.py:777
  20.5 7.5 %collective-permute-start.4 = (f32[208,128]{1,0:T(8,128)S(1)}, f32[208,128]{1,0:T(8,128)S(1)}, u32[]{:S(2)}, u32[]{:S(2)}) collective-permute-start(f32[208,128]{1,0:T(8,128)S(1)} %get-tuple-element.54), channel_id=1, source_target_pairs={{28,0},{0,4},{4,8},{8,12},{12,16},{16,20},{20,24},{24,28},{29,1},{... | collective-permute-start | bytes 319496 | tf_op jit(solution)/shard_map/ppermute | solution.py:26
  22.5 7.6 %collective-permute-start.5 = (f32[208,128]{1,0:T(8,128)S(1)}, f32[208,128]{1,0:T(8,128)S(1)}, u32[]{:S(2)}, u32[]{:S(2)}) collective-permute-start(f32[208,128]{1,0:T(8,128)S(1)} %get-tuple-element.55), channel_id=1, source_target_pairs={{4,0},{8,4},{12,8},{16,12},{20,16},{24,20},{28,24},{0,28},{5,1},{9... | collective-permute-start | bytes 319496 | tf_op jit(solution)/shard_map/ppermute | solution.py:26
  30.1 1.2 %collective-permute-start.6 = (f32[32,128]{1,0:T(8,128)S(1)}, f32[32,128]{1,0:T(8,128)S(1)}, u32[]{:S(2)}, u32[]{:S(2)}) collective-permute-start(f32[32,128]{1,0:T(8,128)S(1)} %sea_labels.1.refs_3_), channel_id=1, source_target_pairs={{16,0},{0,16},{17,1},{1,17},{18,2},{2,18},{19,3},{3,19},{20,4},{4,... | collective-permute-start | bytes 49160 | tf_op jit(solution)/shard_map/ppermute | solution.py:26
  43.6 11.9 %copy-start.6 = (f32[256,128]{1,0:T(8,128)}, f32[256,128]{1,0:T(8,128)S(1)}, u32[]{:S(2)}) copy-start(f32[256,128]{1,0:T(8,128)S(1)} %get-tuple-element.65.refs_12_) | copy-start | bytes 393220
  55.4 11.0 %all-to-all-start.3 = ((f32[16,8,128]{2,1,0:T(8,128)}), f32[16,8,128]{2,1,0:T(8,128)S(1)}, u32[]{:S(2)}, u32[]{:S(2)}) async-start(f32[16,8,128]{2,1,0:T(8,128)} %bitcast.15), calls=%async_computation.3 | async-start | bytes 131072 | tf_op jit(solution)/shard_map/all_to_all | solution.py:844
  58.9 7.5 %copy-start.4 = (f32[16,128,128]{2,1,0:T(8,128)S(1)}, f32[16,128,128]{2,1,0:T(8,128)}, u32[]{:S(2)}) copy-start(f32[16,128,128]{2,1,0:T(8,128)} %refs_1_.9) | copy-start | bytes 3145732

commit v8 on v7

--- a/solution.py
+++ b/solution.py
@@ -643,12 +643,12 @@
         ]
 
 
-def surface_kernel(flux_count, returned, remap, routes, out, tops):
-    rows = remap.shape[0]
+def surface_kernel(flux_count, returned, weights, routes, out, tops):
+    rows = weights.shape[0]
     tops_of_tiles(returned, routes, flux_count, tops)
     for tile in range(rows):
         out[pl.ds(tile, flux_count, stride=rows), :] = remapped(
-            tops[pl.ds(tile * flux_count, flux_count), :], both_halves(jnp.transpose(remap[tile]))
+            tops[pl.ds(tile * flux_count, flux_count), :], weights[tile]
         )
 
 
@@ -885,7 +885,7 @@
         [pltpu.VMEM((sea_fields * rows, width), F32)],
     )(
         returned.reshape(slots * sea_fields, width),
-        remap_atmos,
+        weights_of(remap_atmos, True, "surface_weights", replies),
         tile_slots,
     )
     return (

time: 68 us -> 67.9 us (level)
  waiting for transfers between devices: 6.62 us -> 4.57 us
  starting transfers between devices: 18.3 us -> 20 us
    ppermute x7, waiting for transfers between devices: 5 us -> 3.29 us  [shifted(): return lax.ppermute(block, axis, route)]
    all_to_all x1, starting transfers between devices: 3.61 us -> 5.29 us  [on_device(): lax.all_to_all(pieces.reshape(targets, CAPACITY * PIECE_ROWS, width), SEC...]
    pallas_call x14 -> x15, Pallas kernels: 18.1 us -> 18.4 us  [call(): return lambda *arguments: run(*arguments, *after)]
  transfers between devices with their start and end apart: 9 -> 9, of which waited for: 4 -> 4; matrix products, arithmetic and copies ran while one was open for 0% -> 0% of each run, Pallas kernels for 17% -> 18%
where the time goes in v8:
time: 67.9 us; the launch traced here: 67.5 us
  blocking collectives  22.4 us (33%)
  starting transfers between devices  20 us (29%)
  Pallas kernels  18.4 us (27%)
  waiting for transfers between devices  4.57 us (7%)
  local copies, waits for them, and re-layouts  1.28 us (2%)
  between operations  0.9 us (1%)
    pallas_call x15, Pallas kernels, call(): return lambda *arguments: run(*arguments, *after)  18.4 us
    all_to_all x1, blocking collectives, on_device(): lax.all_to_all(outgoing.reshape(devices, CAPACITY * sea_fields, width), E...  11.8 us
    ppermute x7, starting transfers between devices, shifted(): return lax.ppermute(block, axis, route)  11.2 us
    all_to_all x1, blocking collectives, on_device(): lax.all_to_all(answers.reshape(targets, CAPACITY * sea_fields, width), SE...  10.6 us
    all_to_all x1, starting transfers between devices, on_device(): lax.all_to_all(pieces.reshape(targets, CAPACITY * PIECE_ROWS, width), SEC...  5.29 us
    all_to_all x1, starting transfers between devices, on_device(): lax.all_to_all(replies.reshape(targets, CAPACITY * sea_fields, width), SE...  3.48 us
    ppermute x7, waiting for transfers between devices, shifted(): return lax.ppermute(block, axis, route)  3.29 us
  transfers between devices with their start and end apart: 9, of which 4 were waited for; matrix products, arithmetic and copies ran while one was open for 0% of the time, Pallas kernels for 18%

profile of v8, /device:TPU:0, one launch (start us, length us, event | category | flops | bytes accessed | tf_op | source)
XLA Modules:
  0.0 67.5 jit_solution(14383531534593065903)
XLA Ops:
  0.7 2.1 %edges.1 = (f32[240,128]{1,0:T(8,128)S(1)}, f32[240,128]{1,0:T(8,128)S(1)}, f32[208,128]{1,0:T(8,128)S(1)}, f32[208,128]{1,0:T(8,128)S(1)}, f32[88,128]{1,0:T(8,128)S(1)}, /*index=5*/f32[88,128]{1,0:T(8,128)S(1)}) custom-call(f32[3200,128]{1,0:T(8,128)} %bitcast.18), custom_call_target="tpu_custom_call" | custom-call | bytes 1000000 | tf_op jit(solution)/shard_map/edges/pallas_call | solution.py:678
  3.2 3.1 %collective-permute-start = (f32[240,128]{1,0:T(8,128)S(1)}, f32[240,128]{1,0:T(8,128)S(1)}, u32[]{:S(2)}, u32[]{:S(2)}) collective-permute-start(f32[240,128]{1,0:T(8,128)S(1)} %get-tuple-element.42.refs_8_), channel_id=1, source_target_pairs={{28,0},{0,4},{4,8},{8,12},{12,16},{16,20},{20,24},{24,28},{29,1},{... | collective-permute-start | bytes 368648 | tf_op jit(solution)/shard_map/ppermute | solution.py:26
  6.3 1.5 %collective-permute-start.1 = (f32[240,128]{1,0:T(8,128)S(1)}, f32[240,128]{1,0:T(8,128)S(1)}, u32[]{:S(2)}, u32[]{:S(2)}) collective-permute-start(f32[240,128]{1,0:T(8,128)S(1)} %get-tuple-element.43.refs_7_), channel_id=1, source_target_pairs={{4,0},{8,4},{12,8},{16,12},{20,16},{24,20},{28,24},{0,28},{5,1},{9... | collective-permute-start | bytes 368648 | tf_op jit(solution)/shard_map/ppermute | solution.py:26
  7.8 1.9 %collective-permute-start.2 = (f32[88,128]{1,0:T(8,128)S(1)}, f32[88,128]{1,0:T(8,128)S(1)}, u32[]{:S(2)}, u32[]{:S(2)}) collective-permute-start(f32[88,128]{1,0:T(8,128)S(1)} %get-tuple-element.44.refs_10_), channel_id=1, source_target_pairs={{3,0},{0,1},{1,2},{2,3},{7,4},{4,5},{5,6},{6,7},{11,8},{8,9},{9,10... | collective-permute-start | bytes 135176 | tf_op jit(solution)/shard_map/ppermute | solution.py:26
  9.8 1.0 %collective-permute-start.3 = (f32[88,128]{1,0:T(8,128)S(1)}, f32[88,128]{1,0:T(8,128)S(1)}, u32[]{:S(2)}, u32[]{:S(2)}) collective-permute-start(f32[88,128]{1,0:T(8,128)S(1)} %get-tuple-element.45.refs_9_), channel_id=1, source_target_pairs={{1,0},{2,1},{3,2},{0,3},{5,4},{6,5},{7,6},{4,7},{9,8},{10,9},{11,1... | collective-permute-start | bytes 135176 | tf_op jit(solution)/shard_map/ppermute | solution.py:26
  10.8 1.2 %copy-done.3 = f32[16,128,128]{2,1,0:T(8,128)S(1)} copy-done((f32[16,128,128]{2,1,0:T(8,128)S(1)}, f32[16,128,128]{2,1,0:T(8,128)}, u32[]{:S(2)}) %copy-start.3) | copy-done | bytes 1048600
  12.2 0.9 %routes.1 = (f32[32,128]{1,0:T(8,128)S(1)}, f32[32,128]{1,0:T(8,128)S(1)}, f32[32,128]{1,0:T(8,128)S(1)}, f32[8,128]{1,0:T(8,128)S(1)}, f32[16,128]{1,0:T(8,128)S(1)}) custom-call(s32[4,16]{1,0:T(4,128)S(1)} %pad_add_fusion.refs_0_, s32[1]{0:T(128)} %bitcast.6.refs_1_, f32[10]{0:T(128)S(1)} %copy-done.7), custom_call_target="tpu_custom_call" | custom-call | bytes 1000000 | tf_op jit(solution)/shard_map/routes/pallas_call | solution.py:678
  13.3 0.7 %collective-permute-done.3.refs_4_.refs_5_.refs_3_ = f32[88,128]{1,0:T(8,128)S(1)} collective-permute-done((f32[88,128]{1,0:T(8,128)S(1)}, f32[88,128]{1,0:T(8,128)S(1)}, u32[]{:S(2)}, u32[]{:S(2)}) %collective-permute-start.3) | collective-permute-done | bytes 45088 | tf_op jit(solution)/shard_map/ppermute | solution.py:26
  14.0 1.2 %pieces.1.refs_7_.refs_4_ = f32[256,128]{1,0:T(8,128)} custom-call(f32[160,128]{1,0:T(8,128)S(1)} %inner.1.refs_0_, f32[240,128]{1,0:T(8,128)S(1)} %collective-permute-done.refs_1_.refs_2_, f32[240,128]{1,0:T(8,128)S(1)} %collective-permute-done.1.refs_2_.refs_3_, f32[88,128]{1,0:T(8,128)S(1)} %collective-permute-done.2.refs_3_.refs_4_.refs_2_, ...), custom_call_target="tpu_custom_call" | custom-call | bytes 1000000 | tf_op jit(solution)/shard_map/pieces/pallas_call | solution.py:678
  15.2 5.3 %all-to-all-start = ((f32[16,16,128]{2,1,0:T(8,128)}), f32[16,16,128]{2,1,0:T(8,128)S(1)}, u32[]{:S(2)}, u32[]{:S(2)}) async-start(f32[16,16,128]{2,1,0:T(8,128)} %bitcast.7), calls=%async_computation | async-start | bytes 262144 | tf_op jit(solution)/shard_map/all_to_all | solution.py:777
  20.5 2.0 %collective-permute-start.4 = (f32[208,128]{1,0:T(8,128)S(1)}, f32[208,128]{1,0:T(8,128)S(1)}, u32[]{:S(2)}, u32[]{:S(2)}) collective-permute-start(f32[208,128]{1,0:T(8,128)S(1)} %get-tuple-element.55), channel_id=1, source_target_pairs={{28,0},{0,4},{4,8},{8,12},{12,16},{16,20},{20,24},{24,28},{29,1},{... | collective-permute-start | bytes 319496 | tf_op jit(solution)/shard_map/ppermute | solution.py:26
  22.5 1.6 %collective-permute-start.5 = (f32[208,128]{1,0:T(8,128)S(1)}, f32[208,128]{1,0:T(8,128)S(1)}, u32[]{:S(2)}, u32[]{:S(2)}) collective-permute-start(f32[208,128]{1,0:T(8,128)S(1)} %get-tuple-element.56), channel_id=1, source_target_pairs={{4,0},{8,4},{12,8},{16,12},{20,16},{24,20},{28,24},{0,28},{5,1},{9... | collective-permute-start | bytes 319496 | tf_op jit(solution)/shard_map/ppermute | solution.py:26
  24.2 3.9 %sea_base.1 = (f32[2048,128]{1,0:T(8,128)}, f32[256,128]{1,0:T(8,128)S(1)}) custom-call(f32[2048,128]{1,0:T(8,128)} %bitcast.20, s32[64,128]{1,0:T(8,128)S(1)} %copy-done.5, f32[240,128]{1,0:T(8,128)S(1)} %collective-permute-done.refs_1_.refs_2_, f32[240,128]{1,0:T(8,128)S(1)} %collective-permute-done.1.refs_2_.refs_3_, ...), custom_call_target="tpu_custom_call" | custom-call | bytes 1000000000 | tf_op jit(solution)/shard_map/sea_base/pallas_call | solution.py:678
  28.0 2.1 %collective-permute-done.5.refs_6_ = f32[208,128]{1,0:T(8,128)S(1)} collective-permute-done((f32[208,128]{1,0:T(8,128)S(1)}, f32[208,128]{1,0:T(8,128)S(1)}, u32[]{:S(2)}, u32[]{:S(2)}) %collective-permute-start.5) | collective-permute-done | bytes 106528 | tf_op jit(solution)/shard_map/ppermute | solution.py:26
  30.2 0.6 fluxes.1
  30.8 0.5 collective-permute-done.6.refs_4_
  31.4 11.8 %all_to_all.20 = f32[32,8,128]{2,1,0:T(8,128)S(1)} all-to-all(f32[32,8,128]{2,1,0:T(8,128)S(1)} %bitcast.27), channel_id=1, replica_groups=mesh['comp'=2,'gx'=4,'gy'=4] {'comp','gx','gy'}, dimensions={0} | all-to-all | bytes 262144 | tf_op jit(solution)/shard_map/all_to_all | solution.py:818
  43.2 0.4 sea_top.1
  43.6 10.6 %all_to_all.21 = f32[16,8,128]{2,1,0:T(8,128)S(1)} all-to-all(f32[16,8,128]{2,1,0:T(8,128)S(1)} %bitcast.28), channel_id=1, replica_groups=mesh['comp'=2,'gx'=4,'gy'=4] {'gx','gy'}, dimensions={0} | all-to-all | bytes 131072 | tf_op jit(solution)/shard_map/all_to_all | solution.py:834
  54.1 1.3 %replies.1.refs_14_ = f32[128,128]{1,0:T(8,128)} custom-call(f32[128,128]{1,0:T(8,128)S(1)} %bitcast.26, f32[16,128,128]{2,1,0:T(8,128)S(1)} %copy-done.1, f32[32,128]{1,0:T(8,128)S(1)} %get-tuple-element.60.refs_2_, f32[32,128]{1,0:T(8,128)S(1)} %get-tuple-element.69.refs_3_), custom_call_target="tpu_custom_call" | custom-call | bytes 1000000 | tf_op jit(solution)/shard_map/replies/pallas_call | solution.py:678
  55.4 3.5 %all-to-all-start.3 = ((f32[16,8,128]{2,1,0:T(8,128)}), f32[16,8,128]{2,1,0:T(8,128)S(1)}, u32[]{:S(2)}, u32[]{:S(2)}) async-start(f32[16,8,128]{2,1,0:T(8,128)} %bitcast.15), calls=%async_computation.3 | async-start | bytes 131072 | tf_op jit(solution)/shard_map/all_to_all | solution.py:844
  59.3 5.9 %steps.1 = (f32[3200,128]{1,0:T(8,128)}, f32[4,8,64,128]{3,2,1,0:T(8,128)}) custom-call(f32[3200,128]{1,0:T(8,128)} %bitcast.19, f32[240,128]{1,0:T(8,128)S(1)} %collective-permute-done.refs_1_.refs_2_, f32[240,128]{1,0:T(8,128)S(1)} %collective-permute-done.1.refs_2_.refs_3_, ...), custom_call_target="tpu_custom_call", output_to_operand_aliasing={{1}: (13, {})} | custom-call | bytes 1000000000 | tf_op jit(solution)/shard_map/steps/pallas_call | solution.py:678
  65.1 1.3 %all-to-all-done.3 = f32[16,8,128]{2,1,0:T(8,128)S(1)} async-done(((f32[16,8,128]{2,1,0:T(8,128)}), f32[16,8,128]{2,1,0:T(8,128)S(1)}, u32[]{:S(2)}, u32[]{:S(2)}) %all-to-all-start.3) | async-done | bytes 65568 | tf_op jit(solution)/shard_map/all_to_all | solution.py:844
  66.4 1.1 %surface.1 = f32[64,128]{1,0:T(8,128)} custom-call(f32[128,128]{1,0:T(8,128)S(1)} %bitcast.25, bf16[16,256,128]{2,1,0:T(8,128)(2,1)S(1)} %surface_weights.1.refs_1_, f32[32,128]{1,0:T(8,128)S(1)} %get-tuple-element.50.refs_7_.refs_2_), custom_call_target="tpu_custom_call" | custom-call | bytes 1000000 | tf_op jit(solution)/shard_map/surface/pallas_call | solution.py:678
  (38 shorter events, 1.1 us)
Async XLA Ops:
  0.6 2.2 %copy-start.2 = (f32[4,8,64,128]{3,2,1,0:T(8,128)S(1)}, f32[4,8,64,128]{3,2,1,0:T(8,128)}, u32[]{:S(2)}) copy-start(f32[4,8,64,128]{3,2,1,0:T(8,128)} %param.19) | copy-start | bytes 3145732
  0.6 2.2 %copy-start.5 = (s32[64,128]{1,0:T(8,128)S(1)}, s32[64,128]{1,0:T(8,128)}, u32[]{:S(2)}) copy-start(s32[64,128]{1,0:T(8,128)} %refs_2_.3) | copy-start | bytes 98308
  0.7 10.1 %copy-start.9 = (s32[16]{0:T(128)S(1)}, s32[16]{0:T(128)}, u32[]{:S(2)}) copy-start(s32[16]{0:T(128)} %param.18) | copy-start | bytes 196
  0.7 10.1 %copy-start.10 = (s32[16,1]{0,1:T(1,128)S(1)}, s32[16,1]{0,1:T(1,128)}, u32[]{:S(2)}) copy-start(s32[16,1]{0,1:T(1,128)} %param.17) | copy-start | bytes 196
  0.7 10.1 %copy-start.11 = (s32[16]{0:T(128)S(1)}, s32[16]{0:T(128)}, u32[]{:S(2)}) copy-start(s32[16]{0:T(128)} %param.15) | copy-start | bytes 196
  0.7 10.1 %copy-start.12 = (s32[16,1]{0,1:T(1,128)S(1)}, s32[16,1]{0,1:T(1,128)}, u32[]{:S(2)}) copy-start(s32[16,1]{0,1:T(1,128)} %param.14) | copy-start | bytes 196
  2.8 9.3 %copy-start.7 = (f32[10]{0:T(128)S(1)}, f32[10]{0:T(128)}, u32[]{:S(2)}) copy-start(f32[10]{0:T(128)} %refs_11_.1) | copy-start | bytes 124
  2.9 10.2 %copy-start = (f32[10,20,16,128]{3,2,1,0:T(8,128)S(1)}, f32[10,20,16,128]{3,2,1,0:T(8,128)}, u32[]{:S(2)}) copy-start(f32[10,20,16,128]{3,2,1,0:T(8,128)} %refs_0_) | copy-start | bytes 4915204
  3.2 10.8 %collective-permute-start = (f32[240,128]{1,0:T(8,128)S(1)}, f32[240,128]{1,0:T(8,128)S(1)}, u32[]{:S(2)}, u32[]{:S(2)}) collective-permute-start(f32[240,128]{1,0:T(8,128)S(1)} %get-tuple-element.42.refs_8_), channel_id=1, source_target_pairs={{28,0},{0,4},{4,8},{8,12},{12,16},{16,20},{20,24},{24,28},{29,1},{... | collective-permute-start | bytes 368648 | tf_op jit(solution)/shard_map/ppermute | solution.py:26
  6.3 7.7 %collective-permute-start.1 = (f32[240,128]{1,0:T(8,128)S(1)}, f32[240,128]{1,0:T(8,128)S(1)}, u32[]{:S(2)}, u32[]{:S(2)}) collective-permute-start(f32[240,128]{1,0:T(8,128)S(1)} %get-tuple-element.43.refs_7_), channel_id=1, source_target_pairs={{4,0},{8,4},{12,8},{16,12},{20,16},{24,20},{28,24},{0,28},{5,1},{9... | collective-permute-start | bytes 368648 | tf_op jit(solution)/shard_map/ppermute | solution.py:26
  7.8 5.4 %collective-permute-start.2 = (f32[88,128]{1,0:T(8,128)S(1)}, f32[88,128]{1,0:T(8,128)S(1)}, u32[]{:S(2)}, u32[]{:S(2)}) collective-permute-start(f32[88,128]{1,0:T(8,128)S(1)} %get-tuple-element.44.refs_10_), channel_id=1, source_target_pairs={{3,0},{0,1},{1,2},{2,3},{7,4},{4,5},{5,6},{6,7},{11,8},{8,9},{9,10... | collective-permute-start | bytes 135176 | tf_op jit(solution)/shard_map/ppermute | solution.py:26
  9.8 4.2 %collective-permute-start.3 = (f32[88,128]{1,0:T(8,128)S(1)}, f32[88,128]{1,0:T(8,128)S(1)}, u32[]{:S(2)}, u32[]{:S(2)}) collective-permute-start(f32[88,128]{1,0:T(8,128)S(1)} %get-tuple-element.45.refs_9_), channel_id=1, source_target_pairs={{1,0},{2,1},{3,2},{0,3},{5,4},{6,5},{7,6},{4,7},{9,8},{10,9},{11,1... | collective-permute-start | bytes 135176 | tf_op jit(solution)/shard_map/ppermute | solution.py:26
  10.8 1.2 %copy-start.3 = (f32[16,128,128]{2,1,0:T(8,128)S(1)}, f32[16,128,128]{2,1,0:T(8,128)}, u32[]{:S(2)}) copy-start(f32[16,128,128]{2,1,0:T(8,128)} %refs_0_.2) | copy-start | bytes 3145732
  13.1 11.1 %copy-start.8 = (f32[4]{0:T(128)S(1)}, f32[4]{0:T(128)}, u32[]{:S(2)}) copy-start(f32[4]{0:T(128)} %refs_6_.1) | copy-start | bytes 52
  14.0 16.2 %copy-start.1 = (f32[16,128,128]{2,1,0:T(8,128)S(1)}, f32[16,128,128]{2,1,0:T(8,128)}, u32[]{:S(2)}) copy-start(f32[16,128,128]{2,1,0:T(8,128)} %refs_1_.7) | copy-start | bytes 3145732
  15.2 14.9 %all-to-all-start = ((f32[16,16,128]{2,1,0:T(8,128)}), f32[16,16,128]{2,1,0:T(8,128)S(1)}, u32[]{:S(2)}, u32[]{:S(2)}) async-start(f32[16,16,128]{2,1,0:T(8,128)} %bitcast.7), calls=%async_computation | async-start | bytes 262144 | tf_op jit(solution)/shard_map/all_to_all | solution.py:777
  20.5 7.5 %collective-permute-start.4 = (f32[208,128]{1,0:T(8,128)S(1)}, f32[208,128]{1,0:T(8,128)S(1)}, u32[]{:S(2)}, u32[]{:S(2)}) collective-permute-start(f32[208,128]{1,0:T(8,128)S(1)} %get-tuple-element.55), channel_id=1, source_target_pairs={{28,0},{0,4},{4,8},{8,12},{12,16},{16,20},{20,24},{24,28},{29,1},{... | collective-permute-start | bytes 319496 | tf_op jit(solution)/shard_map/ppermute | solution.py:26
  22.5 7.6 %collective-permute-start.5 = (f32[208,128]{1,0:T(8,128)S(1)}, f32[208,128]{1,0:T(8,128)S(1)}, u32[]{:S(2)}, u32[]{:S(2)}) collective-permute-start(f32[208,128]{1,0:T(8,128)S(1)} %get-tuple-element.56), channel_id=1, source_target_pairs={{4,0},{8,4},{12,8},{16,12},{20,16},{24,20},{28,24},{0,28},{5,1},{9... | collective-permute-start | bytes 319496 | tf_op jit(solution)/shard_map/ppermute | solution.py:26
  30.1 1.2 %collective-permute-start.6 = (f32[32,128]{1,0:T(8,128)S(1)}, f32[32,128]{1,0:T(8,128)S(1)}, u32[]{:S(2)}, u32[]{:S(2)}) collective-permute-start(f32[32,128]{1,0:T(8,128)S(1)} %sea_labels.1.refs_3_), channel_id=1, source_target_pairs={{16,0},{0,16},{17,1},{1,17},{18,2},{2,18},{19,3},{3,19},{20,4},{4,... | collective-permute-start | bytes 49160 | tf_op jit(solution)/shard_map/ppermute | solution.py:26
  30.2 28.7 %copy-start.4 = (f32[16,128,128]{2,1,0:T(8,128)S(1)}, f32[16,128,128]{2,1,0:T(8,128)}, u32[]{:S(2)}) copy-start(f32[16,128,128]{2,1,0:T(8,128)} %refs_0_.2) | copy-start | bytes 3145732
  43.6 11.9 %copy-start.6 = (f32[256,128]{1,0:T(8,128)}, f32[256,128]{1,0:T(8,128)S(1)}, u32[]{:S(2)}) copy-start(f32[256,128]{1,0:T(8,128)S(1)} %get-tuple-element.66.refs_12_) | copy-start | bytes 393220
  55.4 11.0 %all-to-all-start.3 = ((f32[16,8,128]{2,1,0:T(8,128)}), f32[16,8,128]{2,1,0:T(8,128)S(1)}, u32[]{:S(2)}, u32[]{:S(2)}) async-start(f32[16,8,128]{2,1,0:T(8,128)} %bitcast.15), calls=%async_computation.3 | async-start | bytes 131072 | tf_op jit(solution)/shard_map/all_to_all | solution.py:844
